TPU v7x, 32 devices: a whole 2x2x4 slice. The times are simulated.
32 devices in a mesh: section: 2 (over core), seq: 16 (over z, y, x).
Axes of the slice: x: 2, y: 2, z: 4, core: 2. Of those that a mesh axis runs over, the one named last changes fastest.
Arguments:
- inputs: bfloat16 [2, 4096, 1536], P(None, 'seq'), may hold values from -6 to 6
- cotangent: bfloat16 [2, 4096, 1536], P(None, 'seq'), may hold values from -6 to 6
- norm_gain: float32 [2, 1536], P('section'), may hold values from 0.5 to 1.5
- in_weight: bfloat16 [2, 1536, 6448], P('section'), may hold values from -0.15625 to 0.15625
- conv_weight: float32 [2, 3328, 4], P('section'), may hold values from -3 to 3
- conv_bias: float32 [2, 3328], P('section'), may hold values from -0.5 to 0.5
- dt_bias: float32 [2, 48], P('section'), may hold values from -4.5 to -3.5
- a_log: float32 [2, 48], P('section'), may hold values from -8 to 1, as said below
- d_skip: float32 [2, 48], P('section'), may hold values from 0.5 to 1.5
- gate_norm_gain: float32 [2, 3072], P('section'), may hold values from 0.5 to 1.5
- out_weight: bfloat16 [2, 3072, 1536], P('section'), may hold values from -0.109375 to 0.109375
Outputs:
- acts: bfloat16 [2, 2, 4096, 1536], P('section', None, 'seq')
- input_grads: float32 [2, 2, 4096, 1536], P('section', None, 'seq')
- grad_norm_gain: float32 [2, 1536], P('section', 'seq')
- grad_in_weight: float32 [2, 1536, 6448], P('section', 'seq')
- grad_conv_weight: float32 [2, 3328, 4], P('section', 'seq')
- grad_conv_bias: float32 [2, 3328], P('section', 'seq')
- grad_dt_bias: float32 [2, 48], P('section')
- grad_a_log: float32 [2, 48], P('section')
- grad_d_skip: float32 [2, 48], P('section')
- grad_gate_norm_gain: float32 [2, 3072], P('section', 'seq')
- grad_out_weight: float32 [2, 3072, 1536], P('section', 'seq')
Inputs may be any that keep to these rules, and one draw needn't show every extreme that they name: Per layer and head, a_log is log(rate / 0.03) for a decay rate per unit step.
All inputs are finite; a program needn't handle non-finite values.
Results may differ from a plain program's by a relative error of at most 0.015.
The roundings to bfloat16 on the way count: a program that leaves them out, or rounds other values in their place, can miss the bound.
Values may be sent and summed in bfloat16 or wider, within the bound.
A program may use at most 576 MiB of HBM per device.

v0:
```python
import jax
import jax.numpy as jnp
from jax import lax
from jax.sharding import PartitionSpec as P

D = 1536
INNER = 3072
STATE = 128
HEADDIM = 64
CONV = 4
GROUP = 256
HEADS = 48
CONVD = 3328


HIGH = lax.Precision.HIGHEST
epsilon_norm = 1e-05


def shifted(block, axis, distance):
    devices = range(lax.axis_size(axis))
    route = [(i - distance, i) for i in devices if i - distance in devices]
    return lax.ppermute(block, axis, route)


def entering(value, axis, join, neutral):
    count, mine = (lax.axis_size(axis), lax.axis_index(axis))
    pieces = jax.tree.map(lambda part: lax.all_gather(part, axis), value)
    running = jax.tree.map(
        lambda part, zero: jnp.full_like(part, 0) + jnp.asarray(zero, part.dtype), value, neutral
    )

    def entering_lap(position, running):
        longer = join(running, jax.tree.map(lambda part: part[position], pieces))
        return jax.tree.map(lambda new, old: jnp.where(position < mine, new, old), longer, running)

    return lax.fori_loop(0, count - 1, entering_lap, running)


def prefix(shard, axis, combine, identity):
    count, place = (lax.axis_size(axis), lax.axis_index(axis))
    everything = jax.tree.map(
        lambda part, kind: lax.all_gather(part.astype(kind), axis),
        shard,
        jax.tree.map(lambda a: jnp.bfloat16 if a.dtype == jnp.float32 else a.dtype, shard),
    )
    start = jax.tree.map(
        lambda part, zero: jnp.broadcast_to(jnp.asarray(zero, part.dtype), part.shape),
        shard,
        identity,
    )

    def prefix_lap(k, before):
        at = count - 1 - k
        reached = at > place
        new = combine(
            before, jax.tree.map(lambda part, own: part[at].astype(own.dtype), everything, shard)
        )
        return jax.tree.map(lambda a, b: jnp.where(reached, a, b), new, before)

    return lax.fori_loop(0, count, prefix_lap, start)


def rms_scale(value, gain):
    return value * lax.rsqrt(jnp.mean(value * value, axis=-1, keepdims=True) + epsilon_norm) * gain


def ssd_block(carry_state, pieces):
    scaled, decay_log, b_proj, c_proj = pieces
    size = decay_log.shape[0]
    cumulative = jnp.cumsum(decay_log, axis=0)
    by_head = cumulative.T
    row_ids = lax.broadcasted_iota(jnp.int32, (size, size), 0)
    col_ids = lax.broadcasted_iota(jnp.int32, (size, size), 1)
    lower_mask = (row_ids >= col_ids)[None, :, :]
    segment = by_head[:, :, None] - by_head[:, None, :]
    decay = jnp.exp(jnp.where(lower_mask, segment, -jnp.inf))
    intersection = jnp.dot(c_proj, b_proj.T, precision=HIGH)
    mixing = intersection[None, :, :] * decay
    intra_out = jnp.einsum("hts,shp->thp", mixing, scaled, precision=HIGH)
    state_out = jnp.exp(cumulative)[:, :, None] * jnp.einsum(
        "tn,hpn->thp", c_proj, carry_state, precision=HIGH
    )
    to_end = jnp.exp(cumulative[-1][None, :] - cumulative)
    new_state = jnp.exp(cumulative[-1])[:, None, None] * carry_state + jnp.einsum(
        "sh,shp,sn->hpn", to_end, scaled, b_proj, precision=HIGH
    )
    return (new_state, intra_out + state_out)


def front_part(projected, rows_before, conv_w, conv_b, dt_b, a_lg):
    seq_rows = projected.shape[0]
    gate_in = projected[:, :INNER]
    conv_in = projected[:, INNER : INNER + CONVD]
    step_raw = projected[:, INNER + CONVD :]
    extended = jnp.concatenate([rows_before, conv_in], axis=0)
    convolved = conv_b + jnp.zeros((seq_rows, CONVD), jnp.float32)
    for offset in range(CONV):
        convolved = convolved + extended[offset : offset + seq_rows] * conv_w[:, offset]
    activated = jax.nn.silu(convolved)
    values = activated[:, :INNER].reshape(seq_rows, HEADS, HEADDIM)
    b_proj = activated[:, INNER : INNER + STATE]
    c_proj = activated[:, INNER + STATE :]
    step_size = jax.nn.softplus(step_raw + dt_b)
    decay_log = -jnp.exp(a_lg) * step_size
    return (gate_in, values, step_size, decay_log, b_proj, c_proj)


def core_part(front_out):
    gate_in, values, step_size, decay_log, b_proj, c_proj = front_out
    seq_rows = values.shape[0]
    blocks = seq_rows // GROUP
    scaled = values * step_size[:, :, None]

    def by_block(value):
        return value.reshape((blocks, GROUP) + value.shape[1:])

    start = jnp.zeros((HEADS, HEADDIM, STATE), jnp.float32)
    final_state, outputs = lax.scan(
        jax.checkpoint(ssd_block),
        start,
        (by_block(scaled), by_block(decay_log), by_block(b_proj), by_block(c_proj)),
    )
    total_decay = jnp.exp(jnp.sum(decay_log, axis=0))
    return (outputs.reshape(seq_rows, HEADS, HEADDIM), total_decay, final_state)


def tail_part(local_out, front_out, carried, skip_w, gate_g):
    gate_in, values, step_size, decay_log, b_proj, c_proj = front_out
    seq_rows = values.shape[0]
    cumulative = jnp.cumsum(decay_log, axis=0)
    incoming = jnp.exp(cumulative)[:, :, None] * jnp.einsum(
        "tn,hpn->thp", c_proj, carried, precision=HIGH
    )
    mixed = local_out + incoming + skip_w[:, None] * values
    gated = mixed.reshape(seq_rows, INNER) * jax.nn.silu(gate_in)
    return rms_scale(gated, gate_g)


def compose(earlier, later):
    return (earlier[0] * later[0], earlier[1] * later[0][:, None, None] + later[1])


def identity_pair():
    return (jnp.ones((HEADS,), jnp.float32), jnp.zeros((HEADS, HEADDIM, STATE), jnp.float32))


def halo_rows(projected):
    return shifted(projected[-(CONV - 1) :, INNER : INNER + CONVD], "seq", 1)


def state_prefix(total_decay, final_state):
    return entering((total_decay, final_state), "seq", compose, identity_pair())[1]


def reduce_grads(wide_grads, head_local):
    summed = lax.psum_scatter(wide_grads, "seq", scatter_dimension=0, tiled=True)
    heads = lax.psum(head_local, "seq")
    return (summed, heads)


def forward_layer(stream, params):
    norm_g, w_in, conv_w, conv_b, dt_b, a_lg, skip_w, gate_g, w_out = params
    normed = rms_scale(stream, norm_g).astype(jnp.bfloat16)
    projected = jnp.dot(normed, w_in, preferred_element_type=jnp.float32)
    rows_before = halo_rows(projected)
    front_out = front_part(projected, rows_before, conv_w, conv_b, dt_b, a_lg)
    local_out, total_decay, final_state = core_part(front_out)
    carried = state_prefix(total_decay, final_state)
    gated_low = tail_part(local_out, front_out, carried, skip_w, gate_g).astype(jnp.bfloat16)
    result = stream + jnp.dot(gated_low, w_out, preferred_element_type=jnp.float32)
    return (result, (projected, rows_before, carried))


def backward_layer(stream, stored, d_result, params):
    norm_g, w_in, conv_w, conv_b, dt_b, a_lg, skip_w, gate_g, w_out = params
    normed_f, norm_pull = jax.vjp(rms_scale, stream, norm_g)
    normed = normed_f.astype(jnp.bfloat16)
    projected, rows_before, carried = stored
    front_out, front_pull = jax.vjp(front_part, projected, rows_before, conv_w, conv_b, dt_b, a_lg)
    core_out, core_pull = jax.vjp(core_part, front_out)
    gated_f, tail_pull = jax.vjp(tail_part, core_out[0], front_out, carried, skip_w, gate_g)
    gated_low = gated_f.astype(jnp.bfloat16)
    d_low = d_result.astype(jnp.bfloat16)
    grad_out = lax.dot_general(
        gated_low, d_low, (((0,), (0,)), ((), ())), preferred_element_type=jnp.float32
    )
    d_gated = lax.dot_general(
        d_low, w_out, (((1,), (1,)), ((), ())), preferred_element_type=jnp.float32
    )
    d_local, d_front_tail, d_carried, d_skip_w, d_gate_g = tail_pull(d_gated)
    later_grad = prefix((core_out[1], d_carried), "seq", compose, identity_pair())[1]
    d_decay = jnp.sum(later_grad * carried, axis=(1, 2))
    (d_front_core,) = core_pull((d_local, d_decay, later_grad))
    d_front = jax.tree.map(jnp.add, d_front_tail, d_front_core)
    d_projected, d_rows, d_conv_w, d_conv_b, d_dt_b, d_a_lg = front_pull(d_front)
    returned = shifted(d_rows.astype(jnp.bfloat16), "seq", -1).astype(d_rows.dtype)
    d_projected = d_projected.at[-(CONV - 1) :, INNER : INNER + CONVD].add(returned)
    d_proj_low = d_projected.astype(jnp.bfloat16)
    grad_in = lax.dot_general(
        normed, d_proj_low, (((0,), (0,)), ((), ())), preferred_element_type=jnp.float32
    )
    d_normed = lax.dot_general(
        d_proj_low, w_in, (((1,), (1,)), ((), ())), preferred_element_type=jnp.float32
    )
    d_stream, d_norm_g = norm_pull(d_normed)
    wide_grads = (d_norm_g, grad_in, d_conv_w, d_conv_b, d_gate_g, grad_out)
    head_local = (d_dt_b, d_a_lg, d_skip_w)
    return (d_result + d_stream, wide_grads, head_local)


def per_device(
    inputs,
    cotangent,
    norm_gain,
    in_weight,
    conv_weight,
    conv_bias,
    dt_bias,
    a_log,
    d_skip,
    gate_norm_gain,
    out_weight,
):
    params = (
        norm_gain[0],
        in_weight[0],
        conv_weight[0],
        conv_bias[0],
        dt_bias[0],
        a_log[0],
        d_skip[0],
        gate_norm_gain[0],
        out_weight[0],
    )
    is_first = lax.axis_index("section") == 0
    micro_count = inputs.shape[0]
    tokens_here = inputs.shape[1]

    def pick(early, late):
        return jax.tree.map(
            lambda left_value, right_value: jnp.where(is_first, left_value, right_value),
            early,
            late,
        )

    incoming = jnp.zeros((tokens_here, D), jnp.bfloat16)
    stored_list = []
    sent_list = []
    for step_index in range(micro_count + 1):
        own_value = inputs[min(step_index, micro_count - 1)].astype(jnp.float32)
        stream = jnp.where(is_first, own_value, incoming.astype(jnp.float32))
        result, stored = forward_layer(stream, params)
        outgoing = result.astype(jnp.bfloat16)
        stored_list.append((stream, stored))
        sent_list.append(outgoing)
        if step_index < micro_count:
            incoming = shifted(outgoing, "section", 1)
    acts = jnp.stack([pick(sent_list[index], sent_list[index + 1]) for index in range(micro_count)])
    grad_incoming = jnp.zeros((tokens_here, D), jnp.bfloat16)
    back_list = []
    wide_total = None
    head_total = None
    for step_index in range(micro_count + 1):
        if step_index < micro_count:
            own_grad = cotangent[step_index].astype(jnp.float32)
        else:
            own_grad = jnp.zeros((tokens_here, D), jnp.float32)
        d_result = jnp.where(is_first, grad_incoming.astype(jnp.float32), own_grad)
        stream, stored = pick(
            stored_list[max(step_index - 1, 0)], stored_list[min(step_index + 1, micro_count)]
        )
        d_stream, wide_grads, head_local = backward_layer(stream, stored, d_result, params)
        back_list.append(d_stream)
        if step_index < micro_count:
            grad_incoming = shifted(d_stream.astype(jnp.bfloat16), "section", -1)
        if wide_total is None:
            wide_total, head_total = (wide_grads, head_local)
        else:
            wide_total = jax.tree.map(jnp.add, wide_total, wide_grads)
            head_total = jax.tree.map(jnp.add, head_total, head_local)
    wide_total, head_total = reduce_grads(wide_total, head_total)
    input_grads = jnp.stack(
        [pick(back_list[index + 1], back_list[index]) for index in range(micro_count)]
    )
    g_norm, g_in, g_conv_w, g_conv_b, g_gate, g_out = wide_total
    g_dt, g_alog, g_skip = head_total
    return (
        acts[None],
        input_grads[None],
        g_norm[None],
        g_in[None],
        g_conv_w[None],
        g_conv_b[None],
        g_dt[None],
        g_alog[None],
        g_skip[None],
        g_gate[None],
        g_out[None],
    )


def solution(mesh):
    in_specs = (
        P(None, "seq", None),
        P(None, "seq", None),
        P("section", None),
        P("section", None, None),
        P("section", None, None),
        P("section", None),
        P("section", None),
        P("section", None),
        P("section", None),
        P("section", None),
        P("section", None, None),
    )
    out_specs = (
        P("section", None, "seq", None),
        P("section", None, "seq", None),
        P("section", "seq"),
        P("section", "seq", None),
        P("section", "seq", None),
        P("section", "seq"),
        P("section", None),
        P("section", None),
        P("section", None),
        P("section", "seq"),
        P("section", "seq", None),
    )
    return jax.shard_map(
        per_device, mesh=mesh, in_specs=in_specs, out_specs=out_specs, check_vma=False
    )
```

profile of v0, /device:TPU:0, one launch (start us, length us, event | category | flops | bytes accessed | tf_op | source)
XLA Modules:
  0.0 3087.5 jit_solution(10431844748691931224)
XLA Ops:
  57.1 41.0 %all-reduce.48 = f32[768]{0:T(1024)S(1)} all-reduce(f32[768]{0:T(1024)S(1)} %exponential_dynamic-update-slice_fusion.2), channel_id=2, replica_groups=mesh['section'=2,'seq'=16] {'seq'}, use_global_device_ids=true, to_apply=%add.48 | all-reduce | flops 768 | bytes 6144
  104.9 222.2 %all-gather.19.cloned.1.call-done = f32[768,64,128]{2,1,0:T(8,128)} async-done(((f32[48,64,128]{2,1,0:T(8,128)}), f32[768,64,128]{2,1,0:T(8,128)}) %all-gather.19.cloned.1.call-update) | async-done | bytes 25165840 | tf_op jit(solution)/shard_map/all_gather | solution.py:28
  327.0 27.4 while.63
  434.1 38.5 %all-reduce.49 = f32[768]{0:T(1024)S(1)} all-reduce(f32[768]{0:T(1024)S(1)} %exponential_dynamic-update-slice_fusion.1), channel_id=4, replica_groups=mesh['section'=2,'seq'=16] {'seq'}, use_global_device_ids=true, to_apply=%add.49 | all-reduce | flops 768 | bytes 6144
  480.0 223.3 %all-gather.21.cloned.1.call-done = f32[768,64,128]{2,1,0:T(8,128)} async-done(((f32[48,64,128]{2,1,0:T(8,128)}), f32[768,64,128]{2,1,0:T(8,128)}) %all-gather.21.cloned.1.call-update) | async-done | bytes 25165840 | tf_op jit(solution)/shard_map/all_gather | solution.py:28
  703.3 27.4 while.64
  763.8 21.0 broadcast_select_fusion
  838.8 38.5 %all-reduce.50 = f32[768]{0:T(1024)S(1)} all-reduce(f32[768]{0:T(1024)S(1)} %exponential_dynamic-update-slice_fusion), channel_id=6, replica_groups=mesh['section'=2,'seq'=16] {'seq'}, use_global_device_ids=true, to_apply=%add.50 | all-reduce | flops 768 | bytes 6144
  878.4 23.3 fusion.157
  909.2 190.9 %all-gather.23.cloned.1.call-done = f32[768,64,128]{2,1,0:T(8,128)} async-done(((f32[48,64,128]{2,1,0:T(8,128)}), f32[768,64,128]{2,1,0:T(8,128)}) %all-gather.23.cloned.1.call-update) | async-done | bytes 25165840 | tf_op jit(solution)/shard_map/all_gather | solution.py:28
  1100.1 27.4 while.65
  1166.5 41.2 %all-reduce.58 = (bf16[768]{0:T(1024)(128)(2,1)S(1)}, bf16[768]{0:T(1024)(128)(2,1)}, bf16[768]{0:T(1024)(128)(2,1)}) all-reduce(bf16[768]{0:T(1024)(128)(2,1)S(1)} %dynamic-update-slice.9, bf16[768]{0:T(1024)(128)(2,1)S(1)} %dynamic-update-slice.10, ...), channel_id=8, replica_groups=mesh['section'=2,'seq'=16] {'seq'}, use_global_device_ids=true, to_apply=%add.51 | all-reduce | flops 2304 | bytes 9216
  1247.0 70.0 %all-gather.25.cloned.1.call-done = bf16[768,64,128]{2,1,0:T(8,128)(2,1)} async-done(((bf16[48,64,128]{2,1,0:T(8,128)(2,1)}), bf16[768,64,128]{2,1,0:T(8,128)(2,1)}) %all-gather.25.cloned.1.call-update) | async-done | bytes 12582928 | tf_op jit(solution)/shard_map/all_gather | solution.py:43
  1316.9 36.0 %while.66 = (s32[]{:T(128)}, f32[48,64,128]{2,1,0:T(8,128)S(1)}, s32[]{:T(128)}, bf16[16,48]{1,0:T(8,128)(2,1)}, bf16[16,48,64,128]{3,2,1,0:T(8,128)(2,1)}, /*index=5*/s32[]{:T(128)}, s32[]{:T(128)}, s32[]{:T(128)}, s32[]{:T(128)}) while((s32[]{:T(128)}, f32[48,64,128]{2,1,0:T(8,128)S(1)}, s32[]{:T(128)}, ...), condition=%wide.region_27.29_spmd.clone, body=%wide.region_26.28_spmd.clone.sunk | while | flops 1966136 | bytes 3932815 | solution.py:61
  1539.3 115.4 %all-gather.27.cloned.1.call-done = bf16[768,64,128]{2,1,0:T(8,128)(2,1)} async-done(((bf16[48,64,128]{2,1,0:T(8,128)(2,1)}), bf16[768,64,128]{2,1,0:T(8,128)(2,1)}) %all-gather.27.cloned.1.call-update) | async-done | bytes 12582928 | tf_op jit(solution)/shard_map/all_gather | solution.py:43
  1654.7 44.1 %while.67 = (s32[]{:T(128)}, f32[48,64,128]{2,1,0:T(8,128)S(1)}, s32[]{:T(128)}, bf16[16,48]{1,0:T(8,128)(2,1)}, bf16[16,48,64,128]{3,2,1,0:T(8,128)(2,1)}, /*index=5*/s32[]{:T(128)}, s32[]{:T(128)}, s32[]{:T(128)}, s32[]{:T(128)}) while((s32[]{:T(128)}, f32[48,64,128]{2,1,0:T(8,128)S(1)}, s32[]{:T(128)}, ...), condition=%wide.region_51.53_spmd.clone, body=%wide.region_50.52_spmd.clone.sunk | while | flops 1966136 | bytes 3932815 | solution.py:61
  1886.6 121.9 %all-gather.29.cloned.1.call-done = bf16[768,64,128]{2,1,0:T(8,128)(2,1)} async-done(((bf16[48,64,128]{2,1,0:T(8,128)(2,1)}), bf16[768,64,128]{2,1,0:T(8,128)(2,1)}) %all-gather.29.cloned.1.call-update) | async-done | bytes 12582928 | tf_op jit(solution)/shard_map/all_gather | solution.py:43
  2008.5 35.9 %while.68 = (s32[]{:T(128)}, f32[48,64,128]{2,1,0:T(8,128)S(1)}, s32[]{:T(128)}, bf16[16,48]{1,0:T(8,128)(2,1)}, bf16[16,48,64,128]{3,2,1,0:T(8,128)(2,1)}, /*index=5*/s32[]{:T(128)}, s32[]{:T(128)}, s32[]{:T(128)}, s32[]{:T(128)}) while((s32[]{:T(128)}, f32[48,64,128]{2,1,0:T(8,128)S(1)}, s32[]{:T(128)}, ...), condition=%wide.region_75.77_spmd.clone, body=%wide.region_74.76_spmd.clone.sunk | while | flops 1966136 | bytes 3932815 | solution.py:61
  2128.2 21.6 add_add_fusion.1
  2151.2 19.1 fusion.284
  2231.8 43.2 %add_add_fusion = f32[1536,6448]{1,0:T(8,128)} fusion(f32[1536,6448]{1,0:T(8,128)} %fusion.284, f32[1536,6448]{1,0:T(8,128)} %fusion.281, f32[256,6448]{0,1:T(8,128)} %scatter-add.14, f32[256,1536]{1,0:T(8,128)S(1)} %copy-done.35, f32[256]{0:T(256)S(1)} %fusion.504, f32[1536]{0:T(1024)S(1)} %reduce.16), kind=kOutput, calls=%fused_computation.18 | convolution fusion | flops 5093552128 | bytes 127032320 | tf_op jit(solution)/shard_map/dot_general | solution.py:200
  2329.8 79.6 %all-reduce.57 = (f32[1536]{0:T(1024)S(1)}, f32[3328]{0:T(1024)S(1)}, f32[1,48]{1,0:T(1,128)}, f32[1,48]{1,0:T(1,128)}, f32[1,48]{1,0:T(1,128)}, /*index=5*/f32[3072]{0:T(1024)S(1)}) all-reduce(f32[1536]{0:T(1024)S(1)} %add_add_fusion.11, f32[3328]{0:T(1024)S(1)} %add_add_fusion.9, ...), channel_id=14, replica_groups=mesh['section'=2,'seq'=16] {'seq'}, use_global_device_ids=true, to_apply=%region_96.98.clone | all-reduce | flops 8080 | bytes 64640
  2417.0 79.5 %reduce-scatter.8.cloned.1.call-done = f32[192,1536]{1,0:T(8,128)} async-done(((f32[3072,1536]{1,0:T(8,128)}), f32[192,1536]{1,0:T(8,128)}) %reduce-scatter.8.cloned.1.call-update) | async-done | bytes 1179664 | tf_op jit(solution)/shard_map/reduce_scatter | solution.py:157
  2496.5 584.3 %reduce-scatter.6.cloned.1.call-done = f32[96,6448]{1,0:T(8,128)} async-done(((f32[1536,6448]{1,0:T(8,128)}), f32[96,6448]{1,0:T(8,128)}) %reduce-scatter.6.cloned.1.call-update) | async-done | bytes 2476048 | tf_op jit(solution)/shard_map/reduce_scatter | solution.py:157
  (1216 shorter events, 1088.3 us)
Async XLA Ops:
  7.2 319.9 %all-gather.19.cloned.1.call-start = ((), (), s32[]{:S(2)}) async-start(), calls=%async_computation.5 | async-start | bytes 26738688 | tf_op jit(solution)/shard_map/all_gather | solution.py:28
  23.4 12.9 collective-permute-start
  32.2 1747.4 %copy-start.126 = (f32[3328]{0:T(1024)}, f32[3328]{0:T(1024)S(1)}, u32[]{:S(2)}) copy-start(f32[3328]{0:T(1024)S(1)} %get-tuple-element.1190) | copy-start | bytes 39940
  32.2 1747.4 %copy-start.128 = (f32[3328]{0:T(1024)}, f32[3328]{0:T(1024)S(1)}, u32[]{:S(2)}) copy-start(f32[3328]{0:T(1024)S(1)} %get-tuple-element.1191) | copy-start | bytes 39940
  32.3 1747.4 %copy-start.130 = (f32[3328]{0:T(1024)}, f32[3328]{0:T(1024)S(1)}, u32[]{:S(2)}) copy-start(f32[3328]{0:T(1024)S(1)} %get-tuple-element.1192) | copy-start | bytes 39940
  32.3 1747.4 %copy-start.132 = (f32[3328]{0:T(1024)}, f32[3328]{0:T(1024)S(1)}, u32[]{:S(2)}) copy-start(f32[3328]{0:T(1024)S(1)} %get-tuple-element.1193) | copy-start | bytes 39940
  54.9 648.4 %all-gather.21.cloned.1.call-start = ((), (), s32[]{:S(2)}) async-start(), calls=%async_computation.6 | async-start | bytes 26738688 | tf_op jit(solution)/shard_map/all_gather | solution.py:28
  384.0 3.2 collective-permute-start.1
  403.4 10.3 collective-permute-start.2
  433.2 666.9 %all-gather.23.cloned.1.call-start = ((), (), s32[]{:S(2)}) async-start(), calls=%async_computation.7 | async-start | bytes 26738688 | tf_op jit(solution)/shard_map/all_gather | solution.py:28
  756.8 3.4 collective-permute-start.3
  789.2 15.9 collective-permute-start.4
  795.6 370.6 %copy-start.259 = (f32[48]{0:T(128)}, f32[48]{0:T(128)S(1)}, u32[]{:S(2)}) copy-start(f32[48]{0:T(128)S(1)} %get-tuple-element.1300) | copy-start | bytes 580
  830.0 487.0 %all-gather.25.cloned.1.call-start = ((), (), s32[]{:S(2)}) async-start(), calls=%async_computation.8 | async-start | bytes 13369344 | tf_op jit(solution)/shard_map/all_gather | solution.py:43
  1165.7 489.1 %all-gather.27.cloned.1.call-start = ((), (), s32[]{:S(2)}) async-start(), calls=%async_computation.9 | async-start | bytes 13369344 | tf_op jit(solution)/shard_map/all_gather | solution.py:43
  1438.4 7.8 collective-permute-start.5
  1479.9 4.3 collective-permute-start.6
  1502.3 506.3 %all-gather.29.cloned.1.call-start = ((), (), s32[]{:S(2)}) async-start(), calls=%async_computation.10 | async-start | bytes 13369344 | tf_op jit(solution)/shard_map/all_gather | solution.py:43
  1795.2 7.8 collective-permute-start.7
  1835.1 4.8 collective-permute-start.8
  1855.3 560.2 %reduce-scatter.10.cloned.1.call-start = ((), (), s32[]{:S(2)}) async-start(), calls=%async_computation.11 | async-start | bytes 1810432
  2128.2 368.3 %reduce-scatter.8.cloned.1.call-start = ((), (), s32[]{:S(2)}) async-start(), calls=%async_computation.4 | async-start | bytes 20054016 | tf_op jit(solution)/shard_map/reduce_scatter | solution.py:157
  2149.8 931.0 %reduce-scatter.6.cloned.1.call-start = ((), (), s32[]{:S(2)}) async-start(), calls=%async_computation.3 | async-start | bytes 42614784 | tf_op jit(solution)/shard_map/reduce_scatter | solution.py:157
  2208.6 8.2 collective-permute-start.9
  (296 other events, 3933.3 us)
Sparse Core Ops, SparseCore 0:
  55.0 271.9 all-gather.18
  433.3 269.9 all-gather.20
  830.1 269.9 all-gather.22
  1165.8 151.1 all-gather.24
  1502.4 152.3 all-gather.26
  1855.4 153.0 all-gather.28
  2128.3 77.6 reduce-scatter.9
  2213.3 283.0 reduce-scatter.7
  2504.2 576.5 reduce-scatter.5
where the time goes:
time: 3100 us; the launch traced here: 3090 us
  waiting for transfers between devices  1610 us (52%)
  matrix products  570 us (18%)
  other arithmetic  457 us (15%)
  blocking collectives  239 us (8%)
  local copies, waits for them, and re-layouts  160 us (5%)
    reduce_scatter x2, waiting for transfers between devices, reduce_grads(): lax.psum_scatter(wide_grads, 'seq', scatter_dimension=0, tiled=True)  664 us
    all_gather x3, waiting for transfers between devices, entering(): pieces = jax.tree.map(lambda part: lax.all_gather(part, axis), value)  636 us
    all_gather x3, waiting for transfers between devices, prefix(): lax.all_gather(part.astype(kind), axis)  307 us
    unnamed x5, blocking collectives  239 us
    dot_general x12, matrix products, ssd_block(): intra_out = jnp.einsum('hts,shp->thp', mixing, scaled, precision=HIGH)  186 us
    dot_general x3, matrix products, backward_layer(): lax.dot_general(normed, d_proj_low, (((0,), (0,)), ((), ())), preferred_e...  81.3 us
    select_n x45, other arithmetic, entering_lap(): jnp.where(position < mine, new, old)  79.6 us
    select_n x48, other arithmetic, prefix_lap(): return jax.tree.map(lambda a, b: jnp.where(reached, a, b), new, before)  73.5 us
  transfers between devices with their start and end apart: 19, of which 11 were waited for; matrix products, arithmetic and copies ran while one was open for 13% of the time, Pallas kernels for 0%

commit v1 on v0

v1 whole, which is shorter than its diff:
```python
import functools

import jax
import jax.numpy as jnp
from jax import lax
from jax.experimental import pallas as pl
from jax.experimental.pallas import tpu as pltpu
from jax.sharding import PartitionSpec as P

D = 1536
INNER = 3072
STATE = 128
HEADS = 48
HEADDIM = 64
CONV = 4
CONVD = 3328
PROJ = 6448
ROWS = 256
PAIRS = INNER // 128
PLANE = 4
LANES = INNER // PLANE
QUARTER = 1664
EPS = 1e-05
MIB = 2**20
MESH = pl.DeviceIdType.MESH
F32 = jnp.float32
BF16 = jnp.bfloat16


def dot_nn(a, b):
    return lax.dot_general(a, b, (((1,), (0,)), ((), ())), preferred_element_type=F32)


def dot_tn(a, b):
    return lax.dot_general(a, b, (((0,), (0,)), ((), ())), preferred_element_type=F32)


def dot_nt(a, b):
    return lax.dot_general(a, b, (((1,), (1,)), ((), ())), preferred_element_type=F32)


def split3(v):
    high = v.astype(BF16)
    rest = v - high.astype(F32)
    mid = rest.astype(BF16)
    return high, mid, (rest - mid.astype(F32)).astype(BF16)


def split2(v):
    high = v.astype(BF16)
    return high, (v - high.astype(F32)).astype(BF16)


def fine(dot, a, b):
    return dot(a[0], b[0]) + (dot(a[0], b[1]) + dot(a[1], b[0]))


def halves(ref):
    return ref[:, 0:128], ref[:, 128:256]


def exact_right(v, ones):
    a, b, c = split3(v)
    return dot_nn(a, ones) + (dot_nn(b, ones) + dot_nn(c, ones))


def exact_left(ones, v):
    a, b, c = split3(v)
    return dot_nn(ones, a) + (dot_nn(ones, b) + dot_nn(ones, c))


def iota(shape, dim):
    return lax.broadcasted_iota(jnp.int32, shape, dim)


def expander(pair):
    head_of = 2 * pair + (iota((128, 128), 1) >= HEADDIM).astype(jnp.int32)
    return (iota((128, 128), 0) == head_of).astype(F32).astype(BF16)


def collector(pair):
    head_of = 2 * pair + (iota((128, 128), 0) >= HEADDIM).astype(jnp.int32)
    return (iota((128, 128), 1) == head_of).astype(F32).astype(BF16)


def triangle(lower):
    rows, cols = iota((ROWS, ROWS), 0), iota((ROWS, ROWS), 1)
    return ((rows >= cols) if lower else (rows <= cols)).astype(F32).astype(BF16)


def sigmoid(v):
    return 1.0 / (1.0 + jnp.exp(-v))


def extended(block, halo):
    return jnp.concatenate([halo, block], axis=0)


def conv_pre(ext, taps):
    out = taps[4:5] + taps[0:1] * ext[5 : 5 + ROWS]
    for k in range(1, CONV):
        out = out + taps[k : k + 1] * ext[5 + k : 5 + k + ROWS]
    return out


def conv_back(d_pre, taps):
    ext = jnp.concatenate([d_pre, jnp.zeros((8, d_pre.shape[1]), F32)], axis=0)
    out = taps[3:4] * d_pre
    for k in range(CONV - 1):
        out = out + taps[k : k + 1] * ext[3 - k : 3 - k + ROWS]
    return out


def tap_grads(d_pre, ext):
    rows = [jnp.sum(d_pre * ext[5 + k : 5 + k + ROWS], axis=0, keepdims=True) for k in range(CONV)]
    rows.append(jnp.sum(d_pre, axis=0, keepdims=True))
    rows.append(jnp.zeros((3, d_pre.shape[1]), F32))
    return jnp.concatenate(rows, axis=0)


def step_parts(raw_ref, hp_ref):
    real = iota((ROWS, 128), 1) < HEADS
    raw = jnp.where(real, raw_ref[...], 0.0) + hp_ref[0:1, :]
    step = jnp.maximum(raw, 0.0) + jnp.log1p(jnp.exp(-jnp.abs(raw)))
    step = jnp.where(real, step, 0.0)
    rate = jnp.where(real[0:1], -jnp.exp(hp_ref[1:2, :]), 0.0)
    return raw, step, rate


def mm_kernel(flag_ref, x_ref, own_ref, other_ref, o_ref, *, nt):
    dot = dot_nt if nt else dot_nn

    @pl.when(flag_ref[0] == 1)
    def _():
        o_ref[...] = dot(x_ref[...], own_ref[...])

    @pl.when(flag_ref[0] == 0)
    def _():
        o_ref[...] = dot(x_ref[...], other_ref[...])


def mm(x, own, other, flag, nt, tile):
    rows, depth = x.shape
    width = own.shape[0] if nt else own.shape[1]
    block = (tile, depth) if nt else (depth, tile)

    def place(j, keep):
        return (j * keep, 0) if nt else (0, j * keep)

    return pl.pallas_call(
        functools.partial(mm_kernel, nt=nt),
        grid_spec=pltpu.PrefetchScalarGridSpec(
            num_scalar_prefetch=1,
            grid=(pl.cdiv(width, tile),),
            in_specs=[
                pl.BlockSpec((rows, depth), lambda j, f: (0, 0)),
                pl.BlockSpec(block, lambda j, f: place(j, f[0])),
                pl.BlockSpec(block, lambda j, f: place(j, 1 - f[0])),
            ],
            out_specs=pl.BlockSpec((rows, tile), lambda j, f: (0, j)),
        ),
        out_shape=jax.ShapeDtypeStruct((rows, width), F32),
        compiler_params=pltpu.CompilerParams(vmem_limit_bytes=48 * MIB),
        cost_estimate=pl.CostEstimate(
            flops=2 * rows * depth * width, bytes_accessed=2 * depth * width, transcendentals=0
        ),
    )(flag, x, own, other)


def front_kernel(
    x_ref, b_ref, c_ref, raw_ref, xh_ref, bh_ref, ch_ref, xw_ref, bw_ref, cw_ref, hp_ref,
    val_ref, state_ref, dec_ref, step_ref, cum_ref, cumt_ref, bo_ref, co_ref, g_ref,
):
    j = pl.program_id(0)

    @pl.when(j == 0)
    def _():
        _, step, rate = step_parts(raw_ref, hp_ref)
        step_ref[...] = step
        cum = exact_left(triangle(True), rate * step)
        cum_ref[...] = cum
        cumt_ref[...] = cum.T
        pre = conv_pre(extended(b_ref[...], bh_ref[...]), bw_ref[...])
        b_low = split2(pre * sigmoid(pre))
        bo_ref[...] = jnp.concatenate(b_low, axis=1)
        pre = conv_pre(extended(c_ref[...], ch_ref[...]), cw_ref[...])
        c_low = split2(pre * sigmoid(pre))
        co_ref[...] = jnp.concatenate(c_low, axis=1)
        seen = iota((ROWS, ROWS), 0) >= iota((ROWS, ROWS), 1)
        g_ref[...] = jnp.where(seen, fine(dot_nt, c_low, b_low), 0.0)

    pre = conv_pre(extended(x_ref[...], xh_ref[...]), xw_ref[...])
    values = pre * sigmoid(pre)
    heads = expander(j)
    step = exact_right(step_ref[...], heads)
    cum = exact_right(cum_ref[...], heads)
    last = cum[ROWS - 1 : ROWS]
    scaled = values * step
    val_ref[...] = values
    state_ref[...] = fine(dot_tn, halves(bo_ref), split2(scaled * jnp.exp(last - cum)))
    dec_ref[...] = jnp.broadcast_to(jnp.exp(last), (8, 128))


def whole(shape):
    return pl.BlockSpec(shape, lambda j: (0, 0))


def lanes(rows, first=0):
    return pl.BlockSpec((rows, 128), lambda j: (0, first + j))


def fixed(rows, at):
    return pl.BlockSpec((rows, 128), lambda j: (0, at))


def sds(rows, cols, dtype):
    return jax.ShapeDtypeStruct((rows, cols), dtype)


def grid_params():
    return pltpu.CompilerParams(vmem_limit_bytes=48 * MIB)


def front(proj, halo, taps, hp):
    return pl.pallas_call(
        front_kernel,
        grid=(PAIRS,),
        in_specs=[
            lanes(ROWS, 24), fixed(ROWS, 48), fixed(ROWS, 49), fixed(ROWS, 50),
            lanes(8), fixed(8, 24), fixed(8, 25),
            lanes(8), fixed(8, 24), fixed(8, 25),
            whole((8, 128)),
        ],
        out_specs=[
            lanes(ROWS), lanes(128), lanes(8),
            whole((ROWS, 128)), whole((ROWS, 128)), whole((128, ROWS)),
            whole((ROWS, 256)), whole((ROWS, 256)), whole((ROWS, ROWS)),
        ],
        out_shape=[
            sds(ROWS, INNER, F32), sds(128, INNER, F32), sds(8, INNER, F32),
            sds(ROWS, 128, F32), sds(ROWS, 128, F32), sds(128, ROWS, F32),
            sds(ROWS, 256, BF16), sds(ROWS, 256, BF16), sds(ROWS, ROWS, F32),
        ],
        compiler_params=grid_params(),
        cost_estimate=pl.CostEstimate(flops=2 * 10**9, bytes_accessed=10 * MIB, transcendentals=10**6),
    )(proj, proj, proj, proj, halo, halo, halo, taps, taps, taps, hp)


def exchange_kernel(
    n, rev, s_ref, d_ref, o_ref, inbox, dbox, parts, decs, total, chain_out, chain_in, outbox,
    send_a, recv_a, send_d, recv_d, send_c, recv_c, send_o, recv_o,
):
    planes = n // PLANE
    section = lax.axis_index("section")
    q = lax.axis_index("seq")
    u = n - 1 - q if rev else q
    spot, level = lax.rem(u, PLANE), u // PLANE

    def device(at):
        return (section, n - 1 - at if rev else at)

    peers = [lax.rem(spot + k, PLANE) for k in range(1, PLANE)]
    barrier = pltpu.get_barrier_semaphore()
    for peer in peers:
        pl.semaphore_signal(barrier, inc=1, device_id=device(level * PLANE + peer), device_id_type=MESH)

    @pl.when(level > 0)
    def _():
        pl.semaphore_signal(barrier, inc=1, device_id=device(u - PLANE), device_id_type=MESH)

    pl.semaphore_wait(barrier, PLANE - 1 + (level < planes - 1).astype(jnp.int32))

    def group(at):
        return pl.ds(pl.multiple_of(at * LANES, LANES), LANES)

    first = []
    for k, peer in enumerate(peers):
        to = device(level * PLANE + peer)
        first.append(
            pltpu.make_async_remote_copy(
                src_ref=d_ref.at[:, group(peer)], dst_ref=dbox.at[spot],
                send_sem=send_d.at[k], recv_sem=recv_d.at[k], device_id=to, device_id_type=MESH,
            )
        )
        first.append(
            pltpu.make_async_remote_copy(
                src_ref=s_ref.at[:, group(peer)], dst_ref=inbox.at[spot],
                send_sem=send_a.at[k], recv_sem=recv_a.at[k], device_id=to, device_id_type=MESH,
            )
        )
    for copy in first:
        copy.start()
    inbox[spot] = s_ref[:, group(spot)]
    dbox[spot] = d_ref[:, group(spot)]
    for copy in first:
        copy.wait()

    cuts = LANES // 256
    for b in range(cuts):
        at = slice(b * 256, b * 256 + 256)
        state = inbox[0, :, at].astype(F32)
        decay = dbox[0, 0:1, at]
        for p in range(1, PLANE):
            parts[p, :, at] = state
            decs[p, 0:1, at] = decay
            d = dbox[p, 0:1, at]
            state = d * state + inbox[p, :, at].astype(F32)
            decay = decay * d
        total[:, at] = state
        decs[0, 0:1, at] = decay

    def chain(b):
        return pltpu.make_async_remote_copy(
            src_ref=chain_out.at[b], dst_ref=chain_in.at[b],
            send_sem=send_c.at[b], recv_sem=recv_c.at[b],
            device_id=device(lax.rem(u + PLANE, n)), device_id_type=MESH,
        )

    last = []
    for b in range(cuts):
        at = slice(b * 256, b * 256 + 256)

        @pl.when(level > 0)
        def _():
            chain(b).wait_recv()

        @pl.when(level == 0)
        def _():
            chain_in[b] = jnp.zeros((128, 256), chain_in.dtype)

        enter = chain_in[b].astype(F32)

        @pl.when(level < planes - 1)
        def _():
            chain_out[b] = (decs[0, 0:1, at] * enter + total[:, at]).astype(chain_out.dtype)
            chain(b).start()

        outbox[0, :, at] = enter.astype(outbox.dtype)
        for p in range(1, PLANE):
            outbox[p, :, at] = (decs[p, 0:1, at] * enter + parts[p, :, at]).astype(outbox.dtype)
        mine = pl.ds(pl.multiple_of(spot * LANES + b * 256, 256), 256)
        o_ref[:, mine] = outbox[spot, :, at]
        for k, peer in enumerate(peers):
            copy = pltpu.make_async_remote_copy(
                src_ref=outbox.at[peer, :, pl.ds(b * 256, 256)], dst_ref=o_ref.at[:, mine],
                send_sem=send_o.at[b * 3 + k], recv_sem=recv_o.at[b * 3 + k],
                device_id=device(level * PLANE + peer), device_id_type=MESH,
            )
            copy.start()
            last.append(copy)
    for copy in last:
        copy.wait()

    @pl.when(level < planes - 1)
    def _():
        for b in range(cuts):
            chain(b).wait_send()


def exchange(state, decay, n, rev):
    vmem = pl.BlockSpec(memory_space=pltpu.VMEM)
    dma = pltpu.SemaphoreType.DMA
    cuts = LANES // 256
    return pl.pallas_call(
        functools.partial(exchange_kernel, n, rev),
        out_shape=sds(128, INNER, state.dtype),
        in_specs=[vmem, vmem],
        out_specs=vmem,
        scratch_shapes=[
            pltpu.VMEM((PLANE, 128, LANES), state.dtype),
            pltpu.VMEM((PLANE, 8, LANES), F32),
            pltpu.VMEM((PLANE, 128, LANES), F32),
            pltpu.VMEM((PLANE, 8, LANES), F32),
            pltpu.VMEM((128, LANES), F32),
            pltpu.VMEM((cuts, 128, 256), state.dtype),
            pltpu.VMEM((cuts, 128, 256), state.dtype),
            pltpu.VMEM((PLANE, 128, LANES), state.dtype),
            dma((3,)), dma((3,)), dma((3,)), dma((3,)),
            dma((cuts,)), dma((cuts,)), dma((3 * cuts,)), dma((3 * cuts,)),
        ],
        compiler_params=pltpu.CompilerParams(
            collective_id=2 if rev else 1, has_side_effects=True, vmem_limit_bytes=32 * MIB
        ),
    )(state, decay)


def decay_block(cum, row):
    return jnp.exp(jnp.minimum(cum - row, 0.0))


def mix_kernel(
    g_ref, step_ref, cum_ref, cumt_ref, val_ref, gate_ref, c_ref, car_ref, lp_ref, gain_ref,
    y_ref, low_ref, gated_ref, sum_ref,
):
    j = pl.program_id(0)
    heads = expander(j)
    cum = exact_right(cum_ref[...], heads)
    values = val_ref[...]
    scaled = split2(values * exact_right(step_ref[...], heads))
    early = iota((ROWS, 128), 1) < HEADDIM
    y = jnp.exp(cum) * fine(dot_nn, halves(c_ref), split2(car_ref[...])) + lp_ref[0:1, :] * values
    for i in range(2):
        row = cumt_ref[pl.ds(2 * j + i, 1), :]
        decay = decay_block(cum[:, i * HEADDIM : i * HEADDIM + 1], row)
        half = early if i == 0 else ~early
        part = [jnp.where(half, v, jnp.zeros((), BF16)) for v in scaled]
        y = y + fine(dot_nn, split2(g_ref[...] * decay), part)
    y_ref[...] = y
    gate = gate_ref[...]
    gated = y * (gate * sigmoid(gate))
    gated_ref[j] = gated

    @pl.when(j == 0)
    def _():
        sum_ref[...] = jnp.zeros_like(sum_ref)

    sum_ref[...] += gated * gated

    @pl.when(j == PAIRS - 1)
    def _():
        mean = jnp.sum(sum_ref[...], axis=1, keepdims=True) * (1.0 / INNER)
        scale = lax.rsqrt(mean + EPS)
        for k in range(PAIRS):
            at = slice(k * 128, k * 128 + 128)
            low_ref[:, at] = (gated_ref[k] * scale * gain_ref[1:2, at]).astype(BF16)


def mix(g, step, cum, cumt, values, proj, c, carried, lp):
    return pl.pallas_call(
        mix_kernel,
        grid=(PAIRS,),
        in_specs=[
            whole((ROWS, ROWS)), whole((ROWS, 128)), whole((ROWS, 128)), whole((128, ROWS)),
            lanes(ROWS), lanes(ROWS), whole((ROWS, 256)), lanes(128), lanes(8),
            whole((8, INNER)),
        ],
        out_specs=[lanes(ROWS), whole((ROWS, INNER))],
        out_shape=[sds(ROWS, INNER, F32), sds(ROWS, INNER, BF16)],
        scratch_shapes=[pltpu.VMEM((PAIRS, ROWS, 128), F32), pltpu.VMEM((ROWS, 128), F32)],
        compiler_params=grid_params(),
        cost_estimate=pl.CostEstimate(flops=3 * 10**9, bytes_accessed=14 * MIB, transcendentals=4 * 10**6),
    )(g, step, cum, cumt, values, proj, c, carried, lp, lp)


def gate_back_kernel(
    dg_ref, y_ref, gate_ref, cum_ref, c_ref, lp_ref, dy_ref, dgate_ref, gain_ref, dcar_ref
):
    def piece(k):
        at = pl.ds(pl.multiple_of(k * 128, 128), 128)
        gate = gate_ref[:, at]
        s = sigmoid(gate)
        y = y_ref[:, at]
        return at, gate, s, y, y * (gate * s)

    def first(k, sums):
        at, _, _, _, gated = piece(k)
        w = dg_ref[:, at] * lp_ref[1:2, at]
        return sums[0] + gated * gated, sums[1] + w * gated

    zero = jnp.zeros((ROWS, 128), F32)
    squares, cross = lax.fori_loop(0, PAIRS, first, (zero, zero))
    r = lax.rsqrt(jnp.sum(squares, axis=1, keepdims=True) * (1.0 / INNER) + EPS)
    m = jnp.sum(cross, axis=1, keepdims=True) * (1.0 / INNER) * r * r

    def second(k, carry):
        at, gate, s, y, gated = piece(k)
        dg = dg_ref[:, at]
        gain_ref[:, at] = jnp.broadcast_to(jnp.sum(dg * gated * r, axis=0, keepdims=True), (8, 128))
        d_gated = r * (dg * lp_ref[1:2, at] - gated * m)
        dy = d_gated * (gate * s)
        dy_ref[:, at] = dy
        dgate_ref[:, at] = (d_gated * y * (s * (1.0 + gate * (1.0 - s)))).astype(BF16)
        cum = exact_right(cum_ref[...], expander(k))
        dcar_ref[:, at] = fine(dot_tn, halves(c_ref), split2(dy * jnp.exp(cum))).astype(BF16)
        return carry

    lax.fori_loop(0, PAIRS, second, 0)


def gate_back(dg, y, proj, cum, c, lp):
    return pl.pallas_call(
        gate_back_kernel,
        grid=(1,),
        in_specs=[
            whole((ROWS, INNER)), whole((ROWS, INNER)), whole((ROWS, INNER)),
            whole((ROWS, 128)), whole((ROWS, 256)), whole((8, INNER)),
        ],
        out_specs=[whole((ROWS, INNER)), whole((ROWS, INNER)), whole((8, INNER)), whole((128, INNER))],
        out_shape=[sds(ROWS, INNER, F32), sds(ROWS, INNER, BF16), sds(8, INNER, F32), sds(128, INNER, BF16)],
        compiler_params=grid_params(),
        cost_estimate=pl.CostEstimate(flops=10**9, bytes_accessed=16 * MIB, transcendentals=2 * 10**6),
    )(dg, y, proj, cum, c, lp)


def core_back_kernel(
    x_ref, b_ref, c_ref, raw_ref, xh_ref, bh_ref, ch_ref, xw_ref, bw_ref, cw_ref, hp_ref,
    step_ref, cum_ref, cumt_ref, g_ref, bo_ref, co_ref, dy_ref, car_ref, late_ref, lp_ref,
    dx_ref, dbc_ref, tail_ref, tailbc_ref, head_ref, headbc_ref, taps_ref, tapsbc_ref, draw_ref, hg_ref,
    dg_acc, dc_acc, db_acc, dcum_acc, dstep_acc, rows_acc,
):
    j = pl.program_id(0)

    @pl.when(j == 0)
    def _():
        for acc in (dg_acc, dc_acc, db_acc, dcum_acc, dstep_acc, rows_acc):
            acc[...] = jnp.zeros_like(acc)

    ext = extended(x_ref[...], xh_ref[...])
    pre = conv_pre(ext, xw_ref[...])
    sig = sigmoid(pre)
    values = pre * sig
    heads, collect = expander(j), collector(j)
    step = exact_right(step_ref[...], heads)
    cum = exact_right(cum_ref[...], heads)
    last = cum[ROWS - 1 : ROWS]
    to_end, from_start = jnp.exp(last - cum), jnp.exp(cum)
    scaled = values * step
    scaled_parts = split2(scaled)
    scaled_low = scaled_parts[0]
    dy = dy_ref[...]
    dy_parts = split2(dy)
    dy_low = dy_parts[0]
    early = iota((ROWS, 128), 1) < HEADDIM
    y_in = jnp.zeros((ROWS, 128), F32)
    d_scaled = jnp.zeros((ROWS, 128), F32)
    for i in range(2):
        half = early if i == 0 else ~early
        row = cumt_ref[pl.ds(2 * j + i, 1), :]
        decay = decay_block(cum[:, i * HEADDIM : i * HEADDIM + 1], row)
        mixing = (g_ref[...] * decay).astype(BF16)
        dy_half = [jnp.where(half, part, jnp.zeros((), BF16)) for part in dy_parts]
        y_in = y_in + dot_nn(mixing, jnp.where(half, scaled_low, jnp.zeros((), BF16)))
        d_scaled = d_scaled + dot_tn(mixing, dy_half[0])
        dg_acc[...] += fine(dot_nt, dy_half, scaled_parts) * decay
    car, late = car_ref[...], late_ref[...]
    car_parts = split2(car)
    y_across = from_start * fine(dot_nn, halves(co_ref), car_parts)
    d_ended = dot_nn(bo_ref[:, 0:128], late)
    ended = scaled * to_end
    dc_acc[...] += fine(dot_nt, split2(dy * from_start), car_parts)
    ended_parts = split2(ended)
    db_acc[...] += dot_nt(ended_parts[0], late) + dot_nt(ended_parts[1], late)
    d_total = d_scaled + to_end * d_ended
    through_end = ended * d_ended
    d_cum = dy_low.astype(F32) * y_in + dy * y_across - scaled_low.astype(F32) * d_scaled - through_end
    dcum_acc[...] += exact_right(d_cum, collect)
    dstep_acc[...] += exact_right(d_total * values, collect)
    at_last = jnp.exp(last) * jnp.sum(late.astype(F32) * car, axis=0, keepdims=True)
    at_last = at_last + jnp.sum(through_end, axis=0, keepdims=True)
    skip = jnp.sum(dy * values, axis=0, keepdims=True)
    rows_acc[...] += exact_right(jnp.concatenate([at_last, skip, jnp.zeros((6, 128), F32)], axis=0), collect)
    d_values = lp_ref[0:1, :] * dy + step * d_total
    d_pre = d_values * (sig * (1.0 + pre * (1.0 - sig)))
    taps_ref[...] = tap_grads(d_pre, ext)
    head_ref[...] = d_pre[0:8]
    d_conv = conv_back(d_pre, xw_ref[...])
    dx_ref[...] = d_conv.astype(BF16)
    tail_ref[...] = d_conv[ROWS - 8 : ROWS]

    @pl.when(j == PAIRS - 1)
    def _():
        seen = iota((ROWS, ROWS), 0) >= iota((ROWS, ROWS), 1)
        d_g = split2(jnp.where(seen, dg_acc[...], 0.0))
        d_c = dc_acc[...] + fine(dot_nn, d_g, halves(bo_ref))
        d_b = db_acc[...] + fine(dot_tn, d_g, halves(co_ref))
        for k, (block, halo, taps, grad) in enumerate(
            ((b_ref, bh_ref, bw_ref, d_b), (c_ref, ch_ref, cw_ref, d_c))
        ):
            at = slice(k * 128, k * 128 + 128)
            ext_k = extended(block[...], halo[...])
            pre_k = conv_pre(ext_k, taps[...])
            sig_k = sigmoid(pre_k)
            d_pre_k = grad * (sig_k * (1.0 + pre_k * (1.0 - sig_k)))
            tapsbc_ref[:, at] = tap_grads(d_pre_k, ext_k)
            headbc_ref[:, at] = d_pre_k[0:8]
            d_conv_k = conv_back(d_pre_k, taps[...])
            dbc_ref[:, at] = d_conv_k.astype(BF16)
            tailbc_ref[:, at] = d_conv_k[ROWS - 8 : ROWS]
        raw, step_all, rate = step_parts(raw_ref, hp_ref)
        end = iota((ROWS, 128), 0) == ROWS - 1
        d_cum_all = dcum_acc[...] + jnp.where(end, rows_acc[0:1, :], 0.0)
        d_log = exact_left(triangle(False), d_cum_all)
        d_step = dstep_acc[...] + rate * d_log
        d_raw = jnp.where(iota((ROWS, 128), 1) < HEADS, d_step * sigmoid(raw), 0.0)
        draw_ref[...] = d_raw.astype(BF16)
        hg_ref[...] = jnp.concatenate(
            [
                jnp.sum(d_raw, axis=0, keepdims=True),
                jnp.sum(d_log * rate * step_all, axis=0, keepdims=True),
                rows_acc[1:2, :],
                jnp.zeros((5, 128), F32),
            ],
            axis=0,
        )


def core_back(proj, halo, taps, hp, step, cum, cumt, g, b, c, dy, carried, late, lp):
    return pl.pallas_call(
        core_back_kernel,
        grid=(PAIRS,),
        in_specs=[
            lanes(ROWS, 24), fixed(ROWS, 48), fixed(ROWS, 49), fixed(ROWS, 50),
            lanes(8), fixed(8, 24), fixed(8, 25),
            lanes(8), fixed(8, 24), fixed(8, 25),
            whole((8, 128)),
            whole((ROWS, 128)), whole((ROWS, 128)), whole((128, ROWS)), whole((ROWS, ROWS)),
            whole((ROWS, 256)), whole((ROWS, 256)),
            lanes(ROWS), lanes(128), lanes(128), lanes(8),
        ],
        out_specs=[
            lanes(ROWS), whole((ROWS, 256)), lanes(8), whole((8, 256)), lanes(8), whole((8, 256)),
            lanes(8), whole((8, 256)), whole((ROWS, 128)), whole((8, 128)),
        ],
        out_shape=[
            sds(ROWS, INNER, BF16), sds(ROWS, 256, BF16), sds(8, INNER, F32), sds(8, 256, F32),
            sds(8, INNER, F32), sds(8, 256, F32), sds(8, INNER, F32), sds(8, 256, F32),
            sds(ROWS, 128, BF16), sds(8, 128, F32),
        ],
        scratch_shapes=[
            pltpu.VMEM((ROWS, ROWS), F32),
            pltpu.VMEM((ROWS, 128), F32), pltpu.VMEM((ROWS, 128), F32), pltpu.VMEM((ROWS, 128), F32),
            pltpu.VMEM((ROWS, 128), F32), pltpu.VMEM((8, 128), F32),
        ],
        compiler_params=grid_params(),
        cost_estimate=pl.CostEstimate(flops=8 * 10**9, bytes_accessed=14 * MIB, transcendentals=5 * 10**6),
    )(
        proj, proj, proj, proj, halo, halo, halo, taps, taps, taps, hp,
        step, cum, cumt, g, b, c, dy, carried, late, lp,
    )


def swap(value):
    return lax.ppermute(value, "section", [(0, 1), (1, 0)])


def shifted(value, distance, n):
    return lax.ppermute(value, "seq", [(i, i + distance) for i in range(n) if 0 <= i + distance < n])


def plane_route(k, n):
    return [(i, i - i % PLANE + (i + k) % PLANE) for i in range(n)]


def rms(value):
    return lax.rsqrt(jnp.mean(value * value, axis=-1, keepdims=True) + EPS)


def split_small(flat):
    sizes = [D, CONVD * CONV, CONVD, HEADS, HEADS, HEADS, INNER]
    parts, at = [], 0
    for size in sizes:
        parts.append(flat[at : at + size])
        at += size
    return parts


def unpack_params(flat):
    norm_g, conv_w, conv_b, dt_b, a_lg, skip_w, gate_g = split_small(flat)
    taps = jnp.concatenate(
        [conv_w.reshape(CONVD, CONV).T, conv_b[None], jnp.zeros((3, CONVD), F32)], axis=0
    )
    hp = jnp.zeros((8, 128), F32).at[0, :HEADS].set(dt_b).at[1, :HEADS].set(a_lg)
    lp = jnp.concatenate(
        [jnp.repeat(skip_w, HEADDIM)[None], gate_g[None], jnp.zeros((6, INNER), F32)], axis=0
    )
    return norm_g, taps, hp, lp


def forward_layer(h, weights, params, n):
    own_in, other_in, own_out, other_out, flag = weights
    norm_g, taps, hp, lp = params
    normed = (h * rms(h) * norm_g).astype(BF16)
    proj = mm(normed, own_in, other_in, flag, False, 512)
    halo = shifted(proj[ROWS - 8 :, INNER : INNER + CONVD], 1, n)
    values, state, decay, step, cum, cumt, b, c, g = front(proj, halo, taps, hp)
    carried = exchange(state, decay, n, False)
    y, gated_low = mix(g, step, cum, cumt, values, proj, c, carried, lp)
    out = h + mm(gated_low, own_out, other_out, flag, False, 256)
    return out, (h, normed, proj, halo, decay, step, cum, cumt, b, c, g, carried, y, gated_low)


def backward_layer(stored, d_out, weights, params, n):
    own_in, other_in, own_out, other_out, flag = weights
    norm_g, taps, hp, lp = params
    h, normed, proj, halo, decay, step, cum, cumt, b, c, g, carried, y, gated_low = stored
    d_low = d_out.astype(BF16)
    d_gated_low = mm(d_low, own_out, other_out, flag, True, 512)
    dy, d_gate, gate_gain, d_carried = gate_back(d_gated_low, y, proj, cum, c, lp)
    late = exchange(d_carried, decay, n, True)
    dx, dbc, tail, tailbc, head, headbc, gtaps, gtapsbc, d_raw, heads = core_back(
        proj, halo, taps, hp, step, cum, cumt, g, b, c, dy, carried, late, lp
    )
    after = shifted(jnp.concatenate([head, headbc], axis=1), -1, n)
    fix = jnp.concatenate([tail, tailbc], axis=1)
    zero = jnp.zeros((8, CONVD), F32)
    for k in range(CONV - 1):
        fix = fix + zero.at[5 + k :].set(taps[k][None] * after[: 3 - k])
    low = jnp.concatenate([d_gate, dx, dbc, d_raw[:, :HEADS]], axis=1)
    d_proj = low.at[ROWS - 8 :, INNER : INNER + CONVD].set(fix.astype(BF16))
    d_normed = mm(d_proj, own_in, other_in, flag, True, 256)
    r = rms(h)
    v = d_normed * norm_g
    d_h = d_out + r * (v - h * (r * r * jnp.mean(v * h, axis=-1, keepdims=True)))
    norm_gain = jnp.sum(d_normed * h * r, axis=0)
    taps_all = jnp.concatenate([gtaps, gtapsbc], axis=1)
    small = jnp.concatenate(
        [
            norm_gain, taps_all[:CONV].T.reshape(-1), taps_all[CONV],
            heads[0, :HEADS], heads[1, :HEADS], heads[2, :HEADS], gate_gain[0],
        ]
    )
    return d_h, (normed, d_proj, gated_low, d_low), small


def pieces_of(value, count, n):
    spot = lax.axis_index("seq") % PLANE
    width = value.shape[1] // count
    got = [lax.dynamic_slice_in_dim(value, spot * width, width, 1)]
    for k in range(1, PLANE):
        part = lax.dynamic_slice_in_dim(value, (spot + k) % PLANE * width, width, 1)
        got.append(lax.ppermute(part, "seq", plane_route(k, n)))
    return jnp.concatenate(got, axis=0)


def copies_of(value, n):
    got = [value] + [lax.ppermute(value, "seq", plane_route(k, n)) for k in range(1, PLANE)]
    return jnp.concatenate(got, axis=0)


def matrix_grads(factors, n):
    normed, d_proj, gated_low, d_low = factors
    planes = n // PLANE
    columns = [[p + PLANE * z for z in range(planes)] for p in range(PLANE)]
    in_plane = [[PLANE * z + p for p in range(PLANE)] for z in range(planes)]

    def sum_rows(partial):
        return lax.psum_scatter(
            partial.astype(BF16), "seq", scatter_dimension=0, axis_index_groups=columns, tiled=True
        )

    by_owner = gated_low.reshape(ROWS, planes, PLANE, INNER // n).transpose(0, 2, 1, 3).reshape(ROWS, INNER)
    g_out = sum_rows(dot_tn(pieces_of(by_owner, PLANE, n), copies_of(d_low, n)))
    wide = jnp.concatenate([d_proj, jnp.zeros((ROWS, PLANE * QUARTER - PROJ), BF16)], axis=1)
    g_in = sum_rows(dot_tn(copies_of(normed, n), pieces_of(wide, PLANE, n)))
    g_in = lax.all_to_all(g_in, "seq", 0, 1, axis_index_groups=in_plane, tiled=True)
    return g_in[:, :PROJ].astype(F32), g_out.astype(F32)


def per_device(
    inputs, cotangent, norm_gain, in_weight, conv_weight, conv_bias, dt_bias, a_log, d_skip,
    gate_norm_gain, out_weight,
):
    n = lax.axis_size("seq")
    core = lax.axis_index("section")
    place = lax.axis_index("seq")
    first = core == 0
    own_in, own_out = in_weight[0], out_weight[0]
    other_in, other_out = swap(own_in), swap(own_out)
    own_small = jnp.concatenate(
        [
            norm_gain[0], conv_weight[0].reshape(-1), conv_bias[0], dt_bias[0], a_log[0], d_skip[0],
            gate_norm_gain[0],
        ]
    )
    other_small = swap(own_small)
    flags = [(core == layer).astype(jnp.int32)[None] for layer in range(2)]
    weights = [(own_in, other_in, own_out, other_out, flag) for flag in flags]
    params = [
        unpack_params(jnp.where(first, own_small, other_small)),
        unpack_params(jnp.where(first, other_small, own_small)),
    ]

    def mine(pair):
        return lax.dynamic_index_in_dim(pair, core, 0, keepdims=False)

    def settle(early, late):
        return jnp.where(first, early, late), swap(jnp.where(first, late, early))

    def both(early, late):
        own, other = settle(early, late)
        return jnp.stack([jnp.where(first, own, other), jnp.where(first, other, own)])[None]

    out_0, kept_0 = forward_layer(mine(inputs).astype(F32), weights[0], params[0], n)
    act_0 = out_0.astype(BF16)
    out_1, kept_1 = forward_layer(act_0.astype(F32), weights[1], params[1], n)
    acts = both(act_0, out_1.astype(BF16))

    d_1, factors_1, small_1 = backward_layer(kept_1, mine(cotangent).astype(F32), weights[1], params[1], n)
    in_1, outw_1 = matrix_grads(factors_1, n)
    d_0, factors_0, small_0 = backward_layer(kept_0, d_1.astype(BF16).astype(F32), weights[0], params[0], n)
    in_0, outw_0 = matrix_grads(factors_0, n)
    input_grads = both(d_0, d_1)

    def joined(early, late):
        own, other = settle(early, late)
        return own + other

    g_in, g_out, small = joined(in_0, in_1), joined(outw_0, outw_1), joined(small_0, small_1)
    reach = 1
    while reach < n:
        small = small + lax.ppermute(small, "seq", [(i, i ^ reach) for i in range(n)])
        reach *= 2
    norm_g, conv_w, conv_b, dt_b, a_lg, skip_w, gate_g = split_small(small)

    def share(value):
        rows = value.shape[0] // n
        return lax.dynamic_slice_in_dim(value, place * rows, rows, 0)[None]

    return (
        acts, input_grads, share(norm_g), g_in[None], share(conv_w.reshape(CONVD, CONV)), share(conv_b),
        dt_b[None], a_lg[None], skip_w[None], share(gate_g), g_out[None],
    )


def solution(mesh):
    in_specs = (
        P(None, "seq", None), P(None, "seq", None), P("section", None), P("section", None, None),
        P("section", None, None), P("section", None), P("section", None), P("section", None),
        P("section", None), P("section", None), P("section", None, None),
    )
    out_specs = (
        P("section", None, "seq", None), P("section", None, "seq", None), P("section", "seq"),
        P("section", "seq", None), P("section", "seq", None), P("section", "seq"), P("section", None),
        P("section", None), P("section", None), P("section", "seq"), P("section", "seq", None),
    )
    return jax.shard_map(per_device, mesh=mesh, in_specs=in_specs, out_specs=out_specs, check_vma=False)
```

time: 3100 us -> 943 us (0.30)
  waiting for transfers between devices: 1610 us -> 157 us
  matrix products: 570 us -> 30.8 us
  Pallas kernels: 0 us -> 457 us
  other arithmetic: 457 us -> 38.2 us
  blocking collectives: 239 us -> 0 us
  starting transfers between devices: 23.8 us -> 97.9 us
    all_gather x6 -> x0, waiting for transfers between devices: 944 us -> none  [the longest x3 636 us: entering(): pieces = jax.tree.map(lambda part: lax.all_gather(part, axis), value)]
    reduce_scatter x2 -> x4, waiting for transfers between devices: 664 us -> 20.9 us  [sum_rows(): lax.psum_scatter(partial.astype(BF16), 'seq', scatter_dimension=0, axis_i...]
    dot_general x78 -> x4, matrix products: 570 us -> 30.8 us  [dot_tn(): lax.dot_general(a, b, (((0,), (0,)), ((), ())), preferred_element_type=F32)]
    pallas_call x0 -> x20, Pallas kernels: none -> 457 us  [the longest x4 170 us: exchange(): pl.pallas_call(functools.partial(exchange_kernel, n, rev), out_shape=sds(...]
    unnamed x5 -> x0, blocking collectives: 239 us -> none
    select_n x95 -> x6, other arithmetic: 162 us -> 8.17 us  [the longest x5 8.16 us: settle(): return (jnp.where(first, early, late), swap(jnp.where(first, late, early)))]
    ppermute x10 -> x40, waiting for transfers between devices: 5.35 us -> 135 us  [the longest x12 91.2 us: copies_of(): lax.ppermute(value, 'seq', plane_route(k, n))]
    reduce_sum x34 -> x4, other arithmetic: 88.9 us -> 2.24 us  [the longest x2 1.69 us: backward_layer(): norm_gain = jnp.sum(d_normed * h * r, axis=0)]
  transfers between devices with their start and end apart: 19 -> 46, of which waited for: 11 -> 16; matrix products, arithmetic and copies ran while one was open for 13% -> 19% of each run, Pallas kernels for 0% -> 46%
where the time goes in v1:
time: 943 us; the launch traced here: 931 us
  Pallas kernels  457 us (48%)
  waiting for transfers between devices  157 us (17%)
  local copies, waits for them, and re-layouts  134 us (14%)
  starting transfers between devices  97.9 us (10%)
  other arithmetic  38.2 us (4%)
  matrix products  30.8 us (3%)
  between operations  15.7 us (2%)
    pallas_call x4, Pallas kernels, exchange(): pl.pallas_call(functools.partial(exchange_kernel, n, rev), out_shape=sds(...  170 us
    ppermute x12, waiting for transfers between devices, copies_of(): lax.ppermute(value, 'seq', plane_route(k, n))  91.2 us
    pallas_call x8, Pallas kernels, mm(): pl.pallas_call(functools.partial(mm_kernel, nt=nt), grid_spec=pltpu.Prefe...  89 us
    pallas_call x2, Pallas kernels, core_back(): pl.pallas_call(core_back_kernel, grid=(PAIRS,), in_specs=[lanes(ROWS, 24)...  75.5 us
    pallas_call x2, Pallas kernels, mix(): pl.pallas_call(mix_kernel, grid=(PAIRS,), in_specs=[whole((ROWS, ROWS)),...  47.9 us
    ppermute x12, starting transfers between devices, copies_of(): lax.ppermute(value, 'seq', plane_route(k, n))  46.6 us
    unnamed x186, local copies, waits for them, and re-layouts  43.6 us
    pallas_call x2, Pallas kernels, front(): pl.pallas_call(front_kernel, grid=(PAIRS,), in_specs=[lanes(ROWS, 24), fi...  38.7 us
  transfers between devices with their start and end apart: 46, of which 16 were waited for; matrix products, arithmetic and copies ran while one was open for 19% of the time, Pallas kernels for 46%

profile of v1, /device:TPU:0, one launch (start us, length us, event | category | flops | bytes accessed | tf_op | source)
XLA Modules:
  0.0 930.7 jit_solution(1138848390826949168)
XLA Ops:
  15.3 24.9 %copy.51 = bf16[1,1536,6448]{2,1,0:T(8,128)(2,1)} copy(bf16[1,1536,6448]{1,2,0:T(8,128)(2,1)} %param.38) | data formatting | bytes 39616512 | tf_op args[3]
  52.7 24.3 %copy.53.other_ref = bf16[1536,6448]{1,0:T(8,128)(2,1)} copy(bf16[1536,6448]{0,1:T(8,128)(2,1)} %collective-permute-done.1) | data formatting | bytes 39616512 | tf_op jit(solution)/shard_map/ppermute | solution.py:633
  77.0 16.9 %shard_map.194.x_ref.b_ref.c_ref.raw_ref.gate_ref = f32[256,6448]{1,0:T(8,128)} custom-call(s32[1]{0:T(128)} %bitcast.1.flag_ref, bf16[256,1536]{1,0:T(8,128)(2,1)} %fusion.56.x_ref, bf16[1536,6448]{1,0:T(8,128)(2,1)} %bitcast.107, bf16[1536,6448]{1,0:T(8,128)(2,1)} %copy.53.other_ref), custom_call_target="tpu_custom_call" | custom-call | flops 5070913536 | bytes 19808256 | tf_op jit(solution)/shard_map/pallas_call | solution.py:150
  102.0 19.4 %shard_map.195 = (f32[256,3072]{1,0:T(8,128)S(1)}, f32[128,3072]{1,0:T(8,128)S(1)}, f32[8,3072]{1,0:T(8,128)S(1)}, f32[256,128]{1,0:T(8,128)S(1)}, f32[256,128]{...) custom-call(f32[256,6448]{1,0:T(8,128)} %shard_map.194.x_ref.b_ref.c, ...), custom_call_target="tpu_custom_call" | custom-call | flops 2000000000 | bytes 10485760 | tf_op jit(solution)/shard_map/pallas_call | solution.py:225
  123.1 42.3 %shard_map.196.car_ref = f32[128,3072]{1,0:T(8,128)S(1)} custom-call(f32[128,3072]{1,0:T(8,128)S(1)} %get-tuple-element.211.s_ref, f32[8,3072]{1,0:T(8,128)S(1)} %get-tuple-element.212.d_ref), custom_call_target="tpu_custom_call" | custom-call | tf_op jit(solution)/shard_map/pallas_call | solution.py:364
  165.4 24.1 %shard_map.197 = (f32[256,3072]{1,0:T(8,128)}, bf16[256,3072]{1,0:T(8,128)(2,1)S(1)}) custom-call(f32[256,256]{1,0:T(8,128)S(1)} %get-tuple-element.205.g_ref, f32[256,128]{1,0:T(8,128)S(1)} %get-tuple-element.206.step_ref, f32[256,128]{1,0:T(8,128)S(1)} %get-tuple-element.207.cum_ref, f32[128,256]{1,0:T(8,128)S(1)} %get-tuple-element.208.cumt_ref, ...), custom_call_target="tpu_custom_call" | custom-call | flops 3000000000 | bytes 14680064 | tf_op jit(solution)/shard_map/pallas_call | solution.py:429
  199.1 16.8 %shard_map.199.x_ref.b_ref.c_ref.raw_ref.gate_ref = f32[256,6448]{1,0:T(8,128)} custom-call(s32[1]{0:T(128)} %bitcast.14.flag_ref, bf16[256,1536]{1,0:T(8,128)(2,1)} %fusion.46.x_ref, bf16[1536,6448]{1,0:T(8,128)(2,1)} %bitcast.108, bf16[1536,6448]{1,0:T(8,128)(2,1)} %copy.53.other_ref), custom_call_target="tpu_custom_call" | custom-call | flops 5070913536 | bytes 19808256 | tf_op jit(solution)/shard_map/pallas_call | solution.py:150
  230.3 19.4 %shard_map.200 = (f32[256,3072]{1,0:T(8,128)S(1)}, f32[128,3072]{1,0:T(8,128)S(1)}, f32[8,3072]{1,0:T(8,128)S(1)}, f32[256,128]{1,0:T(8,128)S(1)}, f32[256,128]{...) custom-call(f32[256,6448]{1,0:T(8,128)} %shard_map.199.x_ref.b_ref.c, ...), custom_call_target="tpu_custom_call" | custom-call | flops 2000000000 | bytes 10485760 | tf_op jit(solution)/shard_map/pallas_call | solution.py:225
  251.3 45.0 %shard_map.201.car_ref = f32[128,3072]{1,0:T(8,128)S(1)} custom-call(f32[128,3072]{1,0:T(8,128)S(1)} %get-tuple-element.220.s_ref, f32[8,3072]{1,0:T(8,128)S(1)} %get-tuple-element.221.d_ref), custom_call_target="tpu_custom_call" | custom-call | tf_op jit(solution)/shard_map/pallas_call | solution.py:364
  296.4 23.8 %shard_map.202 = (f32[256,3072]{1,0:T(8,128)}, bf16[256,3072]{1,0:T(8,128)(2,1)S(1)}) custom-call(f32[256,256]{1,0:T(8,128)S(1)} %get-tuple-element.214.g_ref, f32[256,128]{1,0:T(8,128)S(1)} %get-tuple-element.215.step_ref, f32[256,128]{1,0:T(8,128)S(1)} %get-tuple-element.216.cum_ref, f32[128,256]{1,0:T(8,128)S(1)} %get-tuple-element.217.cumt_ref, ...), custom_call_target="tpu_custom_call" | custom-call | flops 3000000000 | bytes 14680064 | tf_op jit(solution)/shard_map/pallas_call | solution.py:429
  321.3 17.6 %shard_map.205 = (f32[256,3072]{1,0:T(8,128)S(1)}, bf16[256,3072]{1,0:T(8,128)(2,1)S(1)}, f32[8,3072]{1,0:T(8,128)S(1)}, bf16[128,3072]{1,0:T(8,128)(2,1)S(1)}) custom-call(f32[256,3072]{1,0:T(8,128)} %copy-done.4, f32[256,3072]{1,0:T(8,128)} %get-tuple-element.223.y_ref, f32[256,6448]{1,0:T(8,128)} %shard_map.199.x_ref.b_ref.c_ref.raw_ref.gate_ref, ...), custom_call_target="tpu_custom_call" | custom-call | flops 1000000000 | bytes 16777216 | tf_op jit(solution)/shard_map/pallas_call | solution.py:481
  340.6 43.5 %shard_map.206.late_ref = bf16[128,3072]{1,0:T(8,128)(2,1)S(1)} custom-call(bf16[128,3072]{1,0:T(8,128)(2,1)S(1)} %get-tuple-element.227.s_ref, f32[8,3072]{1,0:T(8,128)S(1)} %get-tuple-element.221.d_ref), custom_call_target="tpu_custom_call" | custom-call | tf_op jit(solution)/shard_map/pallas_call | solution.py:364
  384.1 37.9 %shard_map.207 = (bf16[256,3072]{1,0:T(8,128)(2,1)S(1)}, bf16[256,256]{1,0:T(8,128)(2,1)S(1)}, f32[8,3072]{1,0:T(8,128)S(1)}, f32[8,256]{1,0:T(8,128)S(1)}, f32[...) custom-call(f32[256,6448]{1,0:T(8,128)} %shard_map.199.x_ref.b_ref.c, ...), custom_call_target="tpu_custom_call" | custom-call | flops 8000000000 | bytes 14680064 | tf_op jit(solution)/shard_map/pallas_call | solution.py:598
  445.2 39.1 %collective-permute-done.21 = bf16[256,1536]{1,0:T(8,128)(2,1)S(1)} collective-permute-done((bf16[256,1536]{1,0:T(8,128)(2,1)}, bf16[256,1536]{1,0:T(8,128)(2,1)S(1)}, u32[]{:S(2)}, u32[]{:S(2)}) %collective-permute-start.21) | collective-permute-done | bytes 786464 | tf_op jit(solution)/shard_map/ppermute | solution.py:726
  484.3 18.1 %collective-permute-start.14 = (bf16[256,1536]{1,0:T(8,128)(2,1)}, bf16[256,1536]{1,0:T(8,128)(2,1)}, u32[]{:S(2)}, u32[]{:S(2)}) collective-permute-start(bf16[256,1536]{1,0:T(8,128)(2,1)} %fusion.56.x_ref), channel_id=1, source_target_pairs={{0,1},{1,2},{2,3},{3,0},{4,5},{5,6},{6,7},{7,4},{8,9},{9,10},{10,1... | collective-permute-start | bytes 2359304 | tf_op jit(solution)/shard_map/ppermute | solution.py:726
  512.1 12.4 %shard_map.208 = f32[256,1536]{1,0:T(8,128)S(1)} custom-call(s32[1]{0:T(128)} %bitcast.14.flag_ref, bf16[256,6448]{1,0:T(8,128)(2,1)S(1)} %convert_dynamic-update-slice_fusion.1.x_ref, bf16[1536,6448]{1,0:T(8,128)(2,1)} %bitcast.109, bf16[1536,6448]{1,0:T(8,128)(2,1)} %copy.53.other_ref), custom_call_target="tpu_custom_call" | custom-call | flops 5070913536 | bytes 19808256 | tf_op jit(solution)/shard_map/pallas_call | solution.py:150
  537.3 17.7 %shard_map.210 = (f32[256,3072]{1,0:T(8,128)S(1)}, bf16[256,3072]{1,0:T(8,128)(2,1)S(1)}, f32[8,3072]{1,0:T(8,128)S(1)}, bf16[128,3072]{1,0:T(8,128)(2,1)S(1)}) custom-call(f32[256,3072]{1,0:T(8,128)} %copy-done.5, f32[256,3072]{1,0:T(8,128)} %get-tuple-element.235.y_ref, f32[256,6448]{1,0:T(8,128)} %shard_map.194.x_ref.b_ref.c_ref.raw_ref.gate_ref, ...), custom_call_target="tpu_custom_call" | custom-call | flops 1000000000 | bytes 16777216 | tf_op jit(solution)/shard_map/pallas_call | solution.py:481
  556.7 39.6 %shard_map.211.late_ref = bf16[128,3072]{1,0:T(8,128)(2,1)S(1)} custom-call(bf16[128,3072]{1,0:T(8,128)(2,1)S(1)} %get-tuple-element.239.s_ref, f32[8,3072]{1,0:T(8,128)S(1)} %copy-done.30), custom_call_target="tpu_custom_call" | custom-call | tf_op jit(solution)/shard_map/pallas_call | solution.py:364
  596.4 37.5 %shard_map.212 = (bf16[256,3072]{1,0:T(8,128)(2,1)S(1)}, bf16[256,256]{1,0:T(8,128)(2,1)S(1)}, f32[8,3072]{1,0:T(8,128)S(1)}, f32[8,256]{1,0:T(8,128)S(1)}, f32[...) custom-call(f32[256,6448]{1,0:T(8,128)} %shard_map.194.x_ref.b_ref.c, ...), custom_call_target="tpu_custom_call" | custom-call | flops 8000000000 | bytes 14680064 | tf_op jit(solution)/shard_map/pallas_call | solution.py:598
  657.2 32.8 %collective-permute-done.15 = bf16[256,1536]{1,0:T(8,128)(2,1)S(1)} collective-permute-done((bf16[256,1536]{1,0:T(8,128)(2,1)}, bf16[256,1536]{1,0:T(8,128)(2,1)S(1)}, u32[]{:S(2)}, u32[]{:S(2)}) %collective-permute-start.15) | collective-permute-done | bytes 786464 | tf_op jit(solution)/shard_map/ppermute | solution.py:726
  700.2 18.6 %collective-permute-start.36 = (bf16[256,1536]{1,0:T(8,128)(2,1)}, bf16[256,1536]{1,0:T(8,128)(2,1)}, u32[]{:S(2)}, u32[]{:S(2)}) collective-permute-start(bf16[256,1536]{1,0:T(8,128)(2,1)} %copy-done.9), channel_id=1, source_target_pairs={{0,1},{1,2},{2,3},{3,0},{4,5},{5,6},{6,7},{7,4},{8,9},{9,10},{10,1... | collective-permute-start | bytes 2359304 | tf_op jit(solution)/shard_map/ppermute | solution.py:726
  740.5 11.2 %collective-permute-done.37 = bf16[256,1536]{1,0:T(8,128)(2,1)} collective-permute-done((bf16[256,1536]{1,0:T(8,128)(2,1)}, bf16[256,1536]{1,0:T(8,128)(2,1)}, u32[]{:S(2)}, u32[]{:S(2)}) %collective-permute-start.37) | collective-permute-done | bytes 786464 | tf_op jit(solution)/shard_map/ppermute | solution.py:726
  802.3 11.8 %shard_map.213 = f32[256,1536]{1,0:T(8,128)S(1)} custom-call(s32[1]{0:T(128)} %bitcast.1.flag_ref, bf16[256,6448]{1,0:T(8,128)(2,1)S(1)} %convert_dynamic-update-slice_fusion.x_ref, bf16[1536,6448]{1,0:T(8,128)(2,1)} %bitcast.110, bf16[1536,6448]{1,0:T(8,128)(2,1)} %copy.53.other_ref), custom_call_target="tpu_custom_call" | custom-call | flops 5070913536 | bytes 19808256 | tf_op jit(solution)/shard_map/pallas_call | solution.py:150
  889.0 20.9 %reduce-scatter.9.cloned.1.call-done = bf16[192,1536]{1,0:T(8,128)(2,1)} async-done(((bf16[768,1536]{1,0:T(8,128)(2,1)}), bf16[192,1536]{1,0:T(8,128)(2,1)}) %reduce-scatter.9.cloned.1.call-update) | async-done | bytes 589840 | tf_op jit(solution)/shard_map/reduce_scatter | solution.py:737
  (404 shorter events, 299.4 us)
Async XLA Ops:
  7.3 827.6 %reduce-scatter.7.cloned.1.call-start = ((), (), s32[]{:S(2)}) async-start(), calls=%async_computation.7 | async-start | bytes 6389760 | tf_op jit(solution)/shard_map/reduce_scatter | solution.py:737
  7.3 45.4 %collective-permute-start.1 = (bf16[1536,6448]{0,1:T(8,128)(2,1)}, bf16[1536,6448]{0,1:T(8,128)(2,1)}, u32[]{:S(2)}, u32[]{:S(2)}) collective-permute-start(bf16[1536,6448]{0,1:T(8,128)(2,1)} %bitcast.116), channel_id=1, source_target_pairs={{0,16},{16,0},{1,17},{17,1},{2,18},{18,2},{3,19},{19,3},{4,20},{20... | collective-permute-start | bytes 59424776 | tf_op jit(solution)/shard_map/ppermute | solution.py:633
  7.8 181.8 %collective-permute-start.3 = (bf16[3072,1536]{1,0:T(8,128)(2,1)}, bf16[3072,1536]{1,0:T(8,128)(2,1)}, u32[]{:S(2)}, u32[]{:S(2)}) collective-permute-start(bf16[3072,1536]{1,0:T(8,128)(2,1)} %bitcast.111), channel_id=1, source_target_pairs={{0,16},{16,0},{1,17},{17,1},{2,18},{18,2},{3,19},{19,3},{4,20},{20... | collective-permute-start | bytes 28311560 | tf_op jit(solution)/shard_map/ppermute | solution.py:633
  230.0 212.9 %collective-permute-start.20 = (bf16[256,1536]{1,0:T(8,128)(2,1)}, bf16[256,1536]{1,0:T(8,128)(2,1)}, u32[]{:S(2)}, u32[]{:S(2)}) collective-permute-start(bf16[256,1536]{1,0:T(8,128)(2,1)} %fusion.46.x_ref), channel_id=1, source_target_pairs={{0,1},{1,2},{2,3},{3,0},{4,5},{5,6},{6,7},{7,4},{8,9},{9,10},{10,1... | collective-permute-start | bytes 2359304 | tf_op jit(solution)/shard_map/ppermute | solution.py:726
  437.9 64.5 %collective-permute-start.23 = (bf16[256,1664]{1,0:T(8,128)(2,1)S(1)}, bf16[256,1664]{1,0:T(8,128)(2,1)S(1)}, u32[]{:S(2)}, u32[]{:S(2)}) collective-permute-start(bf16[256,1664]{1,0:T(8,128)(2,1)S(1)} %get-tuple-element.278), channel_id=1, source_target_pairs={{0,1},{1,2},{2,3},{3,0},{4,5},{5,6},{6,7},{7,4},{8,9},{9,10},{10,1... | collective-permute-start | bytes 2555912 | tf_op jit(solution)/shard_map/ppermute | solution.py:721
  439.0 63.4 %collective-permute-start.24 = (bf16[256,1664]{1,0:T(8,128)(2,1)S(1)}, bf16[256,1664]{1,0:T(8,128)(2,1)S(1)}, u32[]{:S(2)}, u32[]{:S(2)}) collective-permute-start(bf16[256,1664]{1,0:T(8,128)(2,1)S(1)} %get-tuple-element.279), channel_id=1, source_target_pairs={{0,2},{1,3},{2,0},{3,1},{4,6},{5,7},{6,4},{7,5},{8,10},{9,11},{10,... | collective-permute-start | bytes 2555912 | tf_op jit(solution)/shard_map/ppermute | solution.py:721
  441.0 61.4 %collective-permute-start.25 = (bf16[256,1664]{1,0:T(8,128)(2,1)S(1)}, bf16[256,1664]{1,0:T(8,128)(2,1)S(1)}, u32[]{:S(2)}, u32[]{:S(2)}) collective-permute-start(bf16[256,1664]{1,0:T(8,128)(2,1)S(1)} %get-tuple-element.280), channel_id=1, source_target_pairs={{0,3},{1,0},{2,1},{3,2},{4,7},{5,4},{6,5},{7,6},{8,11},{9,8},{10,9... | collective-permute-start | bytes 2555912 | tf_op jit(solution)/shard_map/ppermute | solution.py:721
  442.3 42.0 %collective-permute-start.21 = (bf16[256,1536]{1,0:T(8,128)(2,1)}, bf16[256,1536]{1,0:T(8,128)(2,1)S(1)}, u32[]{:S(2)}, u32[]{:S(2)}) collective-permute-start(bf16[256,1536]{1,0:T(8,128)(2,1)} %fusion.46.x_ref), channel_id=1, source_target_pairs={{0,2},{1,3},{2,0},{3,1},{4,6},{5,7},{6,4},{7,5},{8,10},{9,11},{10,... | collective-permute-start | bytes 2359304 | tf_op jit(solution)/shard_map/ppermute | solution.py:726
  442.9 59.5 %collective-permute-start.22 = (bf16[256,1536]{1,0:T(8,128)(2,1)}, bf16[256,1536]{1,0:T(8,128)(2,1)S(1)}, u32[]{:S(2)}, u32[]{:S(2)}) collective-permute-start(bf16[256,1536]{1,0:T(8,128)(2,1)} %fusion.46.x_ref), channel_id=1, source_target_pairs={{0,3},{1,0},{2,1},{3,2},{4,7},{5,4},{6,5},{7,6},{8,11},{9,8},{10,9... | collective-permute-start | bytes 2359304 | tf_op jit(solution)/shard_map/ppermute | solution.py:726
  484.3 171.6 %collective-permute-start.14 = (bf16[256,1536]{1,0:T(8,128)(2,1)}, bf16[256,1536]{1,0:T(8,128)(2,1)}, u32[]{:S(2)}, u32[]{:S(2)}) collective-permute-start(bf16[256,1536]{1,0:T(8,128)(2,1)} %fusion.56.x_ref), channel_id=1, source_target_pairs={{0,1},{1,2},{2,3},{3,0},{4,5},{5,6},{6,7},{7,4},{8,9},{9,10},{10,1... | collective-permute-start | bytes 2359304 | tf_op jit(solution)/shard_map/ppermute | solution.py:726
  512.0 351.9 %reduce-scatter.5.cloned.1.call-start = ((), (), s32[]{:S(2)}) async-start(), calls=%async_computation.6 | async-start | bytes 6389760 | tf_op jit(solution)/shard_map/reduce_scatter | solution.py:737
  650.9 39.4 %collective-permute-start.17 = (bf16[256,1664]{1,0:T(8,128)(2,1)S(1)}, bf16[256,1664]{1,0:T(8,128)(2,1)S(1)}, u32[]{:S(2)}, u32[]{:S(2)}) collective-permute-start(bf16[256,1664]{1,0:T(8,128)(2,1)S(1)} %get-tuple-element.274), channel_id=1, source_target_pairs={{0,1},{1,2},{2,3},{3,0},{4,5},{5,6},{6,7},{7,4},{8,9},{9,10},{10,1... | collective-permute-start | bytes 2555912 | tf_op jit(solution)/shard_map/ppermute | solution.py:721
  652.8 37.5 %collective-permute-start.18 = (bf16[256,1664]{1,0:T(8,128)(2,1)S(1)}, bf16[256,1664]{1,0:T(8,128)(2,1)S(1)}, u32[]{:S(2)}, u32[]{:S(2)}) collective-permute-start(bf16[256,1664]{1,0:T(8,128)(2,1)S(1)} %get-tuple-element.275), channel_id=1, source_target_pairs={{0,2},{1,3},{2,0},{3,1},{4,6},{5,7},{6,4},{7,5},{8,10},{9,11},{10,... | collective-permute-start | bytes 2555912 | tf_op jit(solution)/shard_map/ppermute | solution.py:721
  653.7 36.6 %collective-permute-start.19 = (bf16[256,1664]{1,0:T(8,128)(2,1)S(1)}, bf16[256,1664]{1,0:T(8,128)(2,1)S(1)}, u32[]{:S(2)}, u32[]{:S(2)}) collective-permute-start(bf16[256,1664]{1,0:T(8,128)(2,1)S(1)} %get-tuple-element.276), channel_id=1, source_target_pairs={{0,3},{1,0},{2,1},{3,2},{4,7},{5,4},{6,5},{7,6},{8,11},{9,8},{10,9... | collective-permute-start | bytes 2555912 | tf_op jit(solution)/shard_map/ppermute | solution.py:721
  700.1 188.9 %reduce-scatter.11.cloned.1.call-start = ((), (), s32[]{:S(2)}) async-start(), calls=%async_computation.9 | async-start | bytes 2949120 | tf_op jit(solution)/shard_map/reduce_scatter | solution.py:737
  700.2 38.4 %collective-permute-start.36 = (bf16[256,1536]{1,0:T(8,128)(2,1)}, bf16[256,1536]{1,0:T(8,128)(2,1)}, u32[]{:S(2)}, u32[]{:S(2)}) collective-permute-start(bf16[256,1536]{1,0:T(8,128)(2,1)} %copy-done.9), channel_id=1, source_target_pairs={{0,1},{1,2},{2,3},{3,0},{4,5},{5,6},{6,7},{7,4},{8,9},{9,10},{10,1... | collective-permute-start | bytes 2359304 | tf_op jit(solution)/shard_map/ppermute | solution.py:726
  732.2 40.4 %collective-permute-start.34 = (bf16[256,768]{0,1:T(8,128)(2,1)S(1)}, bf16[256,768]{0,1:T(8,128)(2,1)S(1)}, u32[]{:S(2)}, u32[]{:S(2)}) collective-permute-start(bf16[256,768]{0,1:T(8,128)(2,1)S(1)} %get-tuple-element.289), channel_id=1, source_target_pairs={{0,2},{1,3},{2,0},{3,1},{4,6},{5,7},{6,4},{7,5},{8,10},{9,11},{10,... | collective-permute-start | bytes 1179656 | tf_op jit(solution)/shard_map/ppermute | solution.py:721
  751.7 64.3 %collective-permute-start.27 = (bf16[256,768]{0,1:T(8,128)(2,1)}, bf16[256,768]{0,1:T(8,128)(2,1)}, u32[]{:S(2)}, u32[]{:S(2)}) collective-permute-start(bf16[256,768]{0,1:T(8,128)(2,1)} %get-tuple-element.286), channel_id=1, source_target_pairs={{0,1},{1,2},{2,3},{3,0},{4,5},{5,6},{6,7},{7,4},{8,9},{9,10},{10,1... | collective-permute-start | bytes 1179656 | tf_op jit(solution)/shard_map/ppermute | solution.py:721
  754.4 61.9 %collective-permute-start.28 = (bf16[256,768]{0,1:T(8,128)(2,1)}, bf16[256,768]{0,1:T(8,128)(2,1)}, u32[]{:S(2)}, u32[]{:S(2)}) collective-permute-start(bf16[256,768]{0,1:T(8,128)(2,1)} %get-tuple-element.285), channel_id=1, source_target_pairs={{0,2},{1,3},{2,0},{3,1},{4,6},{5,7},{6,4},{7,5},{8,10},{9,11},{10,... | collective-permute-start | bytes 1179656 | tf_op jit(solution)/shard_map/ppermute | solution.py:721
  778.3 131.7 %reduce-scatter.9.cloned.1.call-start = ((), (), s32[]{:S(2)}) async-start(), calls=%async_computation.8 | async-start | bytes 2949120 | tf_op jit(solution)/shard_map/reduce_scatter | solution.py:737
  790.1 36.3 %collective-permute-start.30 = (bf16[256,1536]{1,0:T(8,128)(2,1)}, bf16[256,1536]{1,0:T(8,128)(2,1)}, u32[]{:S(2)}, u32[]{:S(2)}) collective-permute-start(bf16[256,1536]{1,0:T(8,128)(2,1)} %copy-done.11), channel_id=1, source_target_pairs={{0,1},{1,2},{2,3},{3,0},{4,5},{5,6},{6,7},{7,4},{8,9},{9,10},{10,1... | collective-permute-start | bytes 2359304 | tf_op jit(solution)/shard_map/ppermute | solution.py:726
  790.1 36.3 %collective-permute-start.31 = (bf16[256,1536]{1,0:T(8,128)(2,1)}, bf16[256,1536]{1,0:T(8,128)(2,1)}, u32[]{:S(2)}, u32[]{:S(2)}) collective-permute-start(bf16[256,1536]{1,0:T(8,128)(2,1)} %copy-done.11), channel_id=1, source_target_pairs={{0,2},{1,3},{2,0},{3,1},{4,6},{5,7},{6,4},{7,5},{8,10},{9,11},{10,... | collective-permute-start | bytes 2359304 | tf_op jit(solution)/shard_map/ppermute | solution.py:726
  850.0 36.5 %collective-permute-start.5 = (bf16[256,1536]{1,0:T(8,128)(2,1)}, bf16[256,1536]{1,0:T(8,128)(2,1)}, u32[]{:S(2)}, u32[]{:S(2)}) collective-permute-start(bf16[256,1536]{1,0:T(8,128)(2,1)} %broadcast_select_fusion), channel_id=1, source_target_pairs={{0,16},{16,0},{1,17},{17,1},{2,18},{18,2},{3,19},{19,3},{4,20},{20... | collective-permute-start | bytes 2359304 | tf_op jit(solution)/shard_map/ppermute | solution.py:633
  872.4 41.8 %collective-permute-start.8 = (f32[256,1536]{1,0:T(8,128)}, f32[256,1536]{1,0:T(8,128)}, u32[]{:S(2)}, u32[]{:S(2)}) collective-permute-start(f32[256,1536]{1,0:T(8,128)} %fusion.80), channel_id=1, source_target_pairs={{0,16},{16,0},{1,17},{17,1},{2,18},{18,2},{3,19},{19,3},{4,20},{20... | collective-permute-start | bytes 4718600 | tf_op jit(solution)/shard_map/ppermute | solution.py:633
  (112 other events, 2556.6 us)
Sparse Core Ops, SparseCore 0:
  512.1 92.6 reduce-scatter.6
  700.2 106.8 reduce-scatter.4
  810.0 50.2 reduce-scatter.10
  862.4 47.5 reduce-scatter.8

commit v2 on v1

v2 whole, which is shorter than its diff:
```python
import functools

import jax
import jax.numpy as jnp
from jax import lax
from jax.experimental import pallas as pl
from jax.experimental.pallas import tpu as pltpu
from jax.sharding import PartitionSpec as P

D = 1536
INNER = 3072
STATE = 128
HEADS = 48
HEADDIM = 64
CONV = 4
CONVD = 3328
PROJ = 6448
ROWS = 256
WIDE = 256
STEPS = INNER // WIDE
HALF = ROWS // 2
PLANE = 4
LANES = INNER // PLANE
REST = 3584
EPS = 1e-05
MIB = 2**20
MESH = pl.DeviceIdType.MESH
F32 = jnp.float32
BF16 = jnp.bfloat16


def dot_nn(a, b):
    return lax.dot_general(a, b, (((1,), (0,)), ((), ())), preferred_element_type=F32)


def dot_tn(a, b):
    return lax.dot_general(a, b, (((0,), (0,)), ((), ())), preferred_element_type=F32)


def dot_nt(a, b):
    return lax.dot_general(a, b, (((1,), (1,)), ((), ())), preferred_element_type=F32)


def split3(v):
    high = v.astype(BF16)
    rest = v - high.astype(F32)
    mid = rest.astype(BF16)
    return high, mid, (rest - mid.astype(F32)).astype(BF16)


def split2(v):
    high = v.astype(BF16)
    return high, (v - high.astype(F32)).astype(BF16)


def fine(dot, a, b):
    return dot(a[0], b[0]) + (dot(a[0], b[1]) + dot(a[1], b[0]))


def halves(ref):
    return ref[:, 0:128], ref[:, 128:256]


def parts3(v):
    return jnp.concatenate(split3(v), axis=1)


def exact_left(ones, v):
    a, b, c = split3(v)
    return dot_nn(ones, a) + (dot_nn(ones, b) + dot_nn(ones, c))


def iota(shape, dim):
    return lax.broadcasted_iota(jnp.int32, shape, dim)


def expander(step):
    head_of = (WIDE // HEADDIM) * step + lax.shift_right_logical(iota((128, WIDE), 1), 6)
    ones = (iota((128, WIDE), 0) == head_of).astype(F32).astype(BF16)
    return jnp.concatenate([ones, ones, ones], axis=0)


def collector(step):
    head_of = (WIDE // HEADDIM) * step + lax.shift_right_logical(iota((WIDE, 128), 0), 6)
    return (iota((WIDE, 128), 1) == head_of).astype(F32).astype(BF16)


def collect(v, ones):
    a, b, c = split3(v)
    return dot_nn(a, ones) + (dot_nn(b, ones) + dot_nn(c, ones))


def triangle(lower):
    rows, cols = iota((ROWS, ROWS), 0), iota((ROWS, ROWS), 1)
    return ((rows >= cols) if lower else (rows <= cols)).astype(F32).astype(BF16)


def sigmoid(v):
    return 0.5 * jnp.tanh(0.5 * v) + 0.5


def extended(block, halo):
    return jnp.concatenate([halo, block], axis=0)


def conv_pre(ext, taps):
    out = taps[4:5] + taps[0:1] * ext[5 : 5 + ROWS]
    for k in range(1, CONV):
        out = out + taps[k : k + 1] * ext[5 + k : 5 + k + ROWS]
    return out


def conv_back(d_pre, taps):
    ext = jnp.concatenate([d_pre, jnp.zeros((8, d_pre.shape[1]), F32)], axis=0)
    out = taps[3:4] * d_pre
    for k in range(CONV - 1):
        out = out + taps[k : k + 1] * ext[3 - k : 3 - k + ROWS]
    return out


def tap_grads(d_pre, ext):
    rows = [jnp.sum(d_pre * ext[5 + k : 5 + k + ROWS], axis=0, keepdims=True) for k in range(CONV)]
    rows.append(jnp.sum(d_pre, axis=0, keepdims=True))
    rows.append(jnp.zeros((3, d_pre.shape[1]), F32))
    return jnp.concatenate(rows, axis=0)


def step_parts(raw_ref, hp_ref):
    real = iota((ROWS, 128), 1) < HEADS
    raw = jnp.where(real, raw_ref[...], 0.0) + hp_ref[0:1, :]
    step = jnp.maximum(raw, 0.0) + jnp.log1p(jnp.exp(-jnp.abs(raw)))
    step = jnp.where(real, step, 0.0)
    rate = jnp.where(real[0:1], -jnp.exp(hp_ref[1:2, :]), 0.0)
    return raw, step, rate


def mm_kernel(flag_ref, x_ref, own_ref, other_ref, o_ref, *, nt):
    dot = dot_nt if nt else dot_nn

    @pl.when(flag_ref[0] == 1)
    def _():
        o_ref[...] = dot(x_ref[...], own_ref[...])

    @pl.when(flag_ref[0] == 0)
    def _():
        o_ref[...] = dot(x_ref[...], other_ref[...])


def mm(x, own, other, flag, nt, tile):
    rows, depth = x.shape
    width = own.shape[0] if nt else own.shape[1]
    block = (tile, depth) if nt else (depth, tile)

    def place(j, keep):
        return (j * keep, 0) if nt else (0, j * keep)

    return pl.pallas_call(
        functools.partial(mm_kernel, nt=nt),
        grid_spec=pltpu.PrefetchScalarGridSpec(
            num_scalar_prefetch=1,
            grid=(pl.cdiv(width, tile),),
            in_specs=[
                pl.BlockSpec((rows, depth), lambda j, f: (0, 0)),
                pl.BlockSpec(block, lambda j, f: place(j, f[0])),
                pl.BlockSpec(block, lambda j, f: place(j, 1 - f[0])),
            ],
            out_specs=pl.BlockSpec((rows, tile), lambda j, f: (0, j)),
        ),
        out_shape=jax.ShapeDtypeStruct((rows, width), F32),
        compiler_params=pltpu.CompilerParams(vmem_limit_bytes=48 * MIB),
        cost_estimate=pl.CostEstimate(
            flops=2 * rows * depth * width, bytes_accessed=2 * depth * width, transcendentals=0
        ),
    )(flag, x, own, other)


def front_kernel(
    x_ref, bc_ref, raw_ref, xh_ref, bch_ref, xw_ref, bcw_ref, hp_ref,
    val_ref, state_ref, dec_ref, step_ref, cum_ref, cumt_ref, b_ref, c_ref, ct_ref, g_ref, gt_ref, bt_ref,
):
    j = pl.program_id(0)

    @pl.when(j == 0)
    def _():
        _, step, rate = step_parts(raw_ref, hp_ref)
        step_ref[...] = parts3(step)
        cum = exact_left(triangle(True), rate * step)
        cum_ref[...] = parts3(cum)
        cumt_ref[...] = cum.T
        pre = conv_pre(extended(bc_ref[...], bch_ref[...]), bcw_ref[...])
        both = pre * sigmoid(pre)
        b, c = both[:, 0:128], both[:, 128:256]
        b_low, c_low = split2(b), split2(c)
        b_ref[...] = jnp.concatenate(b_low, axis=1)
        c_ref[...] = jnp.concatenate([c_low[0], c_low[1], c_low[0]], axis=1)
        ct_ref[...] = c.T.astype(BF16)
        bt_ref[...] = jnp.concatenate(split2(b.T), axis=0)
        seen = iota((ROWS, ROWS), 0) >= iota((ROWS, ROWS), 1)
        g = jnp.where(seen, fine(dot_nt, c_low, b_low), 0.0)
        g_ref[...] = g
        gt_ref[...] = g.T

    pre = conv_pre(extended(x_ref[...], xh_ref[...]), xw_ref[...])
    values = pre * sigmoid(pre)
    val_ref[...] = values
    heads = expander(j)
    cum = dot_nn(cum_ref[...], heads)
    last = cum[ROWS - 1 : ROWS]
    high, rest = split2(values * dot_nn(step_ref[...], heads) * jnp.exp(last - cum))
    twice = dot_nn(bt_ref[...], high)
    state_ref[...] = twice[0:128] + twice[128:256] + dot_nn(bt_ref[0:128, :], rest)
    dec_ref[...] = jnp.broadcast_to(jnp.exp(last), (8, WIDE))


def whole(shape):
    return pl.BlockSpec(shape, lambda j: (0, 0))


def lanes(rows, first=0):
    return pl.BlockSpec((rows, WIDE), lambda j: (0, first + j))


def fixed(rows, at, width=WIDE):
    return pl.BlockSpec((rows, width), lambda j: (0, at))


def sds(rows, cols, dtype):
    return jax.ShapeDtypeStruct((rows, cols), dtype)


def grid_params():
    return pltpu.CompilerParams(vmem_limit_bytes=48 * MIB)


def front(proj, halo, taps, hp):
    square = (ROWS, ROWS)
    return pl.pallas_call(
        front_kernel,
        grid=(STEPS,),
        in_specs=[
            lanes(ROWS, STEPS), fixed(ROWS, 2 * STEPS), fixed(ROWS, 50, 128),
            lanes(8), fixed(8, STEPS), lanes(8), fixed(8, STEPS), whole((8, 128)),
        ],
        out_specs=[
            lanes(ROWS), lanes(128), lanes(8),
            whole((ROWS, 384)), whole((ROWS, 384)), whole((128, ROWS)),
            whole((ROWS, 256)), whole((ROWS, 384)), whole((128, ROWS)), whole(square), whole(square),
        ],
        out_shape=[
            sds(ROWS, INNER, F32), sds(128, INNER, F32), sds(8, INNER, F32),
            sds(ROWS, 384, BF16), sds(ROWS, 384, BF16), sds(128, ROWS, F32),
            sds(ROWS, 256, BF16), sds(ROWS, 384, BF16), sds(128, ROWS, BF16), sds(*square, F32), sds(*square, F32),
        ],
        scratch_shapes=[pltpu.VMEM((256, ROWS), BF16)],
        compiler_params=grid_params(),
        cost_estimate=pl.CostEstimate(flops=10**9, bytes_accessed=10 * MIB, transcendentals=10**6),
    )(proj, proj, proj, halo, halo, taps, taps, hp)


def exchange_kernel(
    n, rev, s_ref, d_ref, o_ref, inbox, dbox, parts, decs, total, chain_out, chain_in, outbox,
    send_a, recv_a, send_d, recv_d, send_c, recv_c, send_o, recv_o,
):
    planes = n // PLANE
    section = lax.axis_index("section")
    q = lax.axis_index("seq")
    u = n - 1 - q if rev else q
    spot, level = lax.rem(u, PLANE), u // PLANE

    def device(at):
        return (section, n - 1 - at if rev else at)

    peers = [lax.rem(spot + k, PLANE) for k in range(1, PLANE)]
    barrier = pltpu.get_barrier_semaphore()
    for peer in peers:
        pl.semaphore_signal(barrier, inc=1, device_id=device(level * PLANE + peer), device_id_type=MESH)

    @pl.when(level > 0)
    def _():
        pl.semaphore_signal(barrier, inc=1, device_id=device(u - PLANE), device_id_type=MESH)

    pl.semaphore_wait(barrier, PLANE - 1 + (level < planes - 1).astype(jnp.int32))

    def group(at):
        return pl.ds(pl.multiple_of(at * LANES, LANES), LANES)

    first = []
    for k, peer in enumerate(peers):
        to = device(level * PLANE + peer)
        first.append(
            pltpu.make_async_remote_copy(
                src_ref=d_ref.at[:, group(peer)], dst_ref=dbox.at[spot],
                send_sem=send_d.at[k], recv_sem=recv_d.at[k], device_id=to, device_id_type=MESH,
            )
        )
        first.append(
            pltpu.make_async_remote_copy(
                src_ref=s_ref.at[:, group(peer)], dst_ref=inbox.at[spot],
                send_sem=send_a.at[k], recv_sem=recv_a.at[k], device_id=to, device_id_type=MESH,
            )
        )
    for copy in first:
        copy.start()
    inbox[spot] = s_ref[:, group(spot)]
    dbox[spot] = d_ref[:, group(spot)]
    for copy in first:
        copy.wait()

    cuts = LANES // 256
    for b in range(cuts):
        at = slice(b * 256, b * 256 + 256)
        state = inbox[0, :, at].astype(F32)
        decay = dbox[0, 0:1, at]
        for p in range(1, PLANE):
            parts[p, :, at] = state
            decs[p, 0:1, at] = decay
            d = dbox[p, 0:1, at]
            state = d * state + inbox[p, :, at].astype(F32)
            decay = decay * d
        total[:, at] = state
        decs[0, 0:1, at] = decay

    def chain(b):
        return pltpu.make_async_remote_copy(
            src_ref=chain_out.at[b], dst_ref=chain_in.at[b],
            send_sem=send_c.at[b], recv_sem=recv_c.at[b],
            device_id=device(lax.rem(u + PLANE, n)), device_id_type=MESH,
        )

    last = []
    for b in range(cuts):
        at = slice(b * 256, b * 256 + 256)

        @pl.when(level > 0)
        def _():
            chain(b).wait_recv()

        @pl.when(level == 0)
        def _():
            chain_in[b] = jnp.zeros((128, 256), chain_in.dtype)

        enter = chain_in[b].astype(F32)

        @pl.when(level < planes - 1)
        def _():
            chain_out[b] = (decs[0, 0:1, at] * enter + total[:, at]).astype(chain_out.dtype)
            chain(b).start()

        outbox[0, :, at] = enter.astype(outbox.dtype)
        for p in range(1, PLANE):
            outbox[p, :, at] = (decs[p, 0:1, at] * enter + parts[p, :, at]).astype(outbox.dtype)
        mine = pl.ds(pl.multiple_of(spot * LANES + b * 256, 256), 256)
        o_ref[:, mine] = outbox[spot, :, at]
        for k, peer in enumerate(peers):
            copy = pltpu.make_async_remote_copy(
                src_ref=outbox.at[peer, :, pl.ds(b * 256, 256)], dst_ref=o_ref.at[:, mine],
                send_sem=send_o.at[b * 3 + k], recv_sem=recv_o.at[b * 3 + k],
                device_id=device(level * PLANE + peer), device_id_type=MESH,
            )
            copy.start()
            last.append(copy)
    for copy in last:
        copy.wait()

    @pl.when(level < planes - 1)
    def _():
        for b in range(cuts):
            chain(b).wait_send()


def exchange(state, decay, n, rev):
    vmem = pl.BlockSpec(memory_space=pltpu.VMEM)
    dma = pltpu.SemaphoreType.DMA
    cuts = LANES // 256
    return pl.pallas_call(
        functools.partial(exchange_kernel, n, rev),
        out_shape=sds(128, INNER, state.dtype),
        in_specs=[vmem, vmem],
        out_specs=vmem,
        scratch_shapes=[
            pltpu.VMEM((PLANE, 128, LANES), state.dtype),
            pltpu.VMEM((PLANE, 8, LANES), F32),
            pltpu.VMEM((PLANE, 128, LANES), F32),
            pltpu.VMEM((PLANE, 8, LANES), F32),
            pltpu.VMEM((128, LANES), F32),
            pltpu.VMEM((cuts, 128, 256), state.dtype),
            pltpu.VMEM((cuts, 128, 256), state.dtype),
            pltpu.VMEM((PLANE, 128, LANES), state.dtype),
            dma((3,)), dma((3,)), dma((3,)), dma((3,)),
            dma((cuts,)), dma((cuts,)), dma((3 * cuts,)), dma((3 * cuts,)),
        ],
        compiler_params=pltpu.CompilerParams(
            collective_id=2 if rev else 1, has_side_effects=True, vmem_limit_bytes=32 * MIB
        ),
    )(state, decay)


def decay_block(later, earlier):
    return jnp.exp(jnp.minimum(later - earlier, 0.0))


def head_lanes(parts, i):
    at = (i // 2) * 128
    here = (iota((ROWS, 128), 1) < HEADDIM) if i % 2 == 0 else (iota((ROWS, 128), 1) >= HEADDIM)
    return [jnp.where(here, part[:, at : at + 128], jnp.zeros((), BF16)) for part in parts]


def mix_kernel(
    g_ref, step_ref, cum_ref, cumt_ref, val_ref, gate_ref, c_ref, car_ref, lp_ref, gain_ref,
    y_ref, low_ref, gated_ref, sum_ref,
):
    j = pl.program_id(0)
    heads = expander(j)
    cum = dot_nn(cum_ref[...], heads)
    values = val_ref[...]
    scaled = split2(values * dot_nn(step_ref[...], heads))
    car_high, car_rest = split2(car_ref[...])
    across = dot_nn(c_ref[...], jnp.concatenate([car_high, car_high, car_rest], axis=0))
    y = jnp.exp(cum) * across + lp_ref[0:1, :] * values
    sides = []
    for pair in range(WIDE // 128):
        top = jnp.zeros((HALF, 128), F32)
        bottom = jnp.zeros((HALF, 128), F32)
        for i in (2 * pair, 2 * pair + 1):
            row = cumt_ref[pl.ds((WIDE // HEADDIM) * j + i, 1), :]
            column = cum[:, i * HEADDIM : i * HEADDIM + 1]
            part = head_lanes(scaled, i)
            upper = split2(g_ref[0:HALF, 0:HALF] * decay_block(column[0:HALF], row[:, 0:HALF]))
            top = top + fine(dot_nn, upper, [v[0:HALF] for v in part])
            lower = split2(g_ref[HALF:ROWS, :] * decay_block(column[HALF:ROWS], row))
            bottom = bottom + fine(dot_nn, lower, part)
        sides.append(jnp.concatenate([top, bottom], axis=0))
    y = y + jnp.concatenate(sides, axis=1)
    y_ref[...] = y
    gate = gate_ref[...]
    gated = y * (gate * sigmoid(gate))
    gated_ref[j] = gated

    @pl.when(j == 0)
    def _():
        sum_ref[...] = jnp.zeros_like(sum_ref)

    sum_ref[...] += gated * gated

    @pl.when(j == STEPS - 1)
    def _():
        mean = jnp.sum(sum_ref[...], axis=1, keepdims=True) * (1.0 / INNER)
        scale = lax.rsqrt(mean + EPS)
        for k in range(STEPS):
            at = slice(k * WIDE, k * WIDE + WIDE)
            low_ref[:, at] = (gated_ref[k] * scale * gain_ref[1:2, at]).astype(BF16)


def mix(g, step, cum, cumt, values, proj, c, carried, lp):
    return pl.pallas_call(
        mix_kernel,
        grid=(STEPS,),
        in_specs=[
            whole((ROWS, ROWS)), whole((ROWS, 384)), whole((ROWS, 384)), whole((128, ROWS)),
            lanes(ROWS), lanes(ROWS), whole((ROWS, 384)), lanes(128), lanes(8),
            whole((8, INNER)),
        ],
        out_specs=[lanes(ROWS), whole((ROWS, INNER))],
        out_shape=[sds(ROWS, INNER, F32), sds(ROWS, INNER, BF16)],
        scratch_shapes=[pltpu.VMEM((STEPS, ROWS, WIDE), F32), pltpu.VMEM((ROWS, WIDE), F32)],
        compiler_params=grid_params(),
        cost_estimate=pl.CostEstimate(flops=3 * 10**9, bytes_accessed=14 * MIB, transcendentals=4 * 10**6),
    )(g, step, cum, cumt, values, proj, c, carried, lp, lp)


def gate_back_kernel(
    dg_ref, y_ref, gate_ref, cum_ref, ct_ref, lp_ref, dy_ref, dgate_ref, gain_ref, dcar_ref,
    dg_all, y_all, gate_all, square_acc, cross_acc,
):
    phase, j = pl.program_id(0), pl.program_id(1)

    @pl.when(jnp.logical_and(phase == 0, j == 0))
    def _():
        square_acc[...] = jnp.zeros_like(square_acc)
        cross_acc[...] = jnp.zeros_like(cross_acc)

    @pl.when(phase == 0)
    def _():
        dg, y, gate = dg_ref[...], y_ref[...], gate_ref[...]
        dg_all[j], y_all[j], gate_all[j] = dg, y, gate
        gated = y * (gate * sigmoid(gate))
        square_acc[...] += gated * gated
        cross_acc[...] += dg * lp_ref[1:2, :] * gated

    @pl.when(phase == 1)
    def _():
        r = lax.rsqrt(jnp.sum(square_acc[...], axis=1, keepdims=True) * (1.0 / INNER) + EPS)
        m = jnp.sum(cross_acc[...], axis=1, keepdims=True) * (1.0 / INNER) * r * r
        dg, y, gate = dg_all[j], y_all[j], gate_all[j]
        s = sigmoid(gate)
        silu = gate * s
        gated = y * silu
        gain_ref[...] = jnp.broadcast_to(jnp.sum(dg * gated * r, axis=0, keepdims=True), (8, WIDE))
        d_gated = r * (dg * lp_ref[1:2, :] - gated * m)
        dy = d_gated * silu
        dy_ref[...] = dy
        dgate_ref[...] = (d_gated * y * (s + silu * (1.0 - s))).astype(BF16)
        cum = dot_nn(cum_ref[...], expander(j))
        dcar_ref[...] = dot_nn(ct_ref[...], (dy * jnp.exp(cum)).astype(BF16)).astype(BF16)


def gate_back(dg, y, proj, cum, ct, lp):
    def first(rows):
        return pl.BlockSpec((rows, WIDE), lambda p, j: (0, j * (1 - p) + (STEPS - 1) * p))

    def second(rows):
        return pl.BlockSpec((rows, WIDE), lambda p, j: (0, j * p))

    def both(shape):
        return pl.BlockSpec(shape, lambda p, j: (0, 0))

    kept = pltpu.VMEM((STEPS, ROWS, WIDE), F32)
    return pl.pallas_call(
        gate_back_kernel,
        grid=(2, STEPS),
        in_specs=[
            first(ROWS), first(ROWS), first(ROWS), both((ROWS, 384)), both((128, ROWS)),
            pl.BlockSpec((8, WIDE), lambda p, j: (0, j)),
        ],
        out_specs=[second(ROWS), second(ROWS), second(8), second(128)],
        out_shape=[sds(ROWS, INNER, F32), sds(ROWS, INNER, BF16), sds(8, INNER, F32), sds(128, INNER, BF16)],
        scratch_shapes=[kept, kept, kept, pltpu.VMEM((ROWS, WIDE), F32), pltpu.VMEM((ROWS, WIDE), F32)],
        compiler_params=grid_params(),
        cost_estimate=pl.CostEstimate(flops=10**9, bytes_accessed=16 * MIB, transcendentals=2 * 10**6),
    )(dg, y, proj, cum, ct, lp)


def core_back_kernel(
    x_ref, bc_ref, raw_ref, xh_ref, bch_ref, xw_ref, bcw_ref, hp_ref,
    step_ref, cum_ref, cumt_ref, gt_ref, b_ref, c_ref, y_ref, dy_ref, car_ref, late_ref, lp_ref,
    dx_ref, dbc_ref, tail_ref, tailbc_ref, head_ref, headbc_ref, taps_ref, tapsbc_ref, draw_ref, hg_ref,
    dgt_acc, dc_acc, db_acc, dcum_acc, dstep_acc, rows_acc,
):
    j = pl.program_id(0)

    @pl.when(j == 0)
    def _():
        for acc in (dgt_acc, dc_acc, db_acc, dcum_acc, dstep_acc, rows_acc):
            acc[...] = jnp.zeros_like(acc)

    ext = extended(x_ref[...], xh_ref[...])
    pre = conv_pre(ext, xw_ref[...])
    sig = sigmoid(pre)
    values = pre * sig
    heads, to_heads = expander(j), collector(j)
    step = dot_nn(step_ref[...], heads)
    cum = dot_nn(cum_ref[...], heads)
    last = cum[ROWS - 1 : ROWS]
    scaled = values * step
    scaled_parts = split2(scaled)
    dy = dy_ref[...]
    dy_parts = split2(dy)
    sides = []
    for pair in range(WIDE // 128):
        top = jnp.zeros((HALF, 128), F32)
        bottom = jnp.zeros((HALF, 128), F32)
        at = slice(pair * 128, pair * 128 + 128)
        own = [part[:, at] for part in scaled_parts]
        for i in (2 * pair, 2 * pair + 1):
            row = cumt_ref[pl.ds((WIDE // HEADDIM) * j + i, 1), :]
            column = cum[:, i * HEADDIM : i * HEADDIM + 1]
            part = head_lanes(dy_parts, i)
            decay = decay_block(row, column[0:HALF])
            top = top + fine(dot_nn, split2(gt_ref[0:HALF, :] * decay), part)
            dgt_acc[0:HALF, :] += fine(dot_nt, [v[0:HALF] for v in own], part) * decay
            decay = decay_block(row[:, HALF:ROWS], column[HALF:ROWS])
            late_part = [v[HALF:ROWS] for v in part]
            bottom = bottom + fine(dot_nn, split2(gt_ref[HALF:ROWS, HALF:ROWS] * decay), late_part)
            dgt_acc[HALF:ROWS, HALF:ROWS] += fine(dot_nt, [v[HALF:ROWS] for v in own], late_part) * decay
        sides.append(jnp.concatenate([top, bottom], axis=0))
    car, late = car_ref[...], late_ref[...]
    to_end = jnp.exp(last - cum)
    d_ended = dot_nn(b_ref[:, 0:128], late)
    ended = scaled * to_end
    dc_acc[...] += fine(dot_nt, split2(dy * jnp.exp(cum)), split2(car))
    db_acc[...] += dot_nt(ended.astype(BF16), late)
    d_total = jnp.concatenate(sides, axis=1) + to_end * d_ended
    skip_w = lp_ref[0:1, :]
    dcum_acc[...] += collect(dy * (y_ref[...] - skip_w * values) - scaled * d_total, to_heads)
    dstep_acc[...] += collect(d_total * values, to_heads)
    at_last = jnp.exp(last) * jnp.sum(late.astype(F32) * car, axis=0, keepdims=True)
    at_last = at_last + jnp.sum(ended * d_ended, axis=0, keepdims=True)
    skip = jnp.sum(dy * values, axis=0, keepdims=True)
    rows_acc[...] += collect(jnp.concatenate([at_last, skip, jnp.zeros((6, WIDE), F32)], axis=0), to_heads)
    d_pre = (skip_w * dy + step * d_total) * (sig + values * (1.0 - sig))
    taps_ref[...] = tap_grads(d_pre, ext)
    head_ref[...] = d_pre[0:8]
    d_conv = conv_back(d_pre, xw_ref[...])
    dx_ref[...] = d_conv.astype(BF16)
    tail_ref[...] = d_conv[ROWS - 8 : ROWS]

    @pl.when(j == STEPS - 1)
    def _():
        seen = iota((ROWS, ROWS), 1) >= iota((ROWS, ROWS), 0)
        d_gt = split2(jnp.where(seen, dgt_acc[...], 0.0))
        d_c = dc_acc[...] + fine(dot_tn, d_gt, halves(b_ref))
        d_b = db_acc[...] + fine(dot_nn, d_gt, halves(c_ref))
        ext_bc = extended(bc_ref[...], bch_ref[...])
        pre_bc = conv_pre(ext_bc, bcw_ref[...])
        sig_bc = sigmoid(pre_bc)
        d_pre_bc = jnp.concatenate([d_b, d_c], axis=1) * (sig_bc + pre_bc * sig_bc * (1.0 - sig_bc))
        tapsbc_ref[...] = tap_grads(d_pre_bc, ext_bc)
        headbc_ref[...] = d_pre_bc[0:8]
        d_conv_bc = conv_back(d_pre_bc, bcw_ref[...])
        dbc_ref[...] = d_conv_bc.astype(BF16)
        tailbc_ref[...] = d_conv_bc[ROWS - 8 : ROWS]
        raw, step_all, rate = step_parts(raw_ref, hp_ref)
        end = iota((ROWS, 128), 0) == ROWS - 1
        d_cum_all = dcum_acc[...] + jnp.where(end, rows_acc[0:1, :], 0.0)
        d_log = exact_left(triangle(False), d_cum_all)
        d_step = dstep_acc[...] + rate * d_log
        d_raw = jnp.where(iota((ROWS, 128), 1) < HEADS, d_step * sigmoid(raw), 0.0)
        draw_ref[...] = d_raw.astype(BF16)
        hg_ref[...] = jnp.concatenate(
            [
                jnp.sum(d_raw, axis=0, keepdims=True),
                jnp.sum(d_log * rate * step_all, axis=0, keepdims=True),
                rows_acc[1:2, :],
                jnp.zeros((5, 128), F32),
            ],
            axis=0,
        )


def core_back(proj, halo, taps, hp, step, cum, cumt, gt, b, c, y, dy, carried, late, lp):
    acc = pltpu.VMEM((ROWS, 128), F32)
    return pl.pallas_call(
        core_back_kernel,
        grid=(STEPS,),
        in_specs=[
            lanes(ROWS, STEPS), fixed(ROWS, 2 * STEPS), fixed(ROWS, 50, 128),
            lanes(8), fixed(8, STEPS), lanes(8), fixed(8, STEPS), whole((8, 128)),
            whole((ROWS, 384)), whole((ROWS, 384)), whole((128, ROWS)), whole((ROWS, ROWS)),
            whole((ROWS, 256)), whole((ROWS, 384)),
            lanes(ROWS), lanes(ROWS), lanes(128), lanes(128), lanes(8),
        ],
        out_specs=[
            lanes(ROWS), whole((ROWS, 256)), lanes(8), whole((8, 256)), lanes(8), whole((8, 256)),
            lanes(8), whole((8, 256)), whole((ROWS, 128)), whole((8, 128)),
        ],
        out_shape=[
            sds(ROWS, INNER, BF16), sds(ROWS, 256, BF16), sds(8, INNER, F32), sds(8, 256, F32),
            sds(8, INNER, F32), sds(8, 256, F32), sds(8, INNER, F32), sds(8, 256, F32),
            sds(ROWS, 128, BF16), sds(8, 128, F32),
        ],
        scratch_shapes=[pltpu.VMEM((ROWS, ROWS), F32), acc, acc, acc, acc, pltpu.VMEM((8, 128), F32)],
        compiler_params=grid_params(),
        cost_estimate=pl.CostEstimate(flops=8 * 10**9, bytes_accessed=14 * MIB, transcendentals=5 * 10**6),
    )(
        proj, proj, proj, halo, halo, taps, taps, hp,
        step, cum, cumt, gt, b, c, y, dy, carried, late, lp,
    )


def swap(value):
    return lax.ppermute(value, "section", [(0, 1), (1, 0)])


def shifted(value, distance, n):
    return lax.ppermute(value, "seq", [(i, i + distance) for i in range(n) if 0 <= i + distance < n])


def plane_route(k, n):
    return [(i, i - i % PLANE + (i + k) % PLANE) for i in range(n)]


def rms(value):
    return lax.rsqrt(jnp.mean(value * value, axis=-1, keepdims=True) + EPS)


def tied(value, *others):
    return lax.optimization_barrier((value, *others))[0]


def copies_of(value, n):
    return [value] + [lax.ppermute(value, "seq", plane_route(k, n)) for k in range(1, PLANE)]


def pieces_of(value, n):
    spot = lax.axis_index("seq") % PLANE
    width = value.shape[1] // PLANE
    got = [lax.dynamic_slice_in_dim(value, spot * width, width, 1)]
    for k in range(1, PLANE):
        part = lax.dynamic_slice_in_dim(value, (spot + k) % PLANE * width, width, 1)
        got.append(lax.ppermute(part, "seq", plane_route(k, n)))
    return got


def partial_grad(left, right):
    core = lax.axis_index("section")
    left, right = jnp.concatenate(left, axis=0), jnp.concatenate(right, axis=0)
    half = right.shape[1] // 2
    away = dot_tn(left, lax.dynamic_slice_in_dim(right, (1 - core) * half, half, 1)).astype(BF16)
    mine = dot_tn(left, lax.dynamic_slice_in_dim(right, core * half, half, 1))
    return (mine + swap(away).astype(F32)).astype(BF16)


def plane_rows(partials, n):
    planes = n // PLANE
    columns = [[p + PLANE * z for z in range(planes)] for p in range(PLANE)]
    joined = jnp.concatenate([part.reshape(planes, D // planes, -1) for part in partials], axis=2)
    joined = lax.psum_scatter(joined, "seq", scatter_dimension=0, axis_index_groups=columns)
    return jnp.split(joined, [sum(p.shape[1] for p in partials[:k]) for k in range(1, len(partials))], axis=1)


def stacked_halves(value, n):
    planes = n // PLANE
    value = value.reshape(planes, -1, D // 2)
    return jnp.concatenate([value[:, :, : D // 4], value[:, :, D // 4 :]], axis=1).reshape(D, D // 4)


def unstacked_halves(value):
    rows = value.shape[0] // 2
    return jnp.concatenate([value[:rows], value[rows:]], axis=1)


def by_row(value, n):
    in_plane = [[PLANE * z + p for p in range(PLANE)] for z in range(n // PLANE)]
    rows = value.shape[0] // PLANE
    value = value.reshape(PLANE, rows, value.shape[1])
    return lax.all_to_all(value, "seq", 0, 0, axis_index_groups=in_plane).transpose(1, 0, 2)


SIZES = [D, CONVD * CONV, CONVD, HEADS, HEADS, HEADS, INNER]


def split_small(flat):
    parts, at = [], 0
    for size in SIZES:
        parts.append(flat[at : at + size])
        at += size
    return parts


def unpack_params(flat):
    norm_g, conv_w, conv_b, dt_b, a_lg, skip_w, gate_g = split_small(flat)
    taps = jnp.concatenate(
        [conv_w.reshape(CONV, CONVD), conv_b[None], jnp.zeros((3, CONVD), F32)], axis=0
    )
    pad = jnp.zeros((128 - HEADS,), F32)
    hp = jnp.concatenate([dt_b, pad, a_lg, pad, jnp.zeros((6 * 128,), F32)]).reshape(8, 128)
    lp = jnp.concatenate(
        [jnp.repeat(skip_w, HEADDIM)[None], gate_g[None], jnp.zeros((6, INNER), F32)], axis=0
    )
    return norm_g, taps, hp, lp


def per_device(
    inputs, cotangent, norm_gain, in_weight, conv_weight, conv_bias, dt_bias, a_log, d_skip,
    gate_norm_gain, out_weight,
):
    n = lax.axis_size("seq")
    planes = n // PLANE
    core = lax.axis_index("section")
    place = lax.axis_index("seq")
    first = core == 0
    own_in, own_out = in_weight[0].T, out_weight[0]
    other_in, other_out = swap(own_in), swap(own_out)
    own_small = jnp.concatenate(
        [
            norm_gain[0], conv_weight[0].T.reshape(-1), conv_bias[0], dt_bias[0], a_log[0], d_skip[0],
            gate_norm_gain[0],
        ]
    )
    other_small = swap(own_small)
    flags = [(core == layer).astype(jnp.int32)[None] for layer in range(2)]
    params = [
        unpack_params(jnp.where(first, own_small, other_small)),
        unpack_params(jnp.where(first, other_small, own_small)),
    ]

    def mine(pair):
        return lax.dynamic_index_in_dim(pair, core, 0, keepdims=False)

    def project(layer, h):
        normed = (h * rms(h) * params[layer][0]).astype(BF16)
        return normed, mm(normed, own_in, other_in, flags[layer], True, 1664)

    def blocks(layer, proj):
        _, taps, hp, _ = params[layer]
        halo = shifted(proj[ROWS - 8 :, INNER : INNER + CONVD], 1, n)
        return halo, front(proj, halo, taps, hp)

    def finish(layer, h, proj, parts, carried):
        values, _, _, step, cum, cumt, _, c, _, g, _ = parts
        y, gated_low = mix(g, step, cum, cumt, values, proj, c, carried, params[layer][3])
        return y, gated_low, h + mm(gated_low, own_out, other_out, flags[layer], False, 768)

    def by_owner(gated_low):
        width = INNER // n
        return gated_low.reshape(ROWS, planes, PLANE, width).transpose(0, 2, 1, 3).reshape(ROWS, INNER)

    d_out_1 = mine(cotangent)
    lows_1 = copies_of(d_out_1, n)
    h_0 = mine(inputs).astype(F32)
    normed_0, proj_0 = project(0, h_0)
    proj_0 = tied(proj_0, *lows_1)
    halo_0, parts_0 = blocks(0, proj_0)
    carried_0 = exchange(parts_0[1], parts_0[2], n, False)
    normeds_0 = copies_of(tied(normed_0, carried_0), n)
    y_0, gated_0, out_0 = finish(0, h_0, proj_0, parts_0, carried_0)
    act_0 = out_0.astype(BF16)

    h_1 = act_0.astype(F32)
    normed_1, proj_1 = project(1, h_1)
    proj_1 = tied(proj_1, *normeds_0)
    halo_1, parts_1 = blocks(1, proj_1)
    gateds_0 = pieces_of(by_owner(tied(gated_0, halo_1)), n)
    carried_1 = exchange(tied(parts_1[1], *gateds_0), parts_1[2], n, False)
    normeds_1 = copies_of(tied(normed_1, carried_1), n)
    y_1, gated_1, out_1 = finish(1, h_1, proj_1, parts_1, carried_1)
    act_1 = out_1.astype(BF16)

    def gate_side(layer, d_low, y, proj, parts):
        d_gated_low = mm(d_low, own_out, other_out, flags[layer], True, 1024)
        return gate_back(d_gated_low, y, proj, parts[4], parts[8], params[layer][3])

    def core_side(layer, proj, halo, parts, y, dy, carried, late):
        _, taps, hp, lp = params[layer]
        _, _, _, step, cum, cumt, b, c, _, _, gt = parts
        return core_back(proj, halo, taps, hp, step, cum, cumt, gt, b, c, y, dy, carried, late, lp)

    def conv_side(layer, back):
        dx, dbc, tail, tailbc, head, headbc, gtaps, gtapsbc, d_raw, heads = back
        w = params[layer][1]
        a = shifted(jnp.concatenate([head, headbc], axis=1), -1, n)
        fix = jnp.concatenate(
            [
                jnp.zeros((5, CONVD), F32),
                w[0:1] * a[0:1],
                w[0:1] * a[1:2] + w[1:2] * a[0:1],
                w[0:1] * a[2:3] + w[1:2] * a[1:2] + w[2:3] * a[0:1],
            ],
            axis=0,
        )
        low = (jnp.concatenate([tail, tailbc], axis=1) + fix).astype(BF16)
        main = jnp.concatenate([dx[: ROWS - 8], dbc[: ROWS - 8]], axis=1)
        d_conv = jnp.concatenate([main, low], axis=0)
        return d_conv, d_raw[:, :HEADS]

    def norm_side(layer, h, d_out, d_proj):
        norm_g = params[layer][0]
        d_normed = mm(d_proj, own_in, other_in, flags[layer], False, 512)
        r = rms(h)
        v = d_normed * norm_g
        d_h = d_out + r * (v - h * (r * r * jnp.mean(v * h, axis=-1, keepdims=True)))
        return d_h, jnp.sum(d_normed * h * r, axis=0)

    def small_of(norm_gain_grad, back, gate_gain):
        taps_all = jnp.concatenate([back[6], back[7]], axis=1)
        heads = back[9]
        return jnp.concatenate(
            [
                norm_gain_grad, taps_all[:CONV].reshape(-1), taps_all[CONV],
                heads[0, :HEADS], heads[1, :HEADS], heads[2, :HEADS], gate_gain[0],
            ]
        )

    def padded(d_conv, d_raw):
        pad = jnp.zeros((ROWS, REST - CONVD - HEADS), BF16)
        return jnp.concatenate([d_conv, d_raw, pad], axis=1)

    dy_1, d_gate_1, gain_1, d_carried_1 = gate_side(1, d_out_1, y_1, proj_1, parts_1)
    late_1 = exchange(tied(d_carried_1, *normeds_1), parts_1[2], n, True)
    gates_1 = pieces_of(tied(d_gate_1, late_1), n)
    gateds_1 = pieces_of(by_owner(tied(gated_1, late_1)), n)
    back_1 = core_side(1, proj_1, halo_1, parts_1, y_1, dy_1, carried_1, late_1)
    back_1 = [tied(back_1[0], *gates_1, *gateds_1)] + list(back_1[1:])
    d_conv_1, d_raw_1 = conv_side(1, back_1)
    rests_1 = pieces_of(padded(d_conv_1, d_raw_1), n)
    d_1, ng_1 = norm_side(1, h_1, d_out_1.astype(F32), jnp.concatenate([d_gate_1, d_conv_1, d_raw_1], axis=1))

    d_out_0 = d_1.astype(BF16)
    lows_0 = copies_of(tied(d_out_0, *rests_1), n)
    dy_0, d_gate_0, gain_0, d_carried_0 = gate_side(0, d_out_0, y_0, proj_0, parts_0)
    outw_1 = stacked_halves(partial_grad(gateds_1, lows_1), n)
    grads_1 = [outw_1, partial_grad(normeds_1, gates_1), partial_grad(normeds_1, rests_1)]
    late_0 = exchange(tied(d_carried_0, *grads_1), parts_0[2], n, True)
    outw_1, gatew_1, restw_1 = plane_rows(grads_1, n)
    gates_0 = pieces_of(tied(d_gate_0, late_0, *lows_0), n)
    outw_0 = stacked_halves(partial_grad(gateds_0, lows_0), n)
    back_0 = core_side(0, proj_0, halo_0, parts_0, y_0, dy_0, carried_0, tied(late_0, *lows_0, outw_0))
    (outw_0,) = plane_rows([outw_0], n)
    back_0 = [tied(back_0[0], *gates_0, outw_1, gatew_1, restw_1)] + list(back_0[1:])
    d_conv_0, d_raw_0 = conv_side(0, back_0)
    rests_0 = pieces_of(padded(d_conv_0, d_raw_0), n)
    (gatew_0,) = plane_rows([partial_grad(normeds_0, gates_0)], n)
    d_0, ng_0 = norm_side(0, h_0, d_out_0.astype(F32), jnp.concatenate([d_gate_0, d_conv_0, d_raw_0], axis=1))
    (restw_0,) = plane_rows([partial_grad(normeds_0, rests_0)], n)

    def joined(early, late):
        own = jnp.where(first, early, late)
        other = swap(jnp.where(first, late, early))
        return jnp.where(first, own, other), jnp.where(first, other, own)

    def both(early, late):
        return jnp.stack(joined(early, late))[None]

    acts = both(act_0, act_1)
    input_grads = both(d_0, d_1)
    gate_w = jnp.stack(joined(by_row(gatew_0, n), by_row(gatew_1, n)), axis=2)
    rest_w = jnp.stack(joined(by_row(restw_0, n), by_row(restw_1, n)), axis=2)
    rows = D // n
    g_in = jnp.concatenate(
        [gate_w.reshape(rows, INNER), rest_w.reshape(rows, REST)[:, : PROJ - INNER]], axis=1
    ).astype(F32)
    g_out = jnp.concatenate(joined(unstacked_halves(outw_0), unstacked_halves(outw_1)), axis=1).astype(F32)
    small_0, small_1 = small_of(ng_0, back_0, gain_0), small_of(ng_1, back_1, gain_1)
    small = jnp.where(first, small_0, small_1) + swap(jnp.where(first, small_1, small_0))
    reach = 1
    while reach < n:
        small = small + lax.ppermute(small, "seq", [(i, i ^ reach) for i in range(n)])
        reach *= 2
    norm_g, conv_w, conv_b, dt_b, a_lg, skip_w, gate_g = split_small(small)

    def share(value):
        rows = value.shape[0] // n
        return lax.dynamic_slice_in_dim(value, place * rows, rows, 0)[None]

    conv_rows = CONVD // n
    conv_w = lax.dynamic_slice_in_dim(conv_w.reshape(CONV, CONVD), place * conv_rows, conv_rows, 1).T
    return (
        acts, input_grads, share(norm_g), g_in[None], conv_w[None], share(conv_b),
        dt_b[None], a_lg[None], skip_w[None], share(gate_g), g_out[None],
    )


def solution(mesh):
    in_specs = (
        P(None, "seq", None), P(None, "seq", None), P("section", None), P("section", None, None),
        P("section", None, None), P("section", None), P("section", None), P("section", None),
        P("section", None), P("section", None), P("section", None, None),
    )
    out_specs = (
        P("section", None, "seq", None), P("section", None, "seq", None), P("section", "seq"),
        P("section", "seq", None), P("section", "seq", None), P("section", "seq"), P("section", None),
        P("section", None), P("section", None), P("section", "seq"), P("section", "seq", None),
    )
    return jax.shard_map(per_device, mesh=mesh, in_specs=in_specs, out_specs=out_specs, check_vma=False)
```

time: 943 us -> 814 us (0.86)
  Pallas kernels: 457 us -> 381 us
  local copies, waits for them, and re-layouts: 134 us -> 95.2 us
  waiting for transfers between devices: 157 us -> 129 us
  other arithmetic: 38.2 us -> 50.4 us
    ppermute x12, waiting for transfers between devices: 91.2 us -> 30.1 us  [copies_of(): lax.ppermute(value, 'seq', plane_route(k, n))]
    pallas_call x8, Pallas kernels: 197 us -> 151 us  [the longest x2 64 us: core_back(): pl.pallas_call(core_back_kernel, grid=(STEPS,), in_specs=[lanes(ROWS, STE...]
    ppermute x1 -> x0, local copies, waits for them, and re-layouts: 24.3 us -> none  [swap(): return lax.ppermute(value, 'section', [(0, 1), (1, 0)])]
    unnamed x186 -> x291, local copies, waits for them, and re-layouts: 43.6 us -> 21.1 us
    ppermute x12, starting transfers between devices: 46.6 us -> 24.4 us  [copies_of(): lax.ppermute(value, 'seq', plane_route(k, n))]
    pallas_call x4, Pallas kernels: 170 us -> 151 us  [exchange(): pl.pallas_call(functools.partial(exchange_kernel, n, rev), out_shape=sds(...]
    ppermute x8 -> x15, waiting for transfers between devices: 0.02 us -> 18.9 us  [swap(): return lax.ppermute(value, 'section', [(0, 1), (1, 0)])]
    concatenate x8 -> x16, local copies, waits for them, and re-layouts: 1.16 us -> 19 us  [the longest x2 7.57 us: padded(): return jnp.concatenate([d_conv, d_raw, pad], axis=1)]
  transfers between devices with their start and end apart: 46 -> 61, of which waited for: 16 -> 18; matrix products, arithmetic and copies ran while one was open for 19% -> 18% of each run, Pallas kernels for 46% -> 32%
where the time goes in v2:
time: 814 us; the launch traced here: 805 us
  Pallas kernels  381 us (47%)
  waiting for transfers between devices  129 us (16%)
  local copies, waits for them, and re-layouts  95.2 us (12%)
  starting transfers between devices  94.4 us (12%)
  other arithmetic  50.4 us (6%)
  matrix products  38.2 us (5%)
  between operations  16.1 us (2%)
    pallas_call x4, Pallas kernels, exchange(): pl.pallas_call(functools.partial(exchange_kernel, n, rev), out_shape=sds(...  151 us
    pallas_call x8, Pallas kernels, mm(): pl.pallas_call(functools.partial(mm_kernel, nt=nt), grid_spec=pltpu.Prefe...  79.6 us
    pallas_call x2, Pallas kernels, core_back(): pl.pallas_call(core_back_kernel, grid=(STEPS,), in_specs=[lanes(ROWS, STE...  64 us
    dot_general x12, matrix products, dot_tn(): lax.dot_general(a, b, (((0,), (0,)), ((), ())), preferred_element_type=F32)  38.2 us
    ppermute x18, waiting for transfers between devices, pieces_of(): got.append(lax.ppermute(part, 'seq', plane_route(k, n)))  35.3 us
    pallas_call x2, Pallas kernels, gate_back(): pl.pallas_call(gate_back_kernel, grid=(2, STEPS), in_specs=[first(ROWS),...  31.3 us
    ppermute x12, waiting for transfers between devices, copies_of(): lax.ppermute(value, 'seq', plane_route(k, n))  30.1 us
    pallas_call x2, Pallas kernels, mix(): pl.pallas_call(mix_kernel, grid=(STEPS,), in_specs=[whole((ROWS, ROWS)),...  29.2 us
  transfers between devices with their start and end apart: 61, of which 18 were waited for; matrix products, arithmetic and copies ran while one was open for 18% of the time, Pallas kernels for 32%

profile of v2, /device:TPU:0, one launch (start us, length us, event | category | flops | bytes accessed | tf_op | source)
XLA Modules:
  0.0 804.6 jit_solution(9162487087009323420)
XLA Ops:
  18.2 18.9 %collective-permute-done = f32[21392]{0:T(1024)S(1)} collective-permute-done((f32[21392]{0:T(1024)S(1)}, f32[21392]{0:T(1024)S(1)}, u32[]{:S(2)}, u32[]{:S(2)}) %collective-permute-start) | collective-permute-done | bytes 85600 | tf_op jit(solution)/shard_map/ppermute | solution.py:661
  43.8 13.8 %shard_map.194.x_ref.bc_ref.raw_ref.gate_ref = f32[256,6448]{1,0:T(8,128)} custom-call(s32[1]{0:T(128)} %bitcast.1.flag_ref, bf16[256,1536]{1,0:T(8,128)(2,1)S(1)} %fusion.16.x_ref, bf16[6448,1536]{1,0:T(8,128)(2,1)} %bitcast.152, bf16[6448,1536]{1,0:T(8,128)(2,1)} %collective-permute-done.1.other_ref), custom_call_target="tpu_custom_call" | custom-call | flops 5070913536 | bytes 19808256 | tf_op jit(solution)/shard_map/pallas_call | solution.py:157
  66.4 13.2 %shard_map.195 = (f32[256,3072]{1,0:T(8,128)}, f32[128,3072]{1,0:T(8,128)S(1)}, f32[8,3072]{1,0:T(8,128)S(1)}, bf16[256,384]{1,0:T(8,128)(2,1)S(1)}, bf16[256,38...) custom-call(f32[256,6448]{1,0:T(8,128)} %shard_map.194.x_ref.bc_ref., ...), custom_call_target="tpu_custom_call" | custom-call | flops 1000000000 | bytes 10485760 | tf_op jit(solution)/shard_map/pallas_call | solution.py:237
  80.4 39.1 %shard_map.196.car_ref = f32[128,3072]{1,0:T(8,128)S(1)} custom-call(f32[128,3072]{1,0:T(8,128)S(1)} %get-tuple-element.87.s_ref, f32[8,3072]{1,0:T(8,128)S(1)} %get-tuple-element.88.d_ref), custom_call_target="tpu_custom_call" | custom-call | tf_op jit(solution)/shard_map/pallas_call | solution.py:375
  124.5 14.4 %shard_map.197 = (f32[256,3072]{1,0:T(8,128)}, bf16[256,3072]{1,0:T(8,128)(2,1)S(1)}) custom-call(f32[256,256]{1,0:T(8,128)S(1)} %get-tuple-element.81.g_ref, bf16[256,384]{1,0:T(8,128)(2,1)S(1)} %get-tuple-element.82.step_ref, bf16[256,384]{1,0:T(8,128)(2,1)S(1)} %get-tuple-element.83.cum_ref, f32[128,256]{1,0:T(8,128)S(1)} %get-tuple-element.84.cumt_ref, ...), custom_call_target="tpu_custom_call" | custom-call | flops 3000000000 | bytes 14680064 | tf_op jit(solution)/shard_map/pallas_call | solution.py:455
  139.0 7.3 shard_map.198
  147.0 14.1 %shard_map.199.x_ref.bc_ref.raw_ref.gate_ref = f32[256,6448]{1,0:T(8,128)} custom-call(s32[1]{0:T(128)} %bitcast.16.flag_ref, bf16[256,1536]{1,0:T(8,128)(2,1)S(1)} %fusion.6.x_ref, bf16[6448,1536]{1,0:T(8,128)(2,1)} %bitcast.153, bf16[6448,1536]{1,0:T(8,128)(2,1)} %collective-permute-done.1.other_ref), custom_call_target="tpu_custom_call" | custom-call | flops 5070913536 | bytes 19808256 | tf_op jit(solution)/shard_map/pallas_call | solution.py:157
  187.1 13.2 %shard_map.200 = (f32[256,3072]{1,0:T(8,128)}, f32[128,3072]{1,0:T(8,128)S(1)}, f32[8,3072]{1,0:T(8,128)S(1)}, bf16[256,384]{1,0:T(8,128)(2,1)S(1)}, bf16[256,38...) custom-call(f32[256,6448]{1,0:T(8,128)} %shard_map.199.x_ref.bc_ref., ...), custom_call_target="tpu_custom_call" | custom-call | flops 1000000000 | bytes 10485760 | tf_op jit(solution)/shard_map/pallas_call | solution.py:237
  200.4 37.9 %shard_map.201.car_ref = f32[128,3072]{1,0:T(8,128)S(1)} custom-call(f32[128,3072]{1,0:T(8,128)S(1)} %get-tuple-element.100.s_ref, f32[8,3072]{1,0:T(8,128)S(1)} %get-tuple-element.101.d_ref), custom_call_target="tpu_custom_call" | custom-call | tf_op jit(solution)/shard_map/pallas_call | solution.py:375
  246.1 14.8 %shard_map.202 = (f32[256,3072]{1,0:T(8,128)}, bf16[256,3072]{1,0:T(8,128)(2,1)S(1)}) custom-call(f32[256,256]{1,0:T(8,128)S(1)} %get-tuple-element.92.g_ref, bf16[256,384]{1,0:T(8,128)(2,1)S(1)} %get-tuple-element.93.step_ref, bf16[256,384]{1,0:T(8,128)(2,1)S(1)} %get-tuple-element.94.cum_ref, f32[128,256]{1,0:T(8,128)S(1)} %get-tuple-element.95.cumt_ref, ...), custom_call_target="tpu_custom_call" | custom-call | flops 3000000000 | bytes 14680064 | tf_op jit(solution)/shard_map/pallas_call | solution.py:455
  262.1 15.5 %shard_map.205 = (f32[256,3072]{1,0:T(8,128)S(1)}, bf16[256,3072]{1,0:T(8,128)(2,1)S(1)}, f32[8,3072]{1,0:T(8,128)S(1)}, bf16[128,3072]{1,0:T(8,128)(2,1)S(1)}) custom-call(f32[256,3072]{1,0:T(8,128)} %copy-done, f32[256,3072]{1,0:T(8,128)} %get-tuple-element.103.y_ref, f32[256,6448]{1,0:T(8,128)} %shard_map.199.x_ref.bc_ref.raw_ref.gate_ref, ...), custom_call_target="tpu_custom_call" | custom-call | flops 1000000000 | bytes 16777216 | tf_op jit(solution)/shard_map/pallas_call | solution.py:518
  280.3 42.8 %shard_map.206.late_ref = bf16[128,3072]{1,0:T(8,128)(2,1)S(1)} custom-call(bf16[128,3072]{1,0:T(8,128)(2,1)S(1)} %get-tuple-element.111.s_ref, f32[8,3072]{1,0:T(8,128)S(1)} %get-tuple-element.101.d_ref), custom_call_target="tpu_custom_call" | custom-call | tf_op jit(solution)/shard_map/pallas_call | solution.py:375
  323.2 31.8 %shard_map.207 = (bf16[256,3072]{1,0:T(8,128)(2,1)S(1)}, bf16[256,256]{1,0:T(8,128)(2,1)S(1)}, f32[8,3072]{1,0:T(8,128)S(1)}, f32[8,256]{1,0:T(8,128)S(1)}, f32[...) custom-call(f32[256,6448]{1,0:T(8,128)} %shard_map.199.x_ref.bc_ref., ...), custom_call_target="tpu_custom_call" | custom-call | flops 8000000000 | bytes 14680064 | tf_op jit(solution)/shard_map/pallas_call | solution.py:632
  390.9 11.7 %shard_map.208 = f32[256,1536]{1,0:T(8,128)S(1)} custom-call(s32[1]{0:T(128)} %bitcast.16.flag_ref, bf16[256,6448]{1,0:T(8,128)(2,1)S(1)} %pad_maximum_fusion.1.x_ref, bf16[6448,1536]{1,0:T(8,128)(2,1)} %bitcast.154, bf16[6448,1536]{1,0:T(8,128)(2,1)} %collective-permute-done.1.other_ref), custom_call_target="tpu_custom_call" | custom-call | flops 5070913536 | bytes 19808256 | tf_op jit(solution)/shard_map/pallas_call | solution.py:157
  434.2 14.9 %collective-permute-done.30 = bf16[256,1536]{1,0:T(8,128)(2,1)S(1)} collective-permute-done((bf16[256,1536]{1,0:T(8,128)(2,1)S(1)}, bf16[256,1536]{1,0:T(8,128)(2,1)S(1)}, u32[]{:S(2)}, u32[]{:S(2)}) %collective-permute-start.30) | collective-permute-done | bytes 786464 | tf_op jit(solution)/shard_map/ppermute | solution.py:681
  449.2 14.6 %collective-permute-done.31 = bf16[256,1536]{1,0:T(8,128)(2,1)S(1)} collective-permute-done((bf16[256,1536]{1,0:T(8,128)(2,1)S(1)}, bf16[256,1536]{1,0:T(8,128)(2,1)S(1)}, u32[]{:S(2)}, u32[]{:S(2)}) %collective-permute-start.31) | collective-permute-done | bytes 786464 | tf_op jit(solution)/shard_map/ppermute | solution.py:681
  466.6 15.8 %shard_map.210 = (f32[256,3072]{1,0:T(8,128)S(1)}, bf16[256,3072]{1,0:T(8,128)(2,1)S(1)}, f32[8,3072]{1,0:T(8,128)S(1)}, bf16[128,3072]{1,0:T(8,128)(2,1)S(1)}) custom-call(f32[256,3072]{1,0:T(8,128)} %copy-done.1, f32[256,3072]{1,0:T(8,128)} %get-tuple-element.122.y_ref, f32[256,6448]{1,0:T(8,128)} %shard_map.194.x_ref.bc_ref.raw_ref.gate_ref, ...), custom_call_target="tpu_custom_call" | custom-call | flops 1000000000 | bytes 16777216 | tf_op jit(solution)/shard_map/pallas_call | solution.py:518
  491.7 30.9 %shard_map.211.late_ref = bf16[128,3072]{1,0:T(8,128)(2,1)S(1)} custom-call(bf16[128,3072]{1,0:T(8,128)(2,1)S(1)} %get-tuple-element.129.s_ref, f32[8,3072]{1,0:T(8,128)S(1)} %copy-done.32), custom_call_target="tpu_custom_call" | custom-call | tf_op jit(solution)/shard_map/pallas_call | solution.py:375
  583.2 32.2 %shard_map.212 = (bf16[256,3072]{1,0:T(8,128)(2,1)S(1)}, bf16[256,256]{1,0:T(8,128)(2,1)S(1)}, f32[8,3072]{1,0:T(8,128)S(1)}, f32[8,256]{1,0:T(8,128)S(1)}, f32[...) custom-call(f32[256,6448]{1,0:T(8,128)} %shard_map.194.x_ref.bc_ref., ...), custom_call_target="tpu_custom_call" | custom-call | flops 8000000000 | bytes 14680064 | tf_op jit(solution)/shard_map/pallas_call | solution.py:632
  626.6 11.5 %all-to-all-start = ((bf16[4,96,384]{2,1,0:T(8,128)(2,1)}), bf16[4,96,384]{2,1,0:T(8,128)(2,1)S(1)}, u32[]{:S(2)}, u32[]{:S(2)}) async-start(bf16[4,96,384]{2,1,0:T(8,128)(2,1)} %bitcast.177), calls=%async_computation.2 | async-start | bytes 589824 | tf_op jit(solution)/shard_map/all_to_all | solution.py:726
  638.1 26.0 %reduce-scatter.5.cloned.1.call-done = bf16[1,384,1216]{2,1,0:T(8,128)(2,1)} async-done(((bf16[4,384,1216]{2,1,0:T(8,128)(2,1)}), bf16[1,384,1216]{2,1,0:T(8,128)(2,1)}) %reduce-scatter.5.cloned.1.call-update) | async-done | bytes 933904 | tf_op jit(solution)/shard_map/reduce_scatter | solution.py:707
  678.4 9.7 %collective-permute-done.48 = bf16[256,896]{1,0:T(8,128)(2,1)S(1)} collective-permute-done((bf16[256,896]{1,0:T(8,128)(2,1)S(1)}, bf16[256,896]{1,0:T(8,128)(2,1)S(1)}, u32[]{:S(2)}, u32[]{:S(2)}) %collective-permute-start.48) | collective-permute-done | bytes 458784 | tf_op jit(solution)/shard_map/ppermute | solution.py:690
  688.1 8.3 %collective-permute-done.47 = bf16[256,896]{1,0:T(8,128)(2,1)S(1)} collective-permute-done((bf16[256,896]{1,0:T(8,128)(2,1)S(1)}, bf16[256,896]{1,0:T(8,128)(2,1)S(1)}, u32[]{:S(2)}, u32[]{:S(2)}) %collective-permute-start.47) | collective-permute-done | bytes 458784 | tf_op jit(solution)/shard_map/ppermute | solution.py:690
  701.3 11.7 %shard_map.213 = f32[256,1536]{1,0:T(8,128)S(1)} custom-call(s32[1]{0:T(128)} %bitcast.1.flag_ref, bf16[256,6448]{1,0:T(8,128)(2,1)S(1)} %pad_maximum_fusion.2.x_ref, bf16[6448,1536]{1,0:T(8,128)(2,1)} %bitcast.155, bf16[6448,1536]{1,0:T(8,128)(2,1)} %collective-permute-done.1.other_ref), custom_call_target="tpu_custom_call" | custom-call | flops 5070913536 | bytes 19808256 | tf_op jit(solution)/shard_map/pallas_call | solution.py:157
  (568 shorter events, 324.2 us)
Async XLA Ops:
  7.2 617.7 %reduce-scatter.11.cloned.1.call-start = ((), (), s32[]{:S(2)}) async-start(), calls=%async_computation.11 | async-start | bytes 1474560 | tf_op jit(solution)/shard_map/reduce_scatter | solution.py:707
  7.2 36.6 %collective-permute-start.1 = (bf16[6448,1536]{1,0:T(8,128)(2,1)}, bf16[6448,1536]{1,0:T(8,128)(2,1)}, u32[]{:S(2)}, u32[]{:S(2)}) collective-permute-start(bf16[6448,1536]{1,0:T(8,128)(2,1)} %bitcast.151), channel_id=1, source_target_pairs={{0,16},{16,0},{1,17},{17,1},{2,18},{18,2},{3,19},{19,3},{4,20},{20... | collective-permute-start | bytes 59424776 | tf_op jit(solution)/shard_map/ppermute | solution.py:661
  7.8 131.3 %collective-permute-start.6 = (bf16[3072,1536]{1,0:T(8,128)(2,1)}, bf16[3072,1536]{1,0:T(8,128)(2,1)}, u32[]{:S(2)}, u32[]{:S(2)}) collective-permute-start(bf16[3072,1536]{1,0:T(8,128)(2,1)} %bitcast.156), channel_id=1, source_target_pairs={{0,16},{16,0},{1,17},{17,1},{2,18},{18,2},{3,19},{19,3},{4,20},{20... | collective-permute-start | bytes 28311560 | tf_op jit(solution)/shard_map/ppermute | solution.py:661
  9.0 48.6 %collective-permute-start.2 = (bf16[256,1536]{1,0:T(8,128)(2,1)S(1)}, bf16[256,1536]{1,0:T(8,128)(2,1)}, u32[]{:S(2)}, u32[]{:S(2)}) collective-permute-start(bf16[256,1536]{1,0:T(8,128)(2,1)S(1)} %dynamic-slice_bitcast_fusion.x_ref), channel_id=1, source_target_pairs={{0,1},{1,2},{2,3},{3,0},{4,5},{5,6},{6,7},{7,4},{8,9},{9,10},{10,1... | collective-permute-start | bytes 2359304 | tf_op jit(solution)/shard_map/ppermute | solution.py:681
  12.0 45.6 %collective-permute-start.3 = (bf16[256,1536]{1,0:T(8,128)(2,1)S(1)}, bf16[256,1536]{1,0:T(8,128)(2,1)}, u32[]{:S(2)}, u32[]{:S(2)}) collective-permute-start(bf16[256,1536]{1,0:T(8,128)(2,1)S(1)} %dynamic-slice_bitcast_fusion.x_ref), channel_id=1, source_target_pairs={{0,2},{1,3},{2,0},{3,1},{4,6},{5,7},{6,4},{7,5},{8,10},{9,11},{10,... | collective-permute-start | bytes 2359304 | tf_op jit(solution)/shard_map/ppermute | solution.py:681
  119.5 41.7 %collective-permute-start.7 = (bf16[256,1536]{1,0:T(8,128)(2,1)S(1)}, bf16[256,1536]{1,0:T(8,128)(2,1)S(1)}, u32[]{:S(2)}, u32[]{:S(2)}) collective-permute-start(bf16[256,1536]{1,0:T(8,128)(2,1)S(1)} %fusion.16.x_ref), channel_id=1, source_target_pairs={{0,1},{1,2},{2,3},{3,0},{4,5},{5,6},{6,7},{7,4},{8,9},{9,10},{10,1... | collective-permute-start | bytes 2359304 | tf_op jit(solution)/shard_map/ppermute | solution.py:681
  122.5 38.7 %collective-permute-start.8 = (bf16[256,1536]{1,0:T(8,128)(2,1)S(1)}, bf16[256,1536]{1,0:T(8,128)(2,1)S(1)}, u32[]{:S(2)}, u32[]{:S(2)}) collective-permute-start(bf16[256,1536]{1,0:T(8,128)(2,1)S(1)} %fusion.16.x_ref), channel_id=1, source_target_pairs={{0,2},{1,3},{2,0},{3,1},{4,6},{5,7},{6,4},{7,5},{8,10},{9,11},{10,... | collective-permute-start | bytes 2359304 | tf_op jit(solution)/shard_map/ppermute | solution.py:681
  122.5 38.7 %collective-permute-start.9 = (bf16[256,1536]{1,0:T(8,128)(2,1)S(1)}, bf16[256,1536]{1,0:T(8,128)(2,1)S(1)}, u32[]{:S(2)}, u32[]{:S(2)}) collective-permute-start(bf16[256,1536]{1,0:T(8,128)(2,1)S(1)} %fusion.16.x_ref), channel_id=1, source_target_pairs={{0,3},{1,0},{2,1},{3,2},{4,7},{5,4},{6,5},{7,6},{8,11},{9,8},{10,9... | collective-permute-start | bytes 2359304 | tf_op jit(solution)/shard_map/ppermute | solution.py:681
  178.3 22.0 %collective-permute-start.11 = (bf16[256,768]{0,1:T(8,128)(2,1)S(1)}, bf16[256,768]{0,1:T(8,128)(2,1)S(1)}, u32[]{:S(2)}, u32[]{:S(2)}) collective-permute-start(bf16[256,768]{0,1:T(8,128)(2,1)S(1)} %get-tuple-element.183), channel_id=1, source_target_pairs={{0,1},{1,2},{2,3},{3,0},{4,5},{5,6},{6,7},{7,4},{8,9},{9,10},{10,1... | collective-permute-start | bytes 1179656 | tf_op jit(solution)/shard_map/ppermute | solution.py:690
  238.3 42.0 %collective-permute-start.15 = (bf16[256,1536]{1,0:T(8,128)(2,1)S(1)}, bf16[256,1536]{1,0:T(8,128)(2,1)S(1)}, u32[]{:S(2)}, u32[]{:S(2)}) collective-permute-start(bf16[256,1536]{1,0:T(8,128)(2,1)S(1)} %copy-done.3), channel_id=1, source_target_pairs={{0,1},{1,2},{2,3},{3,0},{4,5},{5,6},{6,7},{7,4},{8,9},{9,10},{10,1... | collective-permute-start | bytes 2359304 | tf_op jit(solution)/shard_map/ppermute | solution.py:681
  244.3 35.9 %collective-permute-start.16 = (bf16[256,1536]{1,0:T(8,128)(2,1)S(1)}, bf16[256,1536]{1,0:T(8,128)(2,1)}, u32[]{:S(2)}, u32[]{:S(2)}) collective-permute-start(bf16[256,1536]{1,0:T(8,128)(2,1)S(1)} %copy-done.3), channel_id=1, source_target_pairs={{0,2},{1,3},{2,0},{3,1},{4,6},{5,7},{6,4},{7,5},{8,10},{9,11},{10,... | collective-permute-start | bytes 2359304 | tf_op jit(solution)/shard_map/ppermute | solution.py:681
  244.3 35.9 %collective-permute-start.17 = (bf16[256,1536]{1,0:T(8,128)(2,1)S(1)}, bf16[256,1536]{1,0:T(8,128)(2,1)}, u32[]{:S(2)}, u32[]{:S(2)}) collective-permute-start(bf16[256,1536]{1,0:T(8,128)(2,1)S(1)} %copy-done.3), channel_id=1, source_target_pairs={{0,3},{1,0},{2,1},{3,2},{4,7},{5,4},{6,5},{7,6},{8,11},{9,8},{10,9... | collective-permute-start | bytes 2359304 | tf_op jit(solution)/shard_map/ppermute | solution.py:681
  419.0 63.4 %collective-permute-start.25 = (bf16[1536,384]{1,0:T(8,128)(2,1)}, bf16[1536,384]{1,0:T(8,128)(2,1)}, u32[]{:S(2)}, u32[]{:S(2)}) collective-permute-start(bf16[1536,384]{1,0:T(8,128)(2,1)} %convolution_convert_fusion.3), channel_id=1, source_target_pairs={{0,16},{16,0},{1,17},{17,1},{2,18},{18,2},{3,19},{19,3},{4,20},{20... | collective-permute-start | bytes 3538952 | tf_op jit(solution)/shard_map/ppermute | solution.py:661
  428.9 34.9 %collective-permute-start.31 = (bf16[256,1536]{1,0:T(8,128)(2,1)S(1)}, bf16[256,1536]{1,0:T(8,128)(2,1)S(1)}, u32[]{:S(2)}, u32[]{:S(2)}) collective-permute-start(bf16[256,1536]{1,0:T(8,128)(2,1)S(1)} %get-tuple-element.130.x_ref), channel_id=1, source_target_pairs={{0,2},{1,3},{2,0},{3,1},{4,6},{5,7},{6,4},{7,5},{8,10},{9,11},{10,... | collective-permute-start | bytes 2359304 | tf_op jit(solution)/shard_map/ppermute | solution.py:681
  429.0 35.0 %collective-permute-start.32 = (bf16[256,1536]{1,0:T(8,128)(2,1)S(1)}, bf16[256,1536]{1,0:T(8,128)(2,1)S(1)}, u32[]{:S(2)}, u32[]{:S(2)}) collective-permute-start(bf16[256,1536]{1,0:T(8,128)(2,1)S(1)} %get-tuple-element.130.x_ref), channel_id=1, source_target_pairs={{0,3},{1,0},{2,1},{3,2},{4,7},{5,4},{6,5},{7,6},{8,11},{9,8},{10,9... | collective-permute-start | bytes 2359304 | tf_op jit(solution)/shard_map/ppermute | solution.py:681
  434.1 53.4 %collective-permute-start.29 = (bf16[1536,448]{0,1:T(8,128)(2,1)}, bf16[1536,448]{0,1:T(8,128)(2,1)}, u32[]{:S(2)}, u32[]{:S(2)}) collective-permute-start(bf16[1536,448]{0,1:T(8,128)(2,1)} %convolution_convert_fusion.1), channel_id=1, source_target_pairs={{0,16},{16,0},{1,17},{17,1},{2,18},{18,2},{3,19},{19,3},{4,20},{20... | collective-permute-start | bytes 4128776 | tf_op jit(solution)/shard_map/ppermute | solution.py:661
  466.6 61.0 %collective-permute-start.51 = (bf16[768,768]{1,0:T(8,128)(2,1)}, bf16[768,768]{1,0:T(8,128)(2,1)}, u32[]{:S(2)}, u32[]{:S(2)}) collective-permute-start(bf16[768,768]{1,0:T(8,128)(2,1)} %fusion.35), channel_id=1, source_target_pairs={{0,16},{16,0},{1,17},{17,1},{2,18},{18,2},{3,19},{19,3},{4,20},{20... | collective-permute-start | bytes 3538952 | tf_op jit(solution)/shard_map/ppermute | solution.py:661
  531.5 95.1 %reduce-scatter.7.cloned.1.call-start = ((), (), s32[]{:S(2)}) async-start(), calls=%async_computation.9 | async-start | bytes 1474560 | tf_op jit(solution)/shard_map/reduce_scatter | solution.py:707
  550.9 113.3 %reduce-scatter.5.cloned.1.call-start = ((), (), s32[]{:S(2)}) async-start(), calls=%async_computation.8 | async-start | bytes 4915200 | tf_op jit(solution)/shard_map/reduce_scatter | solution.py:707
  626.6 104.7 %all-to-all-start = ((bf16[4,96,384]{2,1,0:T(8,128)(2,1)}), bf16[4,96,384]{2,1,0:T(8,128)(2,1)S(1)}, u32[]{:S(2)}, u32[]{:S(2)}) async-start(bf16[4,96,384]{2,1,0:T(8,128)(2,1)} %bitcast.177), calls=%async_computation.2 | async-start | bytes 589824 | tf_op jit(solution)/shard_map/all_to_all | solution.py:726
  638.1 137.7 %reduce-scatter.9.cloned.1.call-start = ((), (), s32[]{:S(2)}) async-start(), calls=%async_computation.10 | async-start | bytes 1966080 | tf_op jit(solution)/shard_map/reduce_scatter | solution.py:707
  739.0 49.4 %collective-permute-start.38 = (f32[256,1536]{1,0:T(8,128)}, f32[256,1536]{1,0:T(8,128)}, u32[]{:S(2)}, u32[]{:S(2)}) collective-permute-start(f32[256,1536]{1,0:T(8,128)} %fusion.48), channel_id=1, source_target_pairs={{0,16},{16,0},{1,17},{17,1},{2,18},{18,2},{3,19},{19,3},{4,20},{20... | collective-permute-start | bytes 4718600 | tf_op jit(solution)/shard_map/ppermute | solution.py:661
  742.5 33.2 %all-to-all-start.3 = ((bf16[4,96,448]{2,1,0:T(8,128)(2,1)}), bf16[4,96,448]{2,1,0:T(8,128)(2,1)S(1)}, u32[]{:S(2)}, u32[]{:S(2)}) async-start(bf16[4,96,448]{2,1,0:T(8,128)(2,1)} %bitcast.167), calls=%async_computation.6 | async-start | bytes 786432 | tf_op jit(solution)/shard_map/all_to_all | solution.py:726
  747.7 32.8 %collective-permute-start.45 = (bf16[96,4,384]{2,0,1:T(8,128)(2,1)}, bf16[96,4,384]{2,0,1:T(8,128)(2,1)}, u32[]{:S(2)}, u32[]{:S(2)}) collective-permute-start(bf16[96,4,384]{2,0,1:T(8,128)(2,1)} %select_bitcast_fusion.7), channel_id=1, source_target_pairs={{0,16},{16,0},{1,17},{17,1},{2,18},{18,2},{3,19},{19,3},{4,20},{20... | collective-permute-start | bytes 884744 | tf_op jit(solution)/shard_map/ppermute | solution.py:661
  (177 other events, 2553.4 us)
Sparse Core Ops, SparseCore 0:
  531.7 26.2 reduce-scatter.10
  560.3 27.8 reduce-scatter.6
  590.5 73.6 reduce-scatter.4
  727.7 38.5 reduce-scatter.8

commit v3 on v2

--- a/solution.py
+++ b/solution.py
@@ -657,6 +657,103 @@
     )
 
 
+def settle_kernel(
+    n, ga0, re0, ga1, re1, ow0, ow1, a0, a1, d0, d1, gin_ref, gout_ref, acts_ref, grads_ref,
+    gate_in, rest_in, out_in, send_g, recv_g, send_r, recv_r, send_o, recv_o, send_x, recv_x, keep_x,
+):
+    core = lax.axis_index("section")
+    q = lax.axis_index("seq")
+    spot = lax.rem(q, PLANE)
+    base = q - spot
+    rows = gin_ref.shape[0]
+    barrier = pltpu.get_barrier_semaphore()
+    for k in range(PLANE):
+        for flip in range(2):
+            if k or flip:
+                to = (core ^ flip, base + lax.rem(spot + k, PLANE))
+                pl.semaphore_signal(barrier, inc=1, device_id=to, device_id_type=MESH)
+    pl.semaphore_wait(barrier, 2 * PLANE - 1)
+
+    def run(layer, gate, rest, outw, act, grad, away_act, away_grad, away_outw, away_gate, away_rest):
+        copies = []
+
+        def send(src, dst, sems, at, to):
+            copy = pltpu.make_async_remote_copy(
+                src_ref=src, dst_ref=dst, send_sem=sems[0].at[at], recv_sem=sems[1].at[at],
+                device_id=to, device_id_type=MESH,
+            )
+            copy.start()
+            copies.append(copy)
+
+        across = (1 - layer, q)
+        kept = []
+        for at, (own, away, dst) in enumerate(((grad, away_grad, grads_ref), (act, away_act, acts_ref))):
+            send(away, dst.at[layer], (send_x, recv_x), at, across)
+            kept.append(pltpu.make_async_copy(own, dst.at[layer], keep_x.at[at]))
+            kept[-1].start()
+        send(away_outw, out_in, (send_o, recv_o), 0, across)
+        for k in range(PLANE):
+            peer = lax.rem(spot + k, PLANE)
+            block = pl.ds(pl.multiple_of(peer * rows, rows), rows)
+            for flip in range(2):
+                if not (k or flip):
+                    continue
+                at = 2 * k + flip
+                to = (1 - layer if flip else layer, base + peer)
+                slot = 2 * spot + layer
+                send((away_gate if flip else gate).at[block], gate_in.at[slot], (send_g, recv_g), at, to)
+                send((away_rest if flip else rest).at[block], rest_in.at[slot], (send_r, recv_r), at, to)
+        mine = pl.ds(pl.multiple_of(spot * rows, rows), rows)
+        gate_in[2 * spot + layer] = gate[mine, :]
+        rest_in[2 * spot + layer] = rest[mine, :]
+        half = D // 2
+        gout_ref[:, layer * half : layer * half + half] = outw[...].astype(F32)
+        for copy in copies + kept:
+            copy.wait()
+        gout_ref[:, (1 - layer) * half : (1 - layer) * half + half] = out_in[...].astype(F32)
+
+    @pl.when(core == 0)
+    def _():
+        run(0, ga0, re0, ow0, a0, d0, a1, d1, ow1, ga1, re1)
+
+    @pl.when(core == 1)
+    def _():
+        run(1, ga1, re1, ow1, a1, d1, a0, d0, ow0, ga0, re0)
+
+    for p in range(2 * PLANE):
+        wide = gate_in.shape[2]
+        gin_ref[:, p * wide : p * wide + wide] = gate_in[p].astype(F32)
+        wide = rest_in.shape[2]
+        at = INNER + p * wide
+        width = min(wide, PROJ - at)
+        gin_ref[:, at : at + width] = rest_in[p].astype(F32)[:, :width]
+
+
+def settle(gates, rests, outs, acts, grads, n):
+    vmem = pl.BlockSpec(memory_space=pltpu.VMEM)
+    anywhere = pl.BlockSpec(memory_space=pl.ANY)
+    dma = pltpu.SemaphoreType.DMA
+    rows = D // n
+    eight = 2 * PLANE
+    return pl.pallas_call(
+        functools.partial(settle_kernel, n),
+        out_shape=[
+            sds(rows, PROJ, F32), sds(INNER // n, D, F32),
+            jax.ShapeDtypeStruct((2, ROWS, D), BF16), jax.ShapeDtypeStruct((2, ROWS, D), F32),
+        ],
+        in_specs=[vmem] * 6 + [anywhere] * 4,
+        out_specs=[vmem, vmem, anywhere, anywhere],
+        scratch_shapes=[
+            pltpu.VMEM((eight, rows, gates[0].shape[1]), BF16),
+            pltpu.VMEM((eight, rows, rests[0].shape[1]), BF16),
+            pltpu.VMEM((INNER // n, D // 2), BF16),
+            dma((eight,)), dma((eight,)), dma((eight,)), dma((eight,)),
+            dma((1,)), dma((1,)), dma((2,)), dma((2,)), dma((2,)),
+        ],
+        compiler_params=pltpu.CompilerParams(collective_id=3, has_side_effects=True, vmem_limit_bytes=40 * MIB),
+    )(gates[0], rests[0], gates[1], rests[1], outs[0], outs[1], acts[0], acts[1], grads[0], grads[1])
+
+
 def swap(value):
     return lax.ppermute(value, "section", [(0, 1), (1, 0)])
 
@@ -675,6 +772,10 @@
 
 def tied(value, *others):
     return lax.optimization_barrier((value, *others))[0]
+
+
+def tied_list(values, other):
+    return list(lax.optimization_barrier((*values, other))[:-1])
 
 
 def copies_of(value, n):
@@ -700,30 +801,9 @@
     return (mine + swap(away).astype(F32)).astype(BF16)
 
 
-def plane_rows(partials, n):
-    planes = n // PLANE
-    columns = [[p + PLANE * z for z in range(planes)] for p in range(PLANE)]
-    joined = jnp.concatenate([part.reshape(planes, D // planes, -1) for part in partials], axis=2)
-    joined = lax.psum_scatter(joined, "seq", scatter_dimension=0, axis_index_groups=columns)
-    return jnp.split(joined, [sum(p.shape[1] for p in partials[:k]) for k in range(1, len(partials))], axis=1)
-
-
-def stacked_halves(value, n):
-    planes = n // PLANE
-    value = value.reshape(planes, -1, D // 2)
-    return jnp.concatenate([value[:, :, : D // 4], value[:, :, D // 4 :]], axis=1).reshape(D, D // 4)
-
-
-def unstacked_halves(value):
-    rows = value.shape[0] // 2
-    return jnp.concatenate([value[:rows], value[rows:]], axis=1)
-
-
-def by_row(value, n):
-    in_plane = [[PLANE * z + p for p in range(PLANE)] for z in range(n // PLANE)]
-    rows = value.shape[0] // PLANE
-    value = value.reshape(PLANE, rows, value.shape[1])
-    return lax.all_to_all(value, "seq", 0, 0, axis_index_groups=in_plane).transpose(1, 0, 2)
+def plane_rows(partial, n):
+    columns = [[p + PLANE * z for z in range(n // PLANE)] for p in range(PLANE)]
+    return lax.psum_scatter(partial, "seq", scatter_dimension=0, axis_index_groups=columns, tiled=True)
 
 
 SIZES = [D, CONVD * CONV, CONVD, HEADS, HEADS, HEADS, INNER]
@@ -870,46 +950,36 @@
     gates_1 = pieces_of(tied(d_gate_1, late_1), n)
     gateds_1 = pieces_of(by_owner(tied(gated_1, late_1)), n)
     back_1 = core_side(1, proj_1, halo_1, parts_1, y_1, dy_1, carried_1, late_1)
-    back_1 = [tied(back_1[0], *gates_1, *gateds_1)] + list(back_1[1:])
+    outw_1 = partial_grad(tied_list(gateds_1, back_1[0]), lows_1)
+    outw_1 = plane_rows(outw_1, n)
+    gatew_1 = partial_grad(normeds_1, tied_list(gates_1, back_1[0]))
     d_conv_1, d_raw_1 = conv_side(1, back_1)
     rests_1 = pieces_of(padded(d_conv_1, d_raw_1), n)
-    d_1, ng_1 = norm_side(1, h_1, d_out_1.astype(F32), jnp.concatenate([d_gate_1, d_conv_1, d_raw_1], axis=1))
+    d_proj_1 = jnp.concatenate([tied(d_gate_1, gatew_1), d_conv_1, d_raw_1], axis=1)
+    gatew_1 = plane_rows(gatew_1, n)
+    d_1, ng_1 = norm_side(1, h_1, d_out_1.astype(F32), d_proj_1)
 
     d_out_0 = d_1.astype(BF16)
     lows_0 = copies_of(tied(d_out_0, *rests_1), n)
     dy_0, d_gate_0, gain_0, d_carried_0 = gate_side(0, d_out_0, y_0, proj_0, parts_0)
-    outw_1 = stacked_halves(partial_grad(gateds_1, lows_1), n)
-    grads_1 = [outw_1, partial_grad(normeds_1, gates_1), partial_grad(normeds_1, rests_1)]
-    late_0 = exchange(tied(d_carried_0, *grads_1), parts_0[2], n, True)
-    outw_1, gatew_1, restw_1 = plane_rows(grads_1, n)
+    restw_1 = partial_grad(normeds_1, rests_1)
+    late_0 = exchange(tied(d_carried_0, restw_1), parts_0[2], n, True)
+    restw_1 = plane_rows(restw_1, n)
     gates_0 = pieces_of(tied(d_gate_0, late_0, *lows_0), n)
-    outw_0 = stacked_halves(partial_grad(gateds_0, lows_0), n)
-    back_0 = core_side(0, proj_0, halo_0, parts_0, y_0, dy_0, carried_0, tied(late_0, *lows_0, outw_0))
-    (outw_0,) = plane_rows([outw_0], n)
-    back_0 = [tied(back_0[0], *gates_0, outw_1, gatew_1, restw_1)] + list(back_0[1:])
+    outw_0 = partial_grad(gateds_0, tied_list(lows_0, late_0))
+    back_0 = core_side(0, proj_0, halo_0, parts_0, y_0, dy_0, carried_0, tied(late_0, outw_0))
+    outw_0 = plane_rows(outw_0, n)
+    gatew_0 = partial_grad(normeds_0, tied_list(gates_0, back_0[0]))
     d_conv_0, d_raw_0 = conv_side(0, back_0)
     rests_0 = pieces_of(padded(d_conv_0, d_raw_0), n)
-    (gatew_0,) = plane_rows([partial_grad(normeds_0, gates_0)], n)
-    d_0, ng_0 = norm_side(0, h_0, d_out_0.astype(F32), jnp.concatenate([d_gate_0, d_conv_0, d_raw_0], axis=1))
-    (restw_0,) = plane_rows([partial_grad(normeds_0, rests_0)], n)
-
-    def joined(early, late):
-        own = jnp.where(first, early, late)
-        other = swap(jnp.where(first, late, early))
-        return jnp.where(first, own, other), jnp.where(first, other, own)
-
-    def both(early, late):
-        return jnp.stack(joined(early, late))[None]
-
-    acts = both(act_0, act_1)
-    input_grads = both(d_0, d_1)
-    gate_w = jnp.stack(joined(by_row(gatew_0, n), by_row(gatew_1, n)), axis=2)
-    rest_w = jnp.stack(joined(by_row(restw_0, n), by_row(restw_1, n)), axis=2)
-    rows = D // n
-    g_in = jnp.concatenate(
-        [gate_w.reshape(rows, INNER), rest_w.reshape(rows, REST)[:, : PROJ - INNER]], axis=1
-    ).astype(F32)
-    g_out = jnp.concatenate(joined(unstacked_halves(outw_0), unstacked_halves(outw_1)), axis=1).astype(F32)
+    d_proj_0 = jnp.concatenate([tied(d_gate_0, gatew_0), d_conv_0, d_raw_0], axis=1)
+    gatew_0 = plane_rows(gatew_0, n)
+    d_0, ng_0 = norm_side(0, h_0, d_out_0.astype(F32), d_proj_0)
+    restw_0 = plane_rows(partial_grad(normeds_0, rests_0), n)
+
+    g_in, g_out, acts, input_grads = settle(
+        (gatew_0, gatew_1), (restw_0, restw_1), (outw_0, outw_1), (act_0, act_1), (d_0, d_1), n
+    )
     small_0, small_1 = small_of(ng_0, back_0, gain_0), small_of(ng_1, back_1, gain_1)
     small = jnp.where(first, small_0, small_1) + swap(jnp.where(first, small_1, small_0))
     reach = 1
@@ -925,7 +995,7 @@
     conv_rows = CONVD // n
     conv_w = lax.dynamic_slice_in_dim(conv_w.reshape(CONV, CONVD), place * conv_rows, conv_rows, 1).T
     return (
-        acts, input_grads, share(norm_g), g_in[None], conv_w[None], share(conv_b),
+        acts[None], input_grads[None], share(norm_g), g_in[None], conv_w[None], share(conv_b),
         dt_b[None], a_lg[None], skip_w[None], share(gate_g), g_out[None],
     )
 

time: 814 us -> 761 us (0.935)
  waiting for transfers between devices: 129 us -> 86.5 us
  starting transfers between devices: 94.4 us -> 68.6 us
  other arithmetic: 50.4 us -> 26 us
  Pallas kernels: 381 us -> 399 us
  local copies, waits for them, and re-layouts: 95.2 us -> 109 us
    unnamed x291 -> x302, local copies, waits for them, and re-layouts: 21.1 us -> 54 us
    reduce_scatter x4 -> x6, waiting for transfers between devices: 26.1 us -> 1.7 us  [plane_rows(): lax.psum_scatter(partial, 'seq', scatter_dimension=0, axis_index_groups=c...]
    all_to_all x4 -> x0, starting transfers between devices: 23.8 us -> none  [by_row(): lax.all_to_all(value, 'seq', 0, 0, axis_index_groups=in_plane)]
    ppermute x12, waiting for transfers between devices: 30.1 us -> 10.7 us  [copies_of(): lax.ppermute(value, 'seq', plane_route(k, n))]
    pallas_call x0 -> x1, Pallas kernels: none -> 19 us  [settle(): pl.pallas_call(functools.partial(settle_kernel, n), out_shape=[sds(rows,...]
    ppermute x4, waiting for transfers between devices: 11.8 us -> 25.4 us  [per_device(): lax.ppermute(small, 'seq', [(i, i ^ reach) for i in range(n)])]
    select_n x5 -> x0, other arithmetic: 8.36 us -> none  [joined(): other = swap(jnp.where(first, late, early))]
    ppermute x15 -> x10, waiting for transfers between devices: 18.9 us -> 19.8 us  [swap(): return lax.ppermute(value, 'section', [(0, 1), (1, 0)])]
  transfers between devices with their start and end apart: 61 -> 54, of which waited for: 18 -> 15; matrix products, arithmetic and copies ran while one was open for 18% -> 18% of each run, Pallas kernels for 32% -> 29%
where the time goes in v3:
time: 761 us; the launch traced here: 751 us
  Pallas kernels  399 us (52%)
  local copies, waits for them, and re-layouts  109 us (14%)
  waiting for transfers between devices  86.5 us (11%)
  starting transfers between devices  68.6 us (9%)
  matrix products  45.1 us (6%)
  other arithmetic  26 us (3%)
  between operations  16.4 us (2%)
    pallas_call x4, Pallas kernels, exchange(): pl.pallas_call(functools.partial(exchange_kernel, n, rev), out_shape=sds(...  149 us
    pallas_call x8, Pallas kernels, mm(): pl.pallas_call(functools.partial(mm_kernel, nt=nt), grid_spec=pltpu.Prefe...  80.2 us
    pallas_call x2, Pallas kernels, core_back(): pl.pallas_call(core_back_kernel, grid=(STEPS,), in_specs=[lanes(ROWS, STE...  64 us
    unnamed x302, local copies, waits for them, and re-layouts  54 us
    dot_general x12, matrix products, dot_tn(): lax.dot_general(a, b, (((0,), (0,)), ((), ())), preferred_element_type=F32)  45.1 us
    pallas_call x2, Pallas kernels, gate_back(): pl.pallas_call(gate_back_kernel, grid=(2, STEPS), in_specs=[first(ROWS),...  31.8 us
    ppermute x18, starting transfers between devices, pieces_of(): got.append(lax.ppermute(part, 'seq', plane_route(k, n)))  29.4 us
    pallas_call x2, Pallas kernels, mix(): pl.pallas_call(mix_kernel, grid=(STEPS,), in_specs=[whole((ROWS, ROWS)),...  28.7 us
  transfers between devices with their start and end apart: 54, of which 15 were waited for; matrix products, arithmetic and copies ran while one was open for 18% of the time, Pallas kernels for 29%

profile of v3, /device:TPU:0, one launch (start us, length us, event | category | flops | bytes accessed | tf_op | source)
XLA Modules:
  0.0 750.9 jit_solution(4442397530521406774)
XLA Ops:
  18.3 18.8 %collective-permute-done = f32[21392]{0:T(1024)S(1)} collective-permute-done((f32[21392]{0:T(1024)S(1)}, f32[21392]{0:T(1024)S(1)}, u32[]{:S(2)}, u32[]{:S(2)}) %collective-permute-start) | collective-permute-done | bytes 85600 | tf_op jit(solution)/shard_map/ppermute | solution.py:758
  47.7 10.3 %collective-permute-done.4 = bf16[256,1536]{1,0:T(8,128)(2,1)} collective-permute-done((bf16[256,1536]{1,0:T(8,128)(2,1)S(1)}, bf16[256,1536]{1,0:T(8,128)(2,1)}, u32[]{:S(2)}, u32[]{:S(2)}) %collective-permute-start.4) | collective-permute-done | bytes 786464 | tf_op jit(solution)/shard_map/ppermute | solution.py:782
  61.1 13.8 %shard_map.194.x_ref.bc_ref.raw_ref.gate_ref = f32[256,6448]{1,0:T(8,128)} custom-call(s32[1]{0:T(128)} %bitcast.8.flag_ref, bf16[256,1536]{1,0:T(8,128)(2,1)S(1)} %fusion.16.x_ref, bf16[6448,1536]{1,0:T(8,128)(2,1)} %bitcast.94, bf16[6448,1536]{1,0:T(8,128)(2,1)} %collective-permute-done.1.other_ref), custom_call_target="tpu_custom_call" | custom-call | flops 5070913536 | bytes 19808256 | tf_op jit(solution)/shard_map/pallas_call | solution.py:157
  88.9 13.2 %shard_map.195 = (f32[256,3072]{1,0:T(8,128)}, f32[128,3072]{1,0:T(8,128)S(1)}, f32[8,3072]{1,0:T(8,128)S(1)}, bf16[256,384]{1,0:T(8,128)(2,1)S(1)}, bf16[256,38...) custom-call(f32[256,6448]{1,0:T(8,128)} %shard_map.194.x_ref.bc_ref., ...), custom_call_target="tpu_custom_call" | custom-call | flops 1000000000 | bytes 10485760 | tf_op jit(solution)/shard_map/pallas_call | solution.py:237
  102.2 38.6 %shard_map.196.car_ref = f32[128,3072]{1,0:T(8,128)S(1)} custom-call(f32[128,3072]{1,0:T(8,128)S(1)} %get-tuple-element.101.s_ref, f32[8,3072]{1,0:T(8,128)S(1)} %get-tuple-element.102.d_ref), custom_call_target="tpu_custom_call" | custom-call | tf_op jit(solution)/shard_map/pallas_call | solution.py:375
  145.2 14.3 %shard_map.197 = (f32[256,3072]{1,0:T(8,128)}, bf16[256,3072]{1,0:T(8,128)(2,1)S(1)}) custom-call(f32[256,256]{1,0:T(8,128)S(1)} %get-tuple-element.104.g_ref, bf16[256,384]{1,0:T(8,128)(2,1)S(1)} %get-tuple-element.105.step_ref, bf16[256,384]{1,0:T(8,128)(2,1)S(1)} %get-tuple-element.106.cum_ref, f32[128,256]{1,0:T(8,128)S(1)} %get-tuple-element.107.cumt_ref, ...), custom_call_target="tpu_custom_call" | custom-call | flops 3000000000 | bytes 14680064 | tf_op jit(solution)/shard_map/pallas_call | solution.py:455
  168.2 14.1 %shard_map.200.x_ref.bc_ref.raw_ref.gate_ref = f32[256,6448]{1,0:T(8,128)} custom-call(s32[1]{0:T(128)} %bitcast.16.flag_ref, bf16[256,1536]{1,0:T(8,128)(2,1)S(1)} %fusion.6.x_ref, bf16[6448,1536]{1,0:T(8,128)(2,1)} %bitcast.95, bf16[6448,1536]{1,0:T(8,128)(2,1)} %collective-permute-done.1.other_ref), custom_call_target="tpu_custom_call" | custom-call | flops 5070913536 | bytes 19808256 | tf_op jit(solution)/shard_map/pallas_call | solution.py:157
  203.7 13.2 %shard_map.201 = (f32[256,3072]{1,0:T(8,128)}, f32[128,3072]{1,0:T(8,128)S(1)}, f32[8,3072]{1,0:T(8,128)S(1)}, bf16[256,384]{1,0:T(8,128)(2,1)S(1)}, bf16[256,38...) custom-call(f32[256,6448]{1,0:T(8,128)} %shard_map.200.x_ref.bc_ref., ...), custom_call_target="tpu_custom_call" | custom-call | flops 1000000000 | bytes 10485760 | tf_op jit(solution)/shard_map/pallas_call | solution.py:237
  217.8 38.7 %shard_map.202.car_ref = f32[128,3072]{1,0:T(8,128)S(1)} custom-call(f32[128,3072]{1,0:T(8,128)S(1)} %get-tuple-element.120.s_ref, f32[8,3072]{1,0:T(8,128)S(1)} %get-tuple-element.121.d_ref), custom_call_target="tpu_custom_call" | custom-call | tf_op jit(solution)/shard_map/pallas_call | solution.py:375
  262.2 14.4 %shard_map.203 = (f32[256,3072]{1,0:T(8,128)}, bf16[256,3072]{1,0:T(8,128)(2,1)S(1)}) custom-call(f32[256,256]{1,0:T(8,128)S(1)} %get-tuple-element.112.g_ref, bf16[256,384]{1,0:T(8,128)(2,1)S(1)} %get-tuple-element.113.step_ref, bf16[256,384]{1,0:T(8,128)(2,1)S(1)} %get-tuple-element.114.cum_ref, f32[128,256]{1,0:T(8,128)S(1)} %get-tuple-element.115.cumt_ref, ...), custom_call_target="tpu_custom_call" | custom-call | flops 3000000000 | bytes 14680064 | tf_op jit(solution)/shard_map/pallas_call | solution.py:455
  276.6 16.1 %shard_map.204 = (f32[256,3072]{1,0:T(8,128)S(1)}, bf16[256,3072]{1,0:T(8,128)(2,1)S(1)}, f32[8,3072]{1,0:T(8,128)S(1)}, bf16[128,3072]{1,0:T(8,128)(2,1)S(1)}) custom-call(f32[256,3072]{1,0:T(8,128)} %copy-done, f32[256,3072]{1,0:T(8,128)} %get-tuple-element.122.y_ref, f32[256,6448]{1,0:T(8,128)} %shard_map.200.x_ref.bc_ref.raw_ref.gate_ref, ...), custom_call_target="tpu_custom_call" | custom-call | flops 1000000000 | bytes 16777216 | tf_op jit(solution)/shard_map/pallas_call | solution.py:518
  294.4 7.3 shard_map.212
  303.1 43.3 %shard_map.205.late_ref = bf16[128,3072]{1,0:T(8,128)(2,1)S(1)} custom-call(bf16[128,3072]{1,0:T(8,128)(2,1)S(1)} %get-tuple-element.127.s_ref, f32[8,3072]{1,0:T(8,128)S(1)} %get-tuple-element.121.d_ref), custom_call_target="tpu_custom_call" | custom-call | tf_op jit(solution)/shard_map/pallas_call | solution.py:375
  346.4 32.1 %shard_map.206 = (bf16[256,3072]{1,0:T(8,128)(2,1)S(1)}, bf16[256,256]{1,0:T(8,128)(2,1)S(1)}, f32[8,3072]{1,0:T(8,128)S(1)}, f32[8,256]{1,0:T(8,128)S(1)}, f32[...) custom-call(f32[256,6448]{1,0:T(8,128)} %shard_map.200.x_ref.bc_ref., ...), custom_call_target="tpu_custom_call" | custom-call | flops 8000000000 | bytes 14680064 | tf_op jit(solution)/shard_map/pallas_call | solution.py:632
  435.9 12.0 %shard_map.207 = f32[256,1536]{1,0:T(8,128)S(1)} custom-call(s32[1]{0:T(128)} %bitcast.16.flag_ref, bf16[256,6448]{1,0:T(8,128)(2,1)S(1)} %pad_maximum_fusion.x_ref, bf16[6448,1536]{1,0:T(8,128)(2,1)} %bitcast.96, bf16[6448,1536]{1,0:T(8,128)(2,1)} %collective-permute-done.1.other_ref), custom_call_target="tpu_custom_call" | custom-call | flops 5070913536 | bytes 19808256 | tf_op jit(solution)/shard_map/pallas_call | solution.py:157
  469.3 15.7 %shard_map.209 = (f32[256,3072]{1,0:T(8,128)S(1)}, bf16[256,3072]{1,0:T(8,128)(2,1)S(1)}, f32[8,3072]{1,0:T(8,128)S(1)}, bf16[128,3072]{1,0:T(8,128)(2,1)S(1)}) custom-call(f32[256,3072]{1,0:T(8,128)} %copy-done.1, f32[256,3072]{1,0:T(8,128)} %get-tuple-element.144.y_ref, f32[256,6448]{1,0:T(8,128)} %shard_map.194.x_ref.bc_ref.raw_ref.gate_ref, ...), custom_call_target="tpu_custom_call" | custom-call | flops 1000000000 | bytes 16777216 | tf_op jit(solution)/shard_map/pallas_call | solution.py:518
  498.3 28.2 %shard_map.210.late_ref = bf16[128,3072]{1,0:T(8,128)(2,1)S(1)} custom-call(bf16[128,3072]{1,0:T(8,128)(2,1)S(1)} %copy-done.32, f32[8,3072]{1,0:T(8,128)S(1)} %copy-done.36), custom_call_target="tpu_custom_call" | custom-call | tf_op jit(solution)/shard_map/pallas_call | solution.py:375
  559.0 31.9 %shard_map.211 = (bf16[256,3072]{1,0:T(8,128)(2,1)S(1)}, bf16[256,256]{1,0:T(8,128)(2,1)S(1)}, f32[8,3072]{1,0:T(8,128)S(1)}, f32[8,256]{1,0:T(8,128)S(1)}, f32[...) custom-call(f32[256,6448]{1,0:T(8,128)} %shard_map.194.x_ref.bc_ref., ...), custom_call_target="tpu_custom_call" | custom-call | flops 8000000000 | bytes 14680064 | tf_op jit(solution)/shard_map/pallas_call | solution.py:632
  614.2 10.0 %collective-permute-done.37 = bf16[256,896]{1,0:T(8,128)(2,1)} collective-permute-done((bf16[256,896]{1,0:T(8,128)(2,1)}, bf16[256,896]{1,0:T(8,128)(2,1)}, u32[]{:S(2)}, u32[]{:S(2)}) %collective-permute-start.37) | collective-permute-done | bytes 458784 | tf_op jit(solution)/shard_map/ppermute | solution.py:791
  624.2 10.3 %collective-permute-done.36 = bf16[256,896]{1,0:T(8,128)(2,1)} collective-permute-done((bf16[256,896]{1,0:T(8,128)(2,1)S(1)}, bf16[256,896]{1,0:T(8,128)(2,1)}, u32[]{:S(2)}, u32[]{:S(2)}) %collective-permute-start.36) | collective-permute-done | bytes 458784 | tf_op jit(solution)/shard_map/ppermute | solution.py:791
  648.9 11.8 %shard_map.213 = f32[256,1536]{1,0:T(8,128)S(1)} custom-call(s32[1]{0:T(128)} %bitcast.8.flag_ref, bf16[256,6448]{1,0:T(8,128)(2,1)S(1)} %pad_maximum_fusion.1.x_ref, bf16[6448,1536]{1,0:T(8,128)(2,1)} %bitcast.97, bf16[6448,1536]{1,0:T(8,128)(2,1)} %collective-permute-done.1.other_ref), custom_call_target="tpu_custom_call" | custom-call | flops 5070913536 | bytes 19808256 | tf_op jit(solution)/shard_map/pallas_call | solution.py:157
  682.1 9.7 %collective-permute-done.46 = f32[21392]{0:T(1024)S(1)} collective-permute-done((f32[21392]{0:T(1024)S(1)}, f32[21392]{0:T(1024)S(1)}, u32[]{:S(2)}, u32[]{:S(2)}) %collective-permute-start.46) | collective-permute-done | bytes 85600 | tf_op jit(solution)/shard_map/ppermute | solution.py:987
  694.6 8.8 %collective-permute-done.47 = f32[21392]{0:T(1024)S(1)} collective-permute-done((f32[21392]{0:T(1024)S(1)}, f32[21392]{0:T(1024)S(1)}, u32[]{:S(2)}, u32[]{:S(2)}) %collective-permute-start.47) | collective-permute-done | bytes 85600 | tf_op jit(solution)/shard_map/ppermute | solution.py:987
  718.2 19.0 %shard_map.214 = (f32[96,6448]{1,0:T(8,128)S(1)}, f32[192,1536]{1,0:T(8,128)S(1)}, bf16[2,256,1536]{2,1,0:T(8,128)(2,1)S(1)}, f32[2,256,1536]{2,1,0:T(8,128)}) custom-call(bf16[384,384]{1,0:T(8,128)(2,1)S(1)} %copy-done.42, bf16[384,448]{1,0:T(8,128)(2,1)S(1)} %copy-done.38, bf16[384,384]{1,0:T(8,128)(2,1)S(1)} %copy-done.39, ...), custom_call_target="tpu_custom_call" | custom-call | tf_op jit(solution)/shard_map/pallas_call | solution.py:738
  (541 shorter events, 288.9 us)
Async XLA Ops:
  7.2 699.5 %reduce-scatter.11.cloned.1.call-start = ((), (), s32[]{:S(2)}) async-start(), calls=%async_computation.8 | async-start | bytes 1474560 | tf_op jit(solution)/shard_map/reduce_scatter | solution.py:806
  7.2 53.9 %collective-permute-start.1 = (bf16[6448,1536]{1,0:T(8,128)(2,1)}, bf16[6448,1536]{1,0:T(8,128)(2,1)}, u32[]{:S(2)}, u32[]{:S(2)}) collective-permute-start(bf16[6448,1536]{1,0:T(8,128)(2,1)} %bitcast.93), channel_id=1, source_target_pairs={{0,16},{16,0},{1,17},{17,1},{2,18},{18,2},{3,19},{19,3},{4,20},{20... | collective-permute-start | bytes 59424776 | tf_op jit(solution)/shard_map/ppermute | solution.py:758
  7.8 72.4 %collective-permute-start.9 = (bf16[3072,1536]{1,0:T(8,128)(2,1)}, bf16[3072,1536]{1,0:T(8,128)(2,1)}, u32[]{:S(2)}, u32[]{:S(2)}) collective-permute-start(bf16[3072,1536]{1,0:T(8,128)(2,1)} %bitcast.98), channel_id=1, source_target_pairs={{0,16},{16,0},{1,17},{17,1},{2,18},{18,2},{3,19},{19,3},{4,20},{20... | collective-permute-start | bytes 28311560 | tf_op jit(solution)/shard_map/ppermute | solution.py:758
  9.0 38.4 %collective-permute-start.2 = (bf16[256,1536]{1,0:T(8,128)(2,1)S(1)}, bf16[256,1536]{1,0:T(8,128)(2,1)}, u32[]{:S(2)}, u32[]{:S(2)}) collective-permute-start(bf16[256,1536]{1,0:T(8,128)(2,1)S(1)} %dynamic-slice_bitcast_fusion.x_ref), channel_id=1, source_target_pairs={{0,1},{1,2},{2,3},{3,0},{4,5},{5,6},{6,7},{7,4},{8,9},{9,10},{10,1... | collective-permute-start | bytes 2359304 | tf_op jit(solution)/shard_map/ppermute | solution.py:782
  12.0 35.7 %collective-permute-start.3 = (bf16[256,1536]{1,0:T(8,128)(2,1)S(1)}, bf16[256,1536]{1,0:T(8,128)(2,1)}, u32[]{:S(2)}, u32[]{:S(2)}) collective-permute-start(bf16[256,1536]{1,0:T(8,128)(2,1)S(1)} %dynamic-slice_bitcast_fusion.x_ref), channel_id=1, source_target_pairs={{0,2},{1,3},{2,0},{3,1},{4,6},{5,7},{6,4},{7,5},{8,10},{9,11},{10,... | collective-permute-start | bytes 2359304 | tf_op jit(solution)/shard_map/ppermute | solution.py:782
  140.8 41.5 %collective-permute-start.6 = (bf16[256,1536]{1,0:T(8,128)(2,1)S(1)}, bf16[256,1536]{1,0:T(8,128)(2,1)S(1)}, u32[]{:S(2)}, u32[]{:S(2)}) collective-permute-start(bf16[256,1536]{1,0:T(8,128)(2,1)S(1)} %fusion.16.x_ref), channel_id=1, source_target_pairs={{0,1},{1,2},{2,3},{3,0},{4,5},{5,6},{6,7},{7,4},{8,9},{9,10},{10,1... | collective-permute-start | bytes 2359304 | tf_op jit(solution)/shard_map/ppermute | solution.py:782
  142.2 40.0 %collective-permute-start.7 = (bf16[256,1536]{1,0:T(8,128)(2,1)S(1)}, bf16[256,1536]{1,0:T(8,128)(2,1)S(1)}, u32[]{:S(2)}, u32[]{:S(2)}) collective-permute-start(bf16[256,1536]{1,0:T(8,128)(2,1)S(1)} %fusion.16.x_ref), channel_id=1, source_target_pairs={{0,2},{1,3},{2,0},{3,1},{4,6},{5,7},{6,4},{7,5},{8,10},{9,11},{10,... | collective-permute-start | bytes 2359304 | tf_op jit(solution)/shard_map/ppermute | solution.py:782
  144.7 37.6 %collective-permute-start.8 = (bf16[256,1536]{1,0:T(8,128)(2,1)S(1)}, bf16[256,1536]{1,0:T(8,128)(2,1)S(1)}, u32[]{:S(2)}, u32[]{:S(2)}) collective-permute-start(bf16[256,1536]{1,0:T(8,128)(2,1)S(1)} %fusion.16.x_ref), channel_id=1, source_target_pairs={{0,3},{1,0},{2,1},{3,2},{4,7},{5,4},{6,5},{7,6},{8,11},{9,8},{10,9... | collective-permute-start | bytes 2359304 | tf_op jit(solution)/shard_map/ppermute | solution.py:782
  256.5 46.2 %collective-permute-start.14 = (bf16[256,1536]{1,0:T(8,128)(2,1)S(1)}, bf16[256,1536]{1,0:T(8,128)(2,1)S(1)}, u32[]{:S(2)}, u32[]{:S(2)}) collective-permute-start(bf16[256,1536]{1,0:T(8,128)(2,1)S(1)} %copy-done.3), channel_id=1, source_target_pairs={{0,1},{1,2},{2,3},{3,0},{4,5},{5,6},{6,7},{7,4},{8,9},{9,10},{10,1... | collective-permute-start | bytes 2359304 | tf_op jit(solution)/shard_map/ppermute | solution.py:782
  260.5 42.3 %collective-permute-start.15 = (bf16[256,1536]{1,0:T(8,128)(2,1)S(1)}, bf16[256,1536]{1,0:T(8,128)(2,1)S(1)}, u32[]{:S(2)}, u32[]{:S(2)}) collective-permute-start(bf16[256,1536]{1,0:T(8,128)(2,1)S(1)} %copy-done.3), channel_id=1, source_target_pairs={{0,2},{1,3},{2,0},{3,1},{4,6},{5,7},{6,4},{7,5},{8,10},{9,11},{10,... | collective-permute-start | bytes 2359304 | tf_op jit(solution)/shard_map/ppermute | solution.py:782
  260.5 42.3 %collective-permute-start.16 = (bf16[256,1536]{1,0:T(8,128)(2,1)S(1)}, bf16[256,1536]{1,0:T(8,128)(2,1)S(1)}, u32[]{:S(2)}, u32[]{:S(2)}) collective-permute-start(bf16[256,1536]{1,0:T(8,128)(2,1)S(1)} %copy-done.3), channel_id=1, source_target_pairs={{0,3},{1,0},{2,1},{3,2},{4,7},{5,4},{6,5},{7,6},{8,11},{9,8},{10,9... | collective-permute-start | bytes 2359304 | tf_op jit(solution)/shard_map/ppermute | solution.py:782
  430.1 58.6 %collective-permute-start.25 = (bf16[1536,448]{0,1:T(8,128)(2,1)}, bf16[1536,448]{0,1:T(8,128)(2,1)}, u32[]{:S(2)}, u32[]{:S(2)}) collective-permute-start(bf16[1536,448]{0,1:T(8,128)(2,1)} %convolution_convert_fusion.1), channel_id=1, source_target_pairs={{0,16},{16,0},{1,17},{17,1},{2,18},{18,2},{3,19},{19,3},{4,20},{20... | collective-permute-start | bytes 4128776 | tf_op jit(solution)/shard_map/ppermute | solution.py:758
  433.0 273.7 %reduce-scatter.17.cloned.1.call-start = ((), (), s32[]{:S(2)}) async-start(), calls=%async_computation.11 | async-start | bytes 1474560 | tf_op jit(solution)/shard_map/reduce_scatter | solution.py:806
  451.3 75.3 %collective-permute-start.26 = (bf16[256,1536]{1,0:T(8,128)(2,1)S(1)}, bf16[256,1536]{1,0:T(8,128)(2,1)}, u32[]{:S(2)}, u32[]{:S(2)}) collective-permute-start(bf16[256,1536]{1,0:T(8,128)(2,1)S(1)} %get-tuple-element.154.x_ref), channel_id=1, source_target_pairs={{0,1},{1,2},{2,3},{3,0},{4,5},{5,6},{6,7},{7,4},{8,9},{9,10},{10,1... | collective-permute-start | bytes 2359304 | tf_op jit(solution)/shard_map/ppermute | solution.py:782
  454.8 71.7 %collective-permute-start.27 = (bf16[256,1536]{1,0:T(8,128)(2,1)S(1)}, bf16[256,1536]{1,0:T(8,128)(2,1)}, u32[]{:S(2)}, u32[]{:S(2)}) collective-permute-start(bf16[256,1536]{1,0:T(8,128)(2,1)S(1)} %get-tuple-element.154.x_ref), channel_id=1, source_target_pairs={{0,2},{1,3},{2,0},{3,1},{4,6},{5,7},{6,4},{7,5},{8,10},{9,11},{10,... | collective-permute-start | bytes 2359304 | tf_op jit(solution)/shard_map/ppermute | solution.py:782
  456.6 70.0 %collective-permute-start.28 = (bf16[256,1536]{1,0:T(8,128)(2,1)S(1)}, bf16[256,1536]{1,0:T(8,128)(2,1)}, u32[]{:S(2)}, u32[]{:S(2)}) collective-permute-start(bf16[256,1536]{1,0:T(8,128)(2,1)S(1)} %get-tuple-element.154.x_ref), channel_id=1, source_target_pairs={{0,3},{1,0},{2,1},{3,2},{4,7},{5,4},{6,5},{7,6},{8,11},{9,8},{10,9... | collective-permute-start | bytes 2359304 | tf_op jit(solution)/shard_map/ppermute | solution.py:782
  460.6 246.2 %reduce-scatter.13.cloned.1.call-start = ((), (), s32[]{:S(2)}) async-start(), calls=%async_computation.9 | async-start | bytes 1966080 | tf_op jit(solution)/shard_map/reduce_scatter | solution.py:806
  537.1 169.7 %reduce-scatter.15.cloned.1.call-start = ((), (), s32[]{:S(2)}) async-start(), calls=%async_computation.10 | async-start | bytes 1474560 | tf_op jit(solution)/shard_map/reduce_scatter | solution.py:806
  543.0 47.9 %collective-permute-start.29 = (bf16[256,768]{1,0:T(8,128)(2,1)}, bf16[256,768]{1,0:T(8,128)(2,1)}, u32[]{:S(2)}, u32[]{:S(2)}) collective-permute-start(bf16[256,768]{1,0:T(8,128)(2,1)} %get-tuple-element.211), channel_id=1, source_target_pairs={{0,1},{1,2},{2,3},{3,0},{4,5},{5,6},{6,7},{7,4},{8,9},{9,10},{10,1... | collective-permute-start | bytes 1179656 | tf_op jit(solution)/shard_map/ppermute | solution.py:791
  543.2 47.7 %collective-permute-start.30 = (bf16[256,768]{1,0:T(8,128)(2,1)}, bf16[256,768]{1,0:T(8,128)(2,1)}, u32[]{:S(2)}, u32[]{:S(2)}) collective-permute-start(bf16[256,768]{1,0:T(8,128)(2,1)} %get-tuple-element.210), channel_id=1, source_target_pairs={{0,2},{1,3},{2,0},{3,1},{4,6},{5,7},{6,4},{7,5},{8,10},{9,11},{10,... | collective-permute-start | bytes 1179656 | tf_op jit(solution)/shard_map/ppermute | solution.py:791
  544.9 46.0 %collective-permute-start.31 = (bf16[256,768]{1,0:T(8,128)(2,1)}, bf16[256,768]{1,0:T(8,128)(2,1)}, u32[]{:S(2)}, u32[]{:S(2)}) collective-permute-start(bf16[256,768]{1,0:T(8,128)(2,1)} %get-tuple-element.209), channel_id=1, source_target_pairs={{0,3},{1,0},{2,1},{3,2},{4,7},{5,4},{6,5},{7,6},{8,11},{9,8},{10,9... | collective-permute-start | bytes 1179656 | tf_op jit(solution)/shard_map/ppermute | solution.py:791
  599.7 37.6 %collective-permute-start.33 = (bf16[1536,384]{1,0:T(8,128)(2,1)}, bf16[1536,384]{1,0:T(8,128)(2,1)}, u32[]{:S(2)}, u32[]{:S(2)}) collective-permute-start(bf16[1536,384]{1,0:T(8,128)(2,1)} %convolution_convert_fusion.2), channel_id=1, source_target_pairs={{0,16},{16,0},{1,17},{17,1},{2,18},{18,2},{3,19},{19,3},{4,20},{20... | collective-permute-start | bytes 3538952 | tf_op jit(solution)/shard_map/ppermute | solution.py:758
  599.9 106.9 %reduce-scatter.7.cloned.1.call-start = ((), (), s32[]{:S(2)}) async-start(), calls=%async_computation.6 | async-start | bytes 1474560 | tf_op jit(solution)/shard_map/reduce_scatter | solution.py:806
  641.8 66.7 %reduce-scatter.9.cloned.1.call-start = ((), (), s32[]{:S(2)}) async-start(), calls=%async_computation.7 | async-start | bytes 1966080 | tf_op jit(solution)/shard_map/reduce_scatter | solution.py:806
  (169 other events, 2000.9 us)
Sparse Core Ops, SparseCore 0:
  433.1 30.0 reduce-scatter.10
  465.5 27.8 reduce-scatter.16
  537.2 33.0 reduce-scatter.12
  600.0 27.7 reduce-scatter.14
  641.9 26.6 reduce-scatter.6
  671.2 37.1 reduce-scatter.8

commit v4 on v3

--- a/solution.py
+++ b/solution.py
@@ -174,6 +174,165 @@
     )(flag, x, own, other)
 
 
+def spread_copies(pairs, sems):
+    send, recv, keep = sems
+    section, q = lax.axis_index("section"), lax.axis_index("seq")
+    spot = lax.rem(q, PLANE)
+    base = q - spot
+    away, own = [], []
+    for at, (src, dst) in enumerate(pairs):
+        width = dst.shape[2]
+        for k in range(PLANE):
+            peer = lax.rem(spot + k, PLANE)
+            part = src.at[:, pl.ds(pl.multiple_of(peer * width, 128), width)]
+            if k:
+                away.append(
+                    pltpu.make_async_remote_copy(
+                        src_ref=part, dst_ref=dst.at[k], send_sem=send.at[3 * at + k - 1],
+                        recv_sem=recv.at[3 * at + k - 1], device_id=(section, base + peer), device_id_type=MESH,
+                    )
+                )
+            else:
+                own.append(pltpu.make_async_copy(part, dst.at[0], keep.at[at]))
+    return away, own
+
+
+def spread_start(pairs, sems):
+    section, q = lax.axis_index("section"), lax.axis_index("seq")
+    spot = lax.rem(q, PLANE)
+    barrier = pltpu.get_barrier_semaphore()
+    for k in range(1, PLANE):
+        peer = q - spot + lax.rem(spot + k, PLANE)
+        pl.semaphore_signal(barrier, inc=1, device_id=(section, peer), device_id_type=MESH)
+    pl.semaphore_wait(barrier, PLANE - 1)
+    away, own = spread_copies(pairs, sems)
+    for copy in away + own:
+        copy.start()
+
+
+def spread_wait(pairs, sems):
+    away, own = spread_copies(pairs, sems)
+    for copy in away + own:
+        copy.wait()
+
+
+def spread_specs(sources):
+    anywhere = pl.BlockSpec(memory_space=pl.ANY)
+    shapes = [jax.ShapeDtypeStruct((PLANE, v.shape[0], v.shape[1] // PLANE), v.dtype) for v in sources]
+    dma = pltpu.SemaphoreType.DMA
+    sems = [dma((3 * len(sources),)), dma((3 * len(sources),)), dma((len(sources),))] if sources else []
+    return [anywhere] * len(sources), shapes, sems
+
+
+def spreading(body, n_in, n_out, count, first, last):
+    if not count:
+        return body
+
+    def kernel(*refs):
+        ins, rest = refs[: n_in + count], refs[n_in + count :]
+        outs, scratch = rest[: n_out + count], rest[n_out + count :]
+        pairs = list(zip(ins[n_in:], outs[n_out:]))
+        sems = scratch[-3:]
+
+        @pl.when(first())
+        def _():
+            spread_start(pairs, sems)
+
+        body(*ins[:n_in], *outs[:n_out], *scratch[:-3])
+
+        @pl.when(last())
+        def _():
+            spread_wait(pairs, sems)
+
+    return kernel
+
+
+def call_params(collective_id):
+    if collective_id is None:
+        return grid_params()
+    return pltpu.CompilerParams(
+        vmem_limit_bytes=48 * MIB, collective_id=collective_id, has_side_effects=True
+    )
+
+
+def project_kernel(flag_ref, x_ref, before_ref, own_ref, other_ref, o_ref, halo_ref):
+    def product(w_ref):
+        o_ref[...] = dot_nt(x_ref[...], w_ref[...])
+        halo_ref[...] = dot_nt(before_ref[...], w_ref[...])
+
+    @pl.when(flag_ref[0] == 1)
+    def _():
+        product(own_ref)
+
+    @pl.when(flag_ref[0] == 0)
+    def _():
+        product(other_ref)
+
+
+def project_mm(x, before, own, other, flag, tile):
+    rows, depth = x.shape
+    width = own.shape[0]
+    return pl.pallas_call(
+        project_kernel,
+        grid_spec=pltpu.PrefetchScalarGridSpec(
+            num_scalar_prefetch=1,
+            grid=(pl.cdiv(width, tile),),
+            in_specs=[
+                pl.BlockSpec((rows, depth), lambda j, f: (0, 0)),
+                pl.BlockSpec((16, depth), lambda j, f: (0, 0)),
+                pl.BlockSpec((tile, depth), lambda j, f: (j * f[0], 0)),
+                pl.BlockSpec((tile, depth), lambda j, f: (j * (1 - f[0]), 0)),
+            ],
+            out_specs=[
+                pl.BlockSpec((rows, tile), lambda j, f: (0, j)),
+                pl.BlockSpec((16, tile), lambda j, f: (0, j)),
+            ],
+        ),
+        out_shape=[sds(rows, width, F32), sds(16, width, F32)],
+        compiler_params=pltpu.CompilerParams(vmem_limit_bytes=48 * MIB),
+        cost_estimate=pl.CostEstimate(
+            flops=2 * rows * depth * width, bytes_accessed=2 * depth * width, transcendentals=0
+        ),
+    )(flag, x, before, own, other)
+
+
+def back_kernel(flag_ref, gate_ref, rest_ref, own_ref, other_ref, o_ref):
+    def product(w_ref):
+        o_ref[...] = dot_nn(gate_ref[...], w_ref[0:INNER, :]) + dot_nn(
+            rest_ref[:, 0 : PROJ - INNER], w_ref[INNER:PROJ, :]
+        )
+
+    @pl.when(flag_ref[0] == 1)
+    def _():
+        product(own_ref)
+
+    @pl.when(flag_ref[0] == 0)
+    def _():
+        product(other_ref)
+
+
+def back_mm(gate, rest, own, other, flag, tile):
+    return pl.pallas_call(
+        back_kernel,
+        grid_spec=pltpu.PrefetchScalarGridSpec(
+            num_scalar_prefetch=1,
+            grid=(D // tile,),
+            in_specs=[
+                pl.BlockSpec((ROWS, INNER), lambda j, f: (0, 0)),
+                pl.BlockSpec((ROWS, REST), lambda j, f: (0, 0)),
+                pl.BlockSpec((PROJ, tile), lambda j, f: (0, j * f[0])),
+                pl.BlockSpec((PROJ, tile), lambda j, f: (0, j * (1 - f[0]))),
+            ],
+            out_specs=pl.BlockSpec((ROWS, tile), lambda j, f: (0, j)),
+        ),
+        out_shape=sds(ROWS, D, F32),
+        compiler_params=pltpu.CompilerParams(vmem_limit_bytes=48 * MIB),
+        cost_estimate=pl.CostEstimate(
+            flops=2 * ROWS * D * PROJ, bytes_accessed=2 * D * PROJ, transcendentals=0
+        ),
+    )(flag, gate, rest, own, other)
+
+
 def front_kernel(
     x_ref, bc_ref, raw_ref, xh_ref, bch_ref, xw_ref, bcw_ref, hp_ref,
     val_ref, state_ref, dec_ref, step_ref, cum_ref, cumt_ref, b_ref, c_ref, ct_ref, g_ref, gt_ref, bt_ref,
@@ -232,29 +391,34 @@
     return pltpu.CompilerParams(vmem_limit_bytes=48 * MIB)
 
 
-def front(proj, halo, taps, hp):
+def front(proj, halo, taps, hp, sources=(), collective_id=None):
     square = (ROWS, ROWS)
+    specs, shapes, sems = spread_specs(sources)
+    body = spreading(
+        front_kernel, 8, 11, len(sources), lambda: pl.program_id(0) == 0, lambda: pl.program_id(0) == STEPS - 1
+    )
     return pl.pallas_call(
-        front_kernel,
+        body,
         grid=(STEPS,),
         in_specs=[
             lanes(ROWS, STEPS), fixed(ROWS, 2 * STEPS), fixed(ROWS, 50, 128),
-            lanes(8), fixed(8, STEPS), lanes(8), fixed(8, STEPS), whole((8, 128)),
+            lanes(8), fixed(8, STEPS), lanes(8), fixed(8, STEPS), whole((8, 128)), *specs,
         ],
         out_specs=[
             lanes(ROWS), lanes(128), lanes(8),
             whole((ROWS, 384)), whole((ROWS, 384)), whole((128, ROWS)),
-            whole((ROWS, 256)), whole((ROWS, 384)), whole((128, ROWS)), whole(square), whole(square),
+            whole((ROWS, 256)), whole((ROWS, 384)), whole((128, ROWS)), whole(square), whole(square), *specs,
         ],
         out_shape=[
             sds(ROWS, INNER, F32), sds(128, INNER, F32), sds(8, INNER, F32),
             sds(ROWS, 384, BF16), sds(ROWS, 384, BF16), sds(128, ROWS, F32),
             sds(ROWS, 256, BF16), sds(ROWS, 384, BF16), sds(128, ROWS, BF16), sds(*square, F32), sds(*square, F32),
+            *shapes,
         ],
-        scratch_shapes=[pltpu.VMEM((256, ROWS), BF16)],
-        compiler_params=grid_params(),
+        scratch_shapes=[pltpu.VMEM((256, ROWS), BF16), *sems],
+        compiler_params=call_params(collective_id),
         cost_estimate=pl.CostEstimate(flops=10**9, bytes_accessed=10 * MIB, transcendentals=10**6),
-    )(proj, proj, proj, halo, halo, taps, taps, hp)
+    )(proj, proj, proj, halo, halo, taps, taps, hp, *sources)
 
 
 def exchange_kernel(
@@ -406,8 +570,8 @@
 
 
 def mix_kernel(
-    g_ref, step_ref, cum_ref, cumt_ref, val_ref, gate_ref, c_ref, car_ref, lp_ref, gain_ref,
-    y_ref, low_ref, gated_ref, sum_ref,
+    n, g_ref, step_ref, cum_ref, cumt_ref, val_ref, gate_ref, c_ref, car_ref, lp_ref, gain_ref,
+    y_ref, low_ref, owned_ref, gated_ref, sum_ref,
 ):
     j = pl.program_id(0)
     heads = expander(j)
@@ -449,19 +613,23 @@
         for k in range(STEPS):
             at = slice(k * WIDE, k * WIDE + WIDE)
             low_ref[:, at] = (gated_ref[k] * scale * gain_ref[1:2, at]).astype(BF16)
-
-
-def mix(g, step, cum, cumt, values, proj, c, carried, lp):
+        width = INNER // n
+        for q in range(n):
+            to = (q % PLANE) * LANES + (q // PLANE) * width
+            owned_ref[:, to : to + width] = low_ref[:, q * width : (q + 1) * width]
+
+
+def mix(g, step, cum, cumt, values, proj, c, carried, lp, n):
     return pl.pallas_call(
-        mix_kernel,
+        functools.partial(mix_kernel, n),
         grid=(STEPS,),
         in_specs=[
             whole((ROWS, ROWS)), whole((ROWS, 384)), whole((ROWS, 384)), whole((128, ROWS)),
             lanes(ROWS), lanes(ROWS), whole((ROWS, 384)), lanes(128), lanes(8),
             whole((8, INNER)),
         ],
-        out_specs=[lanes(ROWS), whole((ROWS, INNER))],
-        out_shape=[sds(ROWS, INNER, F32), sds(ROWS, INNER, BF16)],
+        out_specs=[lanes(ROWS), whole((ROWS, INNER)), whole((ROWS, INNER))],
+        out_shape=[sds(ROWS, INNER, F32), sds(ROWS, INNER, BF16), sds(ROWS, INNER, BF16)],
         scratch_shapes=[pltpu.VMEM((STEPS, ROWS, WIDE), F32), pltpu.VMEM((ROWS, WIDE), F32)],
         compiler_params=grid_params(),
         cost_estimate=pl.CostEstimate(flops=3 * 10**9, bytes_accessed=14 * MIB, transcendentals=4 * 10**6),
@@ -504,7 +672,7 @@
         dcar_ref[...] = dot_nn(ct_ref[...], (dy * jnp.exp(cum)).astype(BF16)).astype(BF16)
 
 
-def gate_back(dg, y, proj, cum, ct, lp):
+def gate_back(dg, y, proj, cum, ct, lp, sources=(), collective_id=None):
     def first(rows):
         return pl.BlockSpec((rows, WIDE), lambda p, j: (0, j * (1 - p) + (STEPS - 1) * p))
 
@@ -514,26 +682,35 @@
     def both(shape):
         return pl.BlockSpec(shape, lambda p, j: (0, 0))
 
+    def at_step(phase, j):
+        return jnp.logical_and(pl.program_id(0) == phase, pl.program_id(1) == j)
+
     kept = pltpu.VMEM((STEPS, ROWS, WIDE), F32)
+    specs, shapes, sems = spread_specs(sources)
+    body = spreading(
+        gate_back_kernel, 6, 4, len(sources), lambda: at_step(0, 0), lambda: at_step(1, STEPS - 1)
+    )
     return pl.pallas_call(
-        gate_back_kernel,
+        body,
         grid=(2, STEPS),
         in_specs=[
             first(ROWS), first(ROWS), first(ROWS), both((ROWS, 384)), both((128, ROWS)),
-            pl.BlockSpec((8, WIDE), lambda p, j: (0, j)),
+            pl.BlockSpec((8, WIDE), lambda p, j: (0, j)), *specs,
         ],
-        out_specs=[second(ROWS), second(ROWS), second(8), second(128)],
-        out_shape=[sds(ROWS, INNER, F32), sds(ROWS, INNER, BF16), sds(8, INNER, F32), sds(128, INNER, BF16)],
-        scratch_shapes=[kept, kept, kept, pltpu.VMEM((ROWS, WIDE), F32), pltpu.VMEM((ROWS, WIDE), F32)],
-        compiler_params=grid_params(),
+        out_specs=[second(ROWS), second(ROWS), second(8), second(128), *specs],
+        out_shape=[
+            sds(ROWS, INNER, F32), sds(ROWS, INNER, BF16), sds(8, INNER, F32), sds(128, INNER, BF16), *shapes,
+        ],
+        scratch_shapes=[kept, kept, kept, pltpu.VMEM((ROWS, WIDE), F32), pltpu.VMEM((ROWS, WIDE), F32), *sems],
+        compiler_params=call_params(collective_id),
         cost_estimate=pl.CostEstimate(flops=10**9, bytes_accessed=16 * MIB, transcendentals=2 * 10**6),
-    )(dg, y, proj, cum, ct, lp)
+    )(dg, y, proj, cum, ct, lp, *sources)
 
 
 def core_back_kernel(
     x_ref, bc_ref, raw_ref, xh_ref, bch_ref, xw_ref, bcw_ref, hp_ref,
     step_ref, cum_ref, cumt_ref, gt_ref, b_ref, c_ref, y_ref, dy_ref, car_ref, late_ref, lp_ref,
-    dx_ref, dbc_ref, tail_ref, tailbc_ref, head_ref, headbc_ref, taps_ref, tapsbc_ref, draw_ref, hg_ref,
+    dx_ref, tail_ref, head_ref, taps_ref, hg_ref,
     dgt_acc, dc_acc, db_acc, dcum_acc, dstep_acc, rows_acc,
 ):
     j = pl.program_id(0)
@@ -543,58 +720,60 @@
         for acc in (dgt_acc, dc_acc, db_acc, dcum_acc, dstep_acc, rows_acc):
             acc[...] = jnp.zeros_like(acc)
 
-    ext = extended(x_ref[...], xh_ref[...])
-    pre = conv_pre(ext, xw_ref[...])
-    sig = sigmoid(pre)
-    values = pre * sig
-    heads, to_heads = expander(j), collector(j)
-    step = dot_nn(step_ref[...], heads)
-    cum = dot_nn(cum_ref[...], heads)
-    last = cum[ROWS - 1 : ROWS]
-    scaled = values * step
-    scaled_parts = split2(scaled)
-    dy = dy_ref[...]
-    dy_parts = split2(dy)
-    sides = []
-    for pair in range(WIDE // 128):
-        top = jnp.zeros((HALF, 128), F32)
-        bottom = jnp.zeros((HALF, 128), F32)
-        at = slice(pair * 128, pair * 128 + 128)
-        own = [part[:, at] for part in scaled_parts]
-        for i in (2 * pair, 2 * pair + 1):
-            row = cumt_ref[pl.ds((WIDE // HEADDIM) * j + i, 1), :]
-            column = cum[:, i * HEADDIM : i * HEADDIM + 1]
-            part = head_lanes(dy_parts, i)
-            decay = decay_block(row, column[0:HALF])
-            top = top + fine(dot_nn, split2(gt_ref[0:HALF, :] * decay), part)
-            dgt_acc[0:HALF, :] += fine(dot_nt, [v[0:HALF] for v in own], part) * decay
-            decay = decay_block(row[:, HALF:ROWS], column[HALF:ROWS])
-            late_part = [v[HALF:ROWS] for v in part]
-            bottom = bottom + fine(dot_nn, split2(gt_ref[HALF:ROWS, HALF:ROWS] * decay), late_part)
-            dgt_acc[HALF:ROWS, HALF:ROWS] += fine(dot_nt, [v[HALF:ROWS] for v in own], late_part) * decay
-        sides.append(jnp.concatenate([top, bottom], axis=0))
-    car, late = car_ref[...], late_ref[...]
-    to_end = jnp.exp(last - cum)
-    d_ended = dot_nn(b_ref[:, 0:128], late)
-    ended = scaled * to_end
-    dc_acc[...] += fine(dot_nt, split2(dy * jnp.exp(cum)), split2(car))
-    db_acc[...] += dot_nt(ended.astype(BF16), late)
-    d_total = jnp.concatenate(sides, axis=1) + to_end * d_ended
-    skip_w = lp_ref[0:1, :]
-    dcum_acc[...] += collect(dy * (y_ref[...] - skip_w * values) - scaled * d_total, to_heads)
-    dstep_acc[...] += collect(d_total * values, to_heads)
-    at_last = jnp.exp(last) * jnp.sum(late.astype(F32) * car, axis=0, keepdims=True)
-    at_last = at_last + jnp.sum(ended * d_ended, axis=0, keepdims=True)
-    skip = jnp.sum(dy * values, axis=0, keepdims=True)
-    rows_acc[...] += collect(jnp.concatenate([at_last, skip, jnp.zeros((6, WIDE), F32)], axis=0), to_heads)
-    d_pre = (skip_w * dy + step * d_total) * (sig + values * (1.0 - sig))
-    taps_ref[...] = tap_grads(d_pre, ext)
-    head_ref[...] = d_pre[0:8]
-    d_conv = conv_back(d_pre, xw_ref[...])
-    dx_ref[...] = d_conv.astype(BF16)
-    tail_ref[...] = d_conv[ROWS - 8 : ROWS]
-
-    @pl.when(j == STEPS - 1)
+    @pl.when(j < STEPS)
+    def _():
+        ext = extended(x_ref[...], xh_ref[...])
+        pre = conv_pre(ext, xw_ref[...])
+        sig = sigmoid(pre)
+        values = pre * sig
+        heads, to_heads = expander(j), collector(j)
+        step = dot_nn(step_ref[...], heads)
+        cum = dot_nn(cum_ref[...], heads)
+        last = cum[ROWS - 1 : ROWS]
+        scaled = values * step
+        scaled_parts = split2(scaled)
+        dy = dy_ref[...]
+        dy_parts = split2(dy)
+        sides = []
+        for pair in range(WIDE // 128):
+            top = jnp.zeros((HALF, 128), F32)
+            bottom = jnp.zeros((HALF, 128), F32)
+            at = slice(pair * 128, pair * 128 + 128)
+            own = [part[:, at] for part in scaled_parts]
+            for i in (2 * pair, 2 * pair + 1):
+                row = cumt_ref[pl.ds((WIDE // HEADDIM) * j + i, 1), :]
+                column = cum[:, i * HEADDIM : i * HEADDIM + 1]
+                part = head_lanes(dy_parts, i)
+                decay = decay_block(row, column[0:HALF])
+                top = top + fine(dot_nn, split2(gt_ref[0:HALF, :] * decay), part)
+                dgt_acc[0:HALF, :] += fine(dot_nt, [v[0:HALF] for v in own], part) * decay
+                decay = decay_block(row[:, HALF:ROWS], column[HALF:ROWS])
+                late_part = [v[HALF:ROWS] for v in part]
+                bottom = bottom + fine(dot_nn, split2(gt_ref[HALF:ROWS, HALF:ROWS] * decay), late_part)
+                dgt_acc[HALF:ROWS, HALF:ROWS] += fine(dot_nt, [v[HALF:ROWS] for v in own], late_part) * decay
+            sides.append(jnp.concatenate([top, bottom], axis=0))
+        car, late = car_ref[...], late_ref[...]
+        to_end = jnp.exp(last - cum)
+        d_ended = dot_nn(b_ref[:, 0:128], late)
+        ended = scaled * to_end
+        dc_acc[...] += fine(dot_nt, split2(dy * jnp.exp(cum)), split2(car))
+        db_acc[...] += dot_nt(ended.astype(BF16), late)
+        d_total = jnp.concatenate(sides, axis=1) + to_end * d_ended
+        skip_w = lp_ref[0:1, :]
+        dcum_acc[...] += collect(dy * (y_ref[...] - skip_w * values) - scaled * d_total, to_heads)
+        dstep_acc[...] += collect(d_total * values, to_heads)
+        at_last = jnp.exp(last) * jnp.sum(late.astype(F32) * car, axis=0, keepdims=True)
+        at_last = at_last + jnp.sum(ended * d_ended, axis=0, keepdims=True)
+        skip = jnp.sum(dy * values, axis=0, keepdims=True)
+        rows_acc[...] += collect(jnp.concatenate([at_last, skip, jnp.zeros((6, WIDE), F32)], axis=0), to_heads)
+        d_pre = (skip_w * dy + step * d_total) * (sig + values * (1.0 - sig))
+        taps_ref[...] = tap_grads(d_pre, ext)
+        head_ref[...] = d_pre[0:8]
+        d_conv = conv_back(d_pre, xw_ref[...])
+        dx_ref[...] = d_conv.astype(BF16)
+        tail_ref[...] = d_conv[ROWS - 16 : ROWS]
+
+    @pl.when(j == STEPS)
     def _():
         seen = iota((ROWS, ROWS), 1) >= iota((ROWS, ROWS), 0)
         d_gt = split2(jnp.where(seen, dgt_acc[...], 0.0))
@@ -604,18 +783,24 @@
         pre_bc = conv_pre(ext_bc, bcw_ref[...])
         sig_bc = sigmoid(pre_bc)
         d_pre_bc = jnp.concatenate([d_b, d_c], axis=1) * (sig_bc + pre_bc * sig_bc * (1.0 - sig_bc))
-        tapsbc_ref[...] = tap_grads(d_pre_bc, ext_bc)
-        headbc_ref[...] = d_pre_bc[0:8]
+        taps_ref[...] = tap_grads(d_pre_bc, ext_bc)
+        head_ref[...] = d_pre_bc[0:8]
         d_conv_bc = conv_back(d_pre_bc, bcw_ref[...])
-        dbc_ref[...] = d_conv_bc.astype(BF16)
-        tailbc_ref[...] = d_conv_bc[ROWS - 8 : ROWS]
+        dx_ref[...] = d_conv_bc.astype(BF16)
+        tail_ref[...] = d_conv_bc[ROWS - 16 : ROWS]
+
+    @pl.when(j == STEPS + 1)
+    def _():
         raw, step_all, rate = step_parts(raw_ref, hp_ref)
         end = iota((ROWS, 128), 0) == ROWS - 1
         d_cum_all = dcum_acc[...] + jnp.where(end, rows_acc[0:1, :], 0.0)
         d_log = exact_left(triangle(False), d_cum_all)
         d_step = dstep_acc[...] + rate * d_log
         d_raw = jnp.where(iota((ROWS, 128), 1) < HEADS, d_step * sigmoid(raw), 0.0)
-        draw_ref[...] = d_raw.astype(BF16)
+        dx_ref[...] = jnp.concatenate([d_raw, jnp.zeros((ROWS, WIDE - 128), F32)], axis=1).astype(BF16)
+        tail_ref[...] = dx_ref[ROWS - 16 : ROWS, :].astype(F32)
+        head_ref[...] = jnp.zeros_like(head_ref)
+        taps_ref[...] = jnp.zeros_like(taps_ref)
         hg_ref[...] = jnp.concatenate(
             [
                 jnp.sum(d_raw, axis=0, keepdims=True),
@@ -627,33 +812,40 @@
         )
 
 
-def core_back(proj, halo, taps, hp, step, cum, cumt, gt, b, c, y, dy, carried, late, lp):
+def core_back(proj, halo, taps, hp, step, cum, cumt, gt, b, c, y, dy, carried, late, lp, sources=(), collective_id=None):
     acc = pltpu.VMEM((ROWS, 128), F32)
+
+    def lanes(rows, first=0):
+        return pl.BlockSpec((rows, WIDE), lambda j: (0, first + jnp.minimum(j, STEPS - 1)))
+
+    def out(rows):
+        return pl.BlockSpec((rows, WIDE), lambda j: (0, j))
+
+    specs, shapes, sems = spread_specs(sources)
+    body = spreading(
+        core_back_kernel, 19, 5, len(sources),
+        lambda: pl.program_id(0) == 0, lambda: pl.program_id(0) == STEPS + 1,
+    )
     return pl.pallas_call(
-        core_back_kernel,
-        grid=(STEPS,),
+        body,
+        grid=(STEPS + 2,),
         in_specs=[
             lanes(ROWS, STEPS), fixed(ROWS, 2 * STEPS), fixed(ROWS, 50, 128),
             lanes(8), fixed(8, STEPS), lanes(8), fixed(8, STEPS), whole((8, 128)),
             whole((ROWS, 384)), whole((ROWS, 384)), whole((128, ROWS)), whole((ROWS, ROWS)),
             whole((ROWS, 256)), whole((ROWS, 384)),
-            lanes(ROWS), lanes(ROWS), lanes(128), lanes(128), lanes(8),
+            lanes(ROWS), lanes(ROWS), lanes(128), lanes(128), lanes(8), *specs,
         ],
-        out_specs=[
-            lanes(ROWS), whole((ROWS, 256)), lanes(8), whole((8, 256)), lanes(8), whole((8, 256)),
-            lanes(8), whole((8, 256)), whole((ROWS, 128)), whole((8, 128)),
+        out_specs=[out(ROWS), out(16), out(8), out(8), whole((8, 128)), *specs],
+        out_shape=[
+            sds(ROWS, REST, BF16), sds(16, REST, F32), sds(8, REST, F32), sds(8, REST, F32), sds(8, 128, F32), *shapes,
         ],
-        out_shape=[
-            sds(ROWS, INNER, BF16), sds(ROWS, 256, BF16), sds(8, INNER, F32), sds(8, 256, F32),
-            sds(8, INNER, F32), sds(8, 256, F32), sds(8, INNER, F32), sds(8, 256, F32),
-            sds(ROWS, 128, BF16), sds(8, 128, F32),
-        ],
-        scratch_shapes=[pltpu.VMEM((ROWS, ROWS), F32), acc, acc, acc, acc, pltpu.VMEM((8, 128), F32)],
-        compiler_params=grid_params(),
+        scratch_shapes=[pltpu.VMEM((ROWS, ROWS), F32), acc, acc, acc, acc, pltpu.VMEM((8, 128), F32), *sems],
+        compiler_params=call_params(collective_id),
         cost_estimate=pl.CostEstimate(flops=8 * 10**9, bytes_accessed=14 * MIB, transcendentals=5 * 10**6),
     )(
         proj, proj, proj, halo, halo, taps, taps, hp,
-        step, cum, cumt, gt, b, c, y, dy, carried, late, lp,
+        step, cum, cumt, gt, b, c, y, dy, carried, late, lp, *sources,
     )
 
 
@@ -774,31 +966,25 @@
     return lax.optimization_barrier((value, *others))[0]
 
 
-def tied_list(values, other):
-    return list(lax.optimization_barrier((*values, other))[:-1])
-
-
 def copies_of(value, n):
     return [value] + [lax.ppermute(value, "seq", plane_route(k, n)) for k in range(1, PLANE)]
 
 
-def pieces_of(value, n):
-    spot = lax.axis_index("seq") % PLANE
-    width = value.shape[1] // PLANE
-    got = [lax.dynamic_slice_in_dim(value, spot * width, width, 1)]
-    for k in range(1, PLANE):
-        part = lax.dynamic_slice_in_dim(value, (spot + k) % PLANE * width, width, 1)
-        got.append(lax.ppermute(part, "seq", plane_route(k, n)))
-    return got
+def arrived(value, *lists):
+    value, *rest = lax.optimization_barrier((value, *(copy for copies in lists for copy in copies)))
+    return (value, *(jnp.stack(rest[k * PLANE : (k + 1) * PLANE]) for k in range(len(lists))))
 
 
 def partial_grad(left, right):
     core = lax.axis_index("section")
-    left, right = jnp.concatenate(left, axis=0), jnp.concatenate(right, axis=0)
-    half = right.shape[1] // 2
-    away = dot_tn(left, lax.dynamic_slice_in_dim(right, (1 - core) * half, half, 1)).astype(BF16)
-    mine = dot_tn(left, lax.dynamic_slice_in_dim(right, core * half, half, 1))
-    return (mine + swap(away).astype(F32)).astype(BF16)
+    half = right.shape[2] // 2
+
+    def part(side):
+        cols = lax.dynamic_slice_in_dim(right, side * half, half, 2)
+        return lax.dot_general(left, cols, (((0, 1), (0, 1)), ((), ())), preferred_element_type=F32)
+
+    away = part(1 - core).astype(BF16)
+    return (part(core) + swap(away).astype(F32)).astype(BF16)
 
 
 def plane_rows(partial, n):
@@ -835,12 +1021,11 @@
     gate_norm_gain, out_weight,
 ):
     n = lax.axis_size("seq")
-    planes = n // PLANE
     core = lax.axis_index("section")
     place = lax.axis_index("seq")
     first = core == 0
     own_in, own_out = in_weight[0].T, out_weight[0]
-    other_in, other_out = swap(own_in), swap(own_out)
+    other_in = swap(own_in)
     own_small = jnp.concatenate(
         [
             norm_gain[0], conv_weight[0].T.reshape(-1), conv_bias[0], dt_bias[0], a_log[0], d_skip[0],
@@ -857,83 +1042,81 @@
     def mine(pair):
         return lax.dynamic_index_in_dim(pair, core, 0, keepdims=False)
 
-    def project(layer, h):
-        normed = (h * rms(h) * params[layer][0]).astype(BF16)
-        return normed, mm(normed, own_in, other_in, flags[layer], True, 1664)
-
-    def blocks(layer, proj):
+    def normed_of(layer, h):
+        return (h * rms(h) * params[layer][0]).astype(BF16)
+
+    def project(layer, normed, before):
+        proj, halo = project_mm(normed, normed_of(layer, before.astype(F32)), own_in, other_in, flags[layer], 1664)
+        return proj, halo[8:, INNER : INNER + CONVD]
+
+    def blocks(layer, proj, halo):
         _, taps, hp, _ = params[layer]
-        halo = shifted(proj[ROWS - 8 :, INNER : INNER + CONVD], 1, n)
-        return halo, front(proj, halo, taps, hp)
+        return front(proj, halo, taps, hp)
 
     def finish(layer, h, proj, parts, carried):
-        values, _, _, step, cum, cumt, _, c, _, g, _ = parts
-        y, gated_low = mix(g, step, cum, cumt, values, proj, c, carried, params[layer][3])
-        return y, gated_low, h + mm(gated_low, own_out, other_out, flags[layer], False, 768)
-
-    def by_owner(gated_low):
-        width = INNER // n
-        return gated_low.reshape(ROWS, planes, PLANE, width).transpose(0, 2, 1, 3).reshape(ROWS, INNER)
-
+        values, _, _, step, cum, cumt, _, c, _, g, _ = parts[:11]
+        y, gated_low, owned = mix(g, step, cum, cumt, values, proj, c, carried, params[layer][3], n)
+        return y, owned, h + mm(gated_low, own_out, other_out, flags[layer], False, 768)
+
+    x_0 = mine(inputs)
+    before_0 = shifted(x_0[ROWS - 16 :], 1, n)
     d_out_1 = mine(cotangent)
-    lows_1 = copies_of(d_out_1, n)
-    h_0 = mine(inputs).astype(F32)
-    normed_0, proj_0 = project(0, h_0)
-    proj_0 = tied(proj_0, *lows_1)
-    halo_0, parts_0 = blocks(0, proj_0)
+    h_0 = x_0.astype(F32)
+    normed_0 = normed_of(0, h_0)
+    normed_0, lows_1 = arrived(normed_0, copies_of(d_out_1, n))
+    proj_0, halo_0 = project(0, normed_0, before_0)
+    other_out = swap(tied(own_out, proj_0))
+    parts_0 = blocks(0, proj_0, halo_0)
     carried_0 = exchange(parts_0[1], parts_0[2], n, False)
     normeds_0 = copies_of(tied(normed_0, carried_0), n)
-    y_0, gated_0, out_0 = finish(0, h_0, proj_0, parts_0, carried_0)
+    y_0, owned_0, out_0 = finish(0, h_0, proj_0, parts_0, carried_0)
     act_0 = out_0.astype(BF16)
 
+    before_1 = shifted(act_0[ROWS - 16 :], 1, n)
     h_1 = act_0.astype(F32)
-    normed_1, proj_1 = project(1, h_1)
-    proj_1 = tied(proj_1, *normeds_0)
-    halo_1, parts_1 = blocks(1, proj_1)
-    gateds_0 = pieces_of(by_owner(tied(gated_0, halo_1)), n)
-    carried_1 = exchange(tied(parts_1[1], *gateds_0), parts_1[2], n, False)
-    normeds_1 = copies_of(tied(normed_1, carried_1), n)
-    y_1, gated_1, out_1 = finish(1, h_1, proj_1, parts_1, carried_1)
+    normed_1 = normed_of(1, h_1)
+    normeds_1 = copies_of(tied(normed_1, before_1), n)
+    proj_1, halo_1 = project(1, normed_1, before_1)
+    parts_1 = blocks(1, proj_1, halo_1)
+    carried_1 = exchange(parts_1[1], parts_1[2], n, False)
+    carried_1, normeds_0, normeds_1 = arrived(carried_1, normeds_0, normeds_1)
+    y_1, owned_1, out_1 = finish(1, h_1, proj_1, parts_1, carried_1)
     act_1 = out_1.astype(BF16)
 
-    def gate_side(layer, d_low, y, proj, parts):
+    def gate_side(layer, d_low, y, proj, parts, *spread):
         d_gated_low = mm(d_low, own_out, other_out, flags[layer], True, 1024)
-        return gate_back(d_gated_low, y, proj, parts[4], parts[8], params[layer][3])
-
-    def core_side(layer, proj, halo, parts, y, dy, carried, late):
+        return gate_back(d_gated_low, y, proj, parts[4], parts[8], params[layer][3], *spread)
+
+    def core_side(layer, proj, halo, parts, y, dy, carried, late, *spread):
         _, taps, hp, lp = params[layer]
-        _, _, _, step, cum, cumt, b, c, _, _, gt = parts
-        return core_back(proj, halo, taps, hp, step, cum, cumt, gt, b, c, y, dy, carried, late, lp)
+        _, _, _, step, cum, cumt, b, c, _, _, gt = parts[:11]
+        return core_back(proj, halo, taps, hp, step, cum, cumt, gt, b, c, y, dy, carried, late, lp, *spread)
 
     def conv_side(layer, back):
-        dx, dbc, tail, tailbc, head, headbc, gtaps, gtapsbc, d_raw, heads = back
-        w = params[layer][1]
-        a = shifted(jnp.concatenate([head, headbc], axis=1), -1, n)
+        rest, tail, head = back[:3]
+        w = jnp.concatenate([params[layer][1], jnp.zeros((8, REST - CONVD), F32)], axis=1)
+        a = shifted(head, -1, n)
         fix = jnp.concatenate(
             [
-                jnp.zeros((5, CONVD), F32),
+                jnp.zeros((13, REST), F32),
                 w[0:1] * a[0:1],
                 w[0:1] * a[1:2] + w[1:2] * a[0:1],
                 w[0:1] * a[2:3] + w[1:2] * a[1:2] + w[2:3] * a[0:1],
             ],
             axis=0,
         )
-        low = (jnp.concatenate([tail, tailbc], axis=1) + fix).astype(BF16)
-        main = jnp.concatenate([dx[: ROWS - 8], dbc[: ROWS - 8]], axis=1)
-        d_conv = jnp.concatenate([main, low], axis=0)
-        return d_conv, d_raw[:, :HEADS]
-
-    def norm_side(layer, h, d_out, d_proj):
+        return lax.dynamic_update_slice(rest, (tail + fix).astype(BF16), (ROWS - 16, 0))
+
+    def norm_side(layer, h, d_out, d_gate, rest):
         norm_g = params[layer][0]
-        d_normed = mm(d_proj, own_in, other_in, flags[layer], False, 512)
+        d_normed = back_mm(d_gate, rest, own_in, other_in, flags[layer], 512)
         r = rms(h)
         v = d_normed * norm_g
         d_h = d_out + r * (v - h * (r * r * jnp.mean(v * h, axis=-1, keepdims=True)))
         return d_h, jnp.sum(d_normed * h * r, axis=0)
 
     def small_of(norm_gain_grad, back, gate_gain):
-        taps_all = jnp.concatenate([back[6], back[7]], axis=1)
-        heads = back[9]
+        taps_all, heads = back[3][:, :CONVD], back[4]
         return jnp.concatenate(
             [
                 norm_gain_grad, taps_all[:CONV].reshape(-1), taps_all[CONV],
@@ -941,40 +1124,42 @@
             ]
         )
 
-    def padded(d_conv, d_raw):
-        pad = jnp.zeros((ROWS, REST - CONVD - HEADS), BF16)
-        return jnp.concatenate([d_conv, d_raw, pad], axis=1)
-
-    dy_1, d_gate_1, gain_1, d_carried_1 = gate_side(1, d_out_1, y_1, proj_1, parts_1)
-    late_1 = exchange(tied(d_carried_1, *normeds_1), parts_1[2], n, True)
-    gates_1 = pieces_of(tied(d_gate_1, late_1), n)
-    gateds_1 = pieces_of(by_owner(tied(gated_1, late_1)), n)
-    back_1 = core_side(1, proj_1, halo_1, parts_1, y_1, dy_1, carried_1, late_1)
-    outw_1 = partial_grad(tied_list(gateds_1, back_1[0]), lows_1)
-    outw_1 = plane_rows(outw_1, n)
-    gatew_1 = partial_grad(normeds_1, tied_list(gates_1, back_1[0]))
-    d_conv_1, d_raw_1 = conv_side(1, back_1)
-    rests_1 = pieces_of(padded(d_conv_1, d_raw_1), n)
-    d_proj_1 = jnp.concatenate([tied(d_gate_1, gatew_1), d_conv_1, d_raw_1], axis=1)
-    gatew_1 = plane_rows(gatew_1, n)
-    d_1, ng_1 = norm_side(1, h_1, d_out_1.astype(F32), d_proj_1)
+    dy_1, d_gate_1, gain_1, d_carried_1, gateds_0 = gate_side(
+        1, tied(d_out_1, carried_1), y_1, proj_1, parts_1, (owned_0,), 4
+    )
+    late_1 = exchange(d_carried_1, parts_1[2], n, True)
+    back_1 = core_side(
+        1, proj_1, halo_1, parts_1, y_1, dy_1, carried_1, late_1, (d_gate_1, owned_1), 5
+    )
+    gates_1, gateds_1 = back_1[5:]
+    outw_1 = partial_grad(gateds_1, lows_1)
+    gatew_1 = partial_grad(normeds_1, gates_1)
+    rest_1 = conv_side(1, back_1)
+    rest_1 = tied(rest_1, outw_1, gatew_1)
+    outw_1, gatew_1 = plane_rows(outw_1, n), plane_rows(gatew_1, n)
+    d_1, ng_1 = norm_side(1, h_1, d_out_1.astype(F32), d_gate_1, rest_1)
 
     d_out_0 = d_1.astype(BF16)
-    lows_0 = copies_of(tied(d_out_0, *rests_1), n)
-    dy_0, d_gate_0, gain_0, d_carried_0 = gate_side(0, d_out_0, y_0, proj_0, parts_0)
+    dy_0, d_gate_0, gain_0, d_carried_0, rests_1 = gate_side(0, d_out_0, y_0, proj_0, parts_0, (rest_1,), 6)
     restw_1 = partial_grad(normeds_1, rests_1)
     late_0 = exchange(tied(d_carried_0, restw_1), parts_0[2], n, True)
     restw_1 = plane_rows(restw_1, n)
-    gates_0 = pieces_of(tied(d_gate_0, late_0, *lows_0), n)
-    outw_0 = partial_grad(gateds_0, tied_list(lows_0, late_0))
-    back_0 = core_side(0, proj_0, halo_0, parts_0, y_0, dy_0, carried_0, tied(late_0, outw_0))
-    outw_0 = plane_rows(outw_0, n)
-    gatew_0 = partial_grad(normeds_0, tied_list(gates_0, back_0[0]))
-    d_conv_0, d_raw_0 = conv_side(0, back_0)
-    rests_0 = pieces_of(padded(d_conv_0, d_raw_0), n)
-    d_proj_0 = jnp.concatenate([tied(d_gate_0, gatew_0), d_conv_0, d_raw_0], axis=1)
+    lows_0 = copies_of(tied(d_out_0, late_0), n)
+    back_0 = core_side(
+        0, proj_0, halo_0, parts_0, y_0, dy_0, carried_0, late_0, (d_gate_0,), 7
+    )
+    gates_0, lows_0 = arrived(back_0[5], lows_0)
+    gatew_0 = partial_grad(normeds_0, gates_0)
+    outw_0 = plane_rows(partial_grad(gateds_0, lows_0), n)
+    rest_0 = conv_side(0, back_0)
+    rest_0 = tied(rest_0, gatew_0)
     gatew_0 = plane_rows(gatew_0, n)
-    d_0, ng_0 = norm_side(0, h_0, d_out_0.astype(F32), d_proj_0)
+    spot = place % PLANE
+    width = REST // PLANE
+    pieces = [lax.dynamic_slice_in_dim(rest_0, (spot + k) % PLANE * width, width, 1) for k in range(PLANE)]
+    rests_0 = pieces[:1] + [lax.ppermute(pieces[k], "seq", plane_route(k, n)) for k in range(1, PLANE)]
+    d_0, ng_0 = norm_side(0, h_0, d_out_0.astype(F32), d_gate_0, rest_0)
+    ng_0, rests_0 = arrived(ng_0, rests_0)
     restw_0 = plane_rows(partial_grad(normeds_0, rests_0), n)
 
     g_in, g_out, acts, input_grads = settle(

time: 761 us -> 707 us (0.929)
  local copies, waits for them, and re-layouts: 109 us -> 62.3 us
  Pallas kernels: 399 us -> 438 us
  starting transfers between devices: 68.6 us -> 36.2 us
  waiting for transfers between devices: 86.5 us -> 76 us
  other arithmetic: 26 us -> 17.5 us
    pallas_call x8 -> x12, Pallas kernels: 151 us -> 243 us  [the longest x2 78.4 us: core_back(): pl.pallas_call(body, grid=(STEPS + 2,), in_specs=[lanes(ROWS, STEPS), fix...]
    pallas_call x8 -> x4, Pallas kernels: 80.2 us -> 27.9 us  [mm(): pl.pallas_call(functools.partial(mm_kernel, nt=nt), grid_spec=pltpu.Prefe...]
    ppermute x4, waiting for transfers between devices: 1.34 us -> 34.4 us  [shifted(): lax.ppermute(value, 'seq', [(i, i + distance) for i in range(n) if 0 <= i...]
    ppermute x18 -> x3, waiting for transfers between devices: 27.5 us -> 0.15 us  [per_device(): lax.ppermute(pieces[k], 'seq', plane_route(k, n))]
    ppermute x18 -> x3, starting transfers between devices: 29.4 us -> 5.3 us  [per_device(): lax.ppermute(pieces[k], 'seq', plane_route(k, n))]
    reduce_scatter x6, waiting for transfers between devices: 1.7 us -> 16.6 us  [plane_rows(): lax.psum_scatter(partial, 'seq', scatter_dimension=0, axis_index_groups=c...]
    ppermute x10, waiting for transfers between devices: 19.8 us -> 5.55 us  [swap(): return lax.ppermute(value, 'section', [(0, 1), (1, 0)])]
    concatenate x9 -> x0, other arithmetic: 13 us -> none  [the longest x3 6.02 us: partial_grad(): jnp.concatenate(right, axis=0)]
  transfers between devices with their start and end apart: 54 -> 39, of which waited for: 15 -> 11; matrix products, arithmetic and copies ran while one was open for 18% -> 11% of each run, Pallas kernels for 29% -> 41%
where the time goes in v4:
time: 707 us; the launch traced here: 696 us
  Pallas kernels  438 us (62%)
  waiting for transfers between devices  76 us (11%)
  local copies, waits for them, and re-layouts  62.3 us (9%)
  matrix products  49.2 us (7%)
  starting transfers between devices  36.2 us (5%)
  other arithmetic  17.5 us (2%)
  between operations  16.3 us (2%)
    pallas_call x4, Pallas kernels, exchange(): pl.pallas_call(functools.partial(exchange_kernel, n, rev), out_shape=sds(...  148 us
    pallas_call x2, Pallas kernels, core_back(): pl.pallas_call(body, grid=(STEPS + 2,), in_specs=[lanes(ROWS, STEPS), fix...  78.4 us
    pallas_call x2, Pallas kernels, gate_back(): pl.pallas_call(body, grid=(2, STEPS), in_specs=[first(ROWS), first(ROWS),...  50.1 us
    dot_general x12, matrix products, part(): lax.dot_general(left, cols, (((0, 1), (0, 1)), ((), ())), preferred_eleme...  49.2 us
    unnamed x248, local copies, waits for them, and re-layouts  44.9 us
    ppermute x4, waiting for transfers between devices, shifted(): lax.ppermute(value, 'seq', [(i, i + distance) for i in range(n) if 0 <= i...  34.4 us
    pallas_call x2, Pallas kernels, project_mm(): pl.pallas_call(project_kernel, grid_spec=pltpu.PrefetchScalarGridSpec(num...  34.4 us
    pallas_call x2, Pallas kernels, mix(): pl.pallas_call(functools.partial(mix_kernel, n), grid=(STEPS,), in_specs=...  29.6 us
  transfers between devices with their start and end apart: 39, of which 11 were waited for; matrix products, arithmetic and copies ran while one was open for 11% of the time, Pallas kernels for 41%

profile of v4, /device:TPU:0, one launch (start us, length us, event | category | flops | bytes accessed | tf_op | source)
XLA Modules:
  0.0 695.6 jit_solution(12828098820369996786)
XLA Ops:
  19.8 28.2 %collective-permute-done.4 = bf16[16,1536]{1,0:T(8,128)(2,1)S(1)} collective-permute-done((bf16[16,1536]{1,0:T(8,128)(2,1)S(1)}, bf16[16,1536]{1,0:T(8,128)(2,1)S(1)}, u32[]{:S(2)}, u32[]{:S(2)}) %collective-permute-start.4) | collective-permute-done | bytes 49184 | tf_op jit(solution)/shard_map/ppermute | solution.py:954
  49.8 17.1 %shard_map.194 = (f32[256,6448]{1,0:T(8,128)}, f32[16,6448]{1,0:T(8,128)S(1)}) custom-call(s32[1]{0:T(128)} %bitcast.2.flag_ref, bf16[256,1536]{1,0:T(8,128)(2,1)S(1)} %fusion.22.x_ref, bf16[16,1536]{1,0:T(8,128)(2,1)S(1)} %fusion.50.before_ref, bf16[6448,1536]{1,0:T(8,128)(2,1)} %bitcast.154, bf16[6448,1536]{1,0:T(8,128)(2,1)} %collective-permute-done.5.other_ref), custom_call_target="tpu_custom_call" | custom-call | flops 5070913536 | bytes 19808256 | tf_op jit(solution)/shard_map/pallas_call | solution.py:275
  68.5 13.2 %shard_map.195 = (f32[256,3072]{1,0:T(8,128)}, f32[128,3072]{1,0:T(8,128)S(1)}, f32[8,3072]{1,0:T(8,128)S(1)}, bf16[256,384]{1,0:T(8,128)(2,1)S(1)}, bf16[256,38...) custom-call(f32[256,6448]{1,0:T(8,128)} %get-tuple-element.103.x_ref, ...), custom_call_target="tpu_custom_call" | custom-call | flops 1000000000 | bytes 10485760 | tf_op jit(solution)/shard_map/pallas_call | solution.py:400
  82.4 42.1 %shard_map.196.car_ref.refs_16_ = f32[128,3072]{1,0:T(8,128)S(1)} custom-call(f32[128,3072]{1,0:T(8,128)S(1)} %get-tuple-element.111.s_ref, f32[8,3072]{1,0:T(8,128)S(1)} %get-tuple-element.112.d_ref), custom_call_target="tpu_custom_call" | custom-call | tf_op jit(solution)/shard_map/pallas_call | solution.py:539
  127.5 14.7 %shard_map.197 = (f32[256,3072]{1,0:T(8,128)}, bf16[256,3072]{1,0:T(8,128)(2,1)S(1)}, bf16[256,3072]{1,0:T(8,128)(2,1)S(1)}) custom-call(f32[256,256]{1,0:T(8,128)S(1)} %get-tuple-element.105.g_ref, bf16[256,384]{1,0:T(8,128)(2,1)S(1)} %get-tuple-element.106.step_ref.refs_8_, bf16[256,384]{1,0:T(8,128)(2,1)S(1)} %get-tuple-element.107.cum_ref.refs_3_.refs_9_, ...), custom_call_target="tpu_custom_call" | custom-call | flops 3000000000 | bytes 14680064 | tf_op jit(solution)/shard_map/pallas_call | solution.py:623
  142.2 6.9 shard_map.198
  164.7 17.2 %shard_map.199 = (f32[256,6448]{1,0:T(8,128)}, f32[16,6448]{1,0:T(8,128)S(1)}) custom-call(s32[1]{0:T(128)} %bitcast.flag_ref, bf16[256,1536]{1,0:T(8,128)(2,1)S(1)} %fusion.12.x_ref, bf16[16,1536]{1,0:T(8,128)(2,1)S(1)} %fusion.53.before_ref, bf16[6448,1536]{1,0:T(8,128)(2,1)} %bitcast.155, bf16[6448,1536]{1,0:T(8,128)(2,1)} %collective-permute-done.5.other_ref), custom_call_target="tpu_custom_call" | custom-call | flops 5070913536 | bytes 19808256 | tf_op jit(solution)/shard_map/pallas_call | solution.py:275
  182.0 13.2 %shard_map.200 = (f32[256,3072]{1,0:T(8,128)}, f32[128,3072]{1,0:T(8,128)S(1)}, f32[8,3072]{1,0:T(8,128)S(1)}, bf16[256,384]{1,0:T(8,128)(2,1)S(1)}, bf16[256,38...) custom-call(f32[256,6448]{1,0:T(8,128)} %get-tuple-element.115.x_ref, ...), custom_call_target="tpu_custom_call" | custom-call | flops 1000000000 | bytes 10485760 | tf_op jit(solution)/shard_map/pallas_call | solution.py:400
  195.2 38.6 %shard_map.201.car_ref.refs_16_ = f32[128,3072]{1,0:T(8,128)S(1)} custom-call(f32[128,3072]{1,0:T(8,128)S(1)} %get-tuple-element.117.s_ref, f32[8,3072]{1,0:T(8,128)S(1)} %get-tuple-element.118.d_ref), custom_call_target="tpu_custom_call" | custom-call | tf_op jit(solution)/shard_map/pallas_call | solution.py:539
  233.9 15.0 %shard_map.203 = (f32[256,3072]{1,0:T(8,128)}, bf16[256,3072]{1,0:T(8,128)(2,1)S(1)}, bf16[256,3072]{1,0:T(8,128)(2,1)S(1)}) custom-call(f32[256,256]{1,0:T(8,128)S(1)} %get-tuple-element.130.g_ref, bf16[256,384]{1,0:T(8,128)(2,1)S(1)} %get-tuple-element.131.step_ref.refs_8_, bf16[256,384]{1,0:T(8,128)(2,1)S(1)} %get-tuple-element.132.cum_ref.refs_3_.refs_9_, ...), custom_call_target="tpu_custom_call" | custom-call | flops 3000000000 | bytes 14680064 | tf_op jit(solution)/shard_map/pallas_call | solution.py:623
  251.3 6.9 shard_map.202.refs_0_
  259.9 22.2 %shard_map.204 = (f32[256,3072]{1,0:T(8,128)}, bf16[256,3072]{1,0:T(8,128)(2,1)S(1)}, f32[8,3072]{1,0:T(8,128)S(1)}, bf16[128,3072]{1,0:T(8,128)(2,1)S(1)}, bf16[4,256,768]{2,1,0:T(8,128)(2,1)S(1)}) custom-call(f32[256,3072]{1,0:T(8,128)} %copy-done.1, f32[256,3072]{1,0:T(8,128)} %get-tuple-element.136.refs_1_.refs_14_, ...), custom_call_target="tpu_custom_call" | custom-call | flops 1000000000 | bytes 16777216 | tf_op jit(solution)/shard_map/pallas_call | solution.py:693
  283.3 38.7 %shard_map.205.refs_17_ = bf16[128,3072]{1,0:T(8,128)(2,1)S(1)} custom-call(bf16[128,3072]{1,0:T(8,128)(2,1)S(1)} %get-tuple-element.143.s_ref, f32[8,3072]{1,0:T(8,128)S(1)} %get-tuple-element.118.d_ref), custom_call_target="tpu_custom_call" | custom-call | tf_op jit(solution)/shard_map/pallas_call | solution.py:539
  322.0 36.4 %shard_map.206 = (bf16[256,3584]{1,0:T(8,128)(2,1)}, f32[16,3584]{1,0:T(8,128)S(1)}, f32[8,3584]{1,0:T(8,128)}, f32[8,3584]{1,0:T(8,128)S(1)}, f32[8,128]{1,0:T(...) custom-call(f32[256,6448]{1,0:T(8,128)} %get-tuple-element.115.x_ref.bc_ref.raw_ref.gate_ref.refs_2_.refs_0_., ...), custom_call_target="tpu_custom_call" | custom-call | flops 8000000000 | bytes 14680064 | tf_op jit(solution)/shard_map/pallas_call | solution.py:829
  375.5 7.0 %shard_map.213 = f32[256,1536]{1,0:T(8,128)S(1)} custom-call(s32[1]{0:T(128)} %bitcast.flag_ref, bf16[256,3072]{1,0:T(8,128)(2,1)S(1)} %copy-done.33, bf16[3072,1536]{1,0:T(8,128)(2,1)} %bitcast.17.own_ref, bf16[3072,1536]{1,0:T(8,128)(2,1)} %collective-permute-done.6.other_ref), custom_call_target="tpu_custom_call" | custom-call | flops 2415919104 | bytes 9437184 | tf_op jit(solution)/shard_map/pallas_call | solution.py:157
  391.4 11.9 %shard_map.207 = f32[256,1536]{1,0:T(8,128)S(1)} custom-call(s32[1]{0:T(128)} %bitcast.flag_ref, bf16[256,3072]{1,0:T(8,128)(2,1)S(1)} %copy-done.10, bf16[256,3584]{1,0:T(8,128)(2,1)S(1)} %copy-done.6, bf16[6448,1536]{1,0:T(8,128)(2,1)} %bitcast.156, bf16[6448,1536]{1,0:T(8,128)(2,1)} %collective-permute-done.5.other_ref), custom_call_target="tpu_custom_call" | custom-call | flops 5070913536 | bytes 19808256 | tf_op jit(solution)/shard_map/pallas_call | solution.py:315
  406.7 7.0 %shard_map.208.refs_0_ = f32[256,3072]{1,0:T(8,128)S(1)} custom-call(s32[1]{0:T(128)} %bitcast.2.flag_ref, bf16[256,1536]{1,0:T(8,128)(2,1)S(1)} %get-tuple-element.177.x_ref, bf16[3072,1536]{1,0:T(8,128)(2,1)} %bitcast.17.own_ref, bf16[3072,1536]{1,0:T(8,128)(2,1)} %collective-permute-done.6.other_ref), custom_call_target="tpu_custom_call" | custom-call | flops 2415919104 | bytes 9437184 | tf_op jit(solution)/shard_map/pallas_call | solution.py:157
  415.5 27.9 %shard_map.209 = (f32[256,3072]{1,0:T(8,128)}, bf16[256,3072]{1,0:T(8,128)(2,1)S(1)}, f32[8,3072]{1,0:T(8,128)S(1)}, bf16[128,3072]{1,0:T(8,128)(2,1)S(1)}, bf16[4,256,896]{2,1,0:T(8,128)(2,1)S(1)}) custom-call(f32[256,3072]{1,0:T(8,128)} %copy-done.2, f32[256,3072]{1,0:T(8,128)} %get-tuple-element.127.refs_1_.refs_14_, ...), custom_call_target="tpu_custom_call" | custom-call | flops 1000000000 | bytes 16777216 | tf_op jit(solution)/shard_map/pallas_call | solution.py:693
  462.1 28.8 %shard_map.210.refs_17_ = bf16[128,3072]{1,0:T(8,128)(2,1)S(1)} custom-call(bf16[128,3072]{1,0:T(8,128)(2,1)S(1)} %copy-done.39, f32[8,3072]{1,0:T(8,128)S(1)} %copy-done.43), custom_call_target="tpu_custom_call" | custom-call | tf_op jit(solution)/shard_map/pallas_call | solution.py:539
  500.8 42.0 %shard_map.211 = (bf16[256,3584]{1,0:T(8,128)(2,1)}, f32[16,3584]{1,0:T(8,128)S(1)}, f32[8,3584]{1,0:T(8,128)S(1)}, f32[8,3584]{1,0:T(8,128)S(1)}, f32[8,128]{1,...) custom-call(f32[256,6448]{1,0:T(8,128)} %get-tuple-element.103.x_ref.bc_ref.raw_ref.gate_ref.refs_2_.refs_0_.refs_1_, ...), custom_call_target="tpu_custom_call" | custom-call | flops 8000000000 | bytes 14680064 | tf_op jit(solution)/shard_map/pallas_call | solution.py:829
  574.0 11.8 %shard_map.212 = f32[256,1536]{1,0:T(8,128)S(1)} custom-call(s32[1]{0:T(128)} %bitcast.2.flag_ref, bf16[256,3072]{1,0:T(8,128)(2,1)S(1)} %copy-done.8, bf16[256,3584]{1,0:T(8,128)(2,1)S(1)} %copy-done.5, bf16[6448,1536]{1,0:T(8,128)(2,1)} %bitcast.157, bf16[6448,1536]{1,0:T(8,128)(2,1)} %collective-permute-done.5.other_ref), custom_call_target="tpu_custom_call" | custom-call | flops 5070913536 | bytes 19808256 | tf_op jit(solution)/shard_map/pallas_call | solution.py:315
  625.0 7.6 %collective-permute-done.32 = f32[21392]{0:T(1024)S(1)} collective-permute-done((f32[21392]{0:T(1024)S(1)}, f32[21392]{0:T(1024)S(1)}, u32[]{:S(2)}, u32[]{:S(2)}) %collective-permute-start.32) | collective-permute-done | bytes 85600 | tf_op jit(solution)/shard_map/ppermute | solution.py:1172
  636.0 16.6 %reduce-scatter.9.cloned.1.call-done.re0 = bf16[384,448]{1,0:T(8,128)(2,1)} async-done(((bf16[1536,448]{1,0:T(8,128)(2,1)}), bf16[384,448]{1,0:T(8,128)(2,1)}) %reduce-scatter.9.cloned.1.call-update) | async-done | bytes 344080 | tf_op jit(solution)/shard_map/reduce_scatter | solution.py:992
  662.4 19.4 %shard_map.214 = (f32[96,6448]{1,0:T(8,128)S(1)}, f32[192,1536]{1,0:T(8,128)S(1)}, bf16[2,256,1536]{2,1,0:T(8,128)(2,1)S(1)}, f32[2,256,1536]{2,1,0:T(8,128)}) custom-call(bf16[384,384]{1,0:T(8,128)(2,1)S(1)} %copy-done.48, bf16[384,448]{1,0:T(8,128)(2,1)S(1)} %copy-done.45, bf16[384,384]{1,0:T(8,128)(2,1)S(1)} %copy-done.46, ...), custom_call_target="tpu_custom_call" | custom-call | tf_op jit(solution)/shard_map/pallas_call | solution.py:930
  (436 shorter events, 188.8 us)
Async XLA Ops:
  7.3 628.7 %reduce-scatter.11.cloned.1.call-start = ((), (), s32[]{:S(2)}) async-start(), calls=%async_computation.8 | async-start | bytes 1474560 | tf_op jit(solution)/shard_map/reduce_scatter | solution.py:992
  7.3 42.3 %collective-permute-start.5 = (bf16[6448,1536]{1,0:T(8,128)(2,1)}, bf16[6448,1536]{1,0:T(8,128)(2,1)}, u32[]{:S(2)}, u32[]{:S(2)}) collective-permute-start(bf16[6448,1536]{1,0:T(8,128)(2,1)} %bitcast.153), channel_id=1, source_target_pairs={{0,16},{16,0},{1,17},{17,1},{2,18},{18,2},{3,19},{19,3},{4,20},{20... | collective-permute-start | bytes 59424776 | tf_op jit(solution)/shard_map/ppermute | solution.py:950
  9.0 40.6 %collective-permute-start.3 = (bf16[256,1536]{1,0:T(8,128)(2,1)S(1)}, bf16[256,1536]{1,0:T(8,128)(2,1)}, u32[]{:S(2)}, u32[]{:S(2)}) collective-permute-start(bf16[256,1536]{1,0:T(8,128)(2,1)S(1)} %dynamic-slice_bitcast_fusion.x_ref), channel_id=1, source_target_pairs={{0,3},{1,0},{2,1},{3,2},{4,7},{5,4},{6,5},{7,6},{8,11},{9,8},{10,9... | collective-permute-start | bytes 2359304 | tf_op jit(solution)/shard_map/ppermute | solution.py:970
  12.7 37.0 %collective-permute-start.2 = (bf16[256,1536]{1,0:T(8,128)(2,1)S(1)}, bf16[256,1536]{1,0:T(8,128)(2,1)}, u32[]{:S(2)}, u32[]{:S(2)}) collective-permute-start(bf16[256,1536]{1,0:T(8,128)(2,1)S(1)} %dynamic-slice_bitcast_fusion.x_ref), channel_id=1, source_target_pairs={{0,2},{1,3},{2,0},{3,1},{4,6},{5,7},{6,4},{7,5},{8,10},{9,11},{10,... | collective-permute-start | bytes 2359304 | tf_op jit(solution)/shard_map/ppermute | solution.py:970
  13.2 36.5 %collective-permute-start.1 = (bf16[256,1536]{1,0:T(8,128)(2,1)S(1)}, bf16[256,1536]{1,0:T(8,128)(2,1)}, u32[]{:S(2)}, u32[]{:S(2)}) collective-permute-start(bf16[256,1536]{1,0:T(8,128)(2,1)S(1)} %dynamic-slice_bitcast_fusion.x_ref), channel_id=1, source_target_pairs={{0,1},{1,2},{2,3},{3,0},{4,5},{5,6},{6,7},{7,4},{8,9},{9,10},{10,1... | collective-permute-start | bytes 2359304 | tf_op jit(solution)/shard_map/ppermute | solution.py:970
  14.6 33.4 %collective-permute-start.4 = (bf16[16,1536]{1,0:T(8,128)(2,1)S(1)}, bf16[16,1536]{1,0:T(8,128)(2,1)S(1)}, u32[]{:S(2)}, u32[]{:S(2)}) collective-permute-start(bf16[16,1536]{1,0:T(8,128)(2,1)S(1)} %dynamic-slice_bitcast_fusion.1), channel_id=1, source_target_pairs={{0,1},{1,2},{2,3},{3,4},{4,5},{5,6},{6,7},{7,8},{8,9},{9,10},{10,1... | collective-permute-start | bytes 147464 | tf_op jit(solution)/shard_map/ppermute | solution.py:954
  67.0 75.2 %collective-permute-start.6 = (bf16[3072,1536]{1,0:T(8,128)(2,1)}, bf16[3072,1536]{1,0:T(8,128)(2,1)}, u32[]{:S(2)}, u32[]{:S(2)}) collective-permute-start(bf16[3072,1536]{1,0:T(8,128)(2,1)} %bitcast.17.own_ref), channel_id=1, source_target_pairs={{0,16},{16,0},{1,17},{17,1},{2,18},{18,2},{3,19},{19,3},{4,20},{20... | collective-permute-start | bytes 28311560 | tf_op jit(solution)/shard_map/ppermute | solution.py:950
  124.4 40.1 %collective-permute-start.10 = (bf16[256,1536]{1,0:T(8,128)(2,1)S(1)}, bf16[256,1536]{1,0:T(8,128)(2,1)S(1)}, u32[]{:S(2)}, u32[]{:S(2)}) collective-permute-start(bf16[256,1536]{1,0:T(8,128)(2,1)S(1)} %copy-done.17), channel_id=1, source_target_pairs={{0,3},{1,0},{2,1},{3,2},{4,7},{5,4},{6,5},{7,6},{8,11},{9,8},{10,9... | collective-permute-start | bytes 2359304 | tf_op jit(solution)/shard_map/ppermute | solution.py:970
  126.4 107.5 %collective-permute-start.9 = (bf16[256,1536]{1,0:T(8,128)(2,1)S(1)}, bf16[256,1536]{1,0:T(8,128)(2,1)S(1)}, u32[]{:S(2)}, u32[]{:S(2)}) collective-permute-start(bf16[256,1536]{1,0:T(8,128)(2,1)S(1)} %copy-done.17), channel_id=1, source_target_pairs={{0,2},{1,3},{2,0},{3,1},{4,6},{5,7},{6,4},{7,5},{8,10},{9,11},{10,... | collective-permute-start | bytes 2359304 | tf_op jit(solution)/shard_map/ppermute | solution.py:970
  126.6 107.2 %collective-permute-start.8 = (bf16[256,1536]{1,0:T(8,128)(2,1)S(1)}, bf16[256,1536]{1,0:T(8,128)(2,1)S(1)}, u32[]{:S(2)}, u32[]{:S(2)}) collective-permute-start(bf16[256,1536]{1,0:T(8,128)(2,1)S(1)} %copy-done.17), channel_id=1, source_target_pairs={{0,1},{1,2},{2,3},{3,0},{4,5},{5,6},{6,7},{7,4},{8,9},{9,10},{10,1... | collective-permute-start | bytes 2359304 | tf_op jit(solution)/shard_map/ppermute | solution.py:970
  160.4 73.4 %collective-permute-start.13 = (bf16[256,1536]{1,0:T(8,128)(2,1)S(1)}, bf16[256,1536]{1,0:T(8,128)(2,1)S(1)}, u32[]{:S(2)}, u32[]{:S(2)}) collective-permute-start(bf16[256,1536]{1,0:T(8,128)(2,1)S(1)} %fusion.12.x_ref), channel_id=1, source_target_pairs={{0,3},{1,0},{2,1},{3,2},{4,7},{5,4},{6,5},{7,6},{8,11},{9,8},{10,9... | collective-permute-start | bytes 2359304 | tf_op jit(solution)/shard_map/ppermute | solution.py:970
  162.4 71.5 %collective-permute-start.12 = (bf16[256,1536]{1,0:T(8,128)(2,1)S(1)}, bf16[256,1536]{1,0:T(8,128)(2,1)S(1)}, u32[]{:S(2)}, u32[]{:S(2)}) collective-permute-start(bf16[256,1536]{1,0:T(8,128)(2,1)S(1)} %fusion.12.x_ref), channel_id=1, source_target_pairs={{0,2},{1,3},{2,0},{3,1},{4,6},{5,7},{6,4},{7,5},{8,10},{9,11},{10,... | collective-permute-start | bytes 2359304 | tf_op jit(solution)/shard_map/ppermute | solution.py:970
  164.5 69.4 %collective-permute-start.11 = (bf16[256,1536]{1,0:T(8,128)(2,1)S(1)}, bf16[256,1536]{1,0:T(8,128)(2,1)}, u32[]{:S(2)}, u32[]{:S(2)}) collective-permute-start(bf16[256,1536]{1,0:T(8,128)(2,1)S(1)} %fusion.12.x_ref), channel_id=1, source_target_pairs={{0,1},{1,2},{2,3},{3,0},{4,5},{5,6},{6,7},{7,4},{8,9},{9,10},{10,1... | collective-permute-start | bytes 2359304 | tf_op jit(solution)/shard_map/ppermute | solution.py:970
  374.0 261.9 %reduce-scatter.17.cloned.1.call-start = ((), (), s32[]{:S(2)}) async-start(), calls=%async_computation.11 | async-start | bytes 1474560 | tf_op jit(solution)/shard_map/reduce_scatter | solution.py:992
  388.3 247.7 %reduce-scatter.13.cloned.1.call-start = ((), (), s32[]{:S(2)}) async-start(), calls=%async_computation.9 | async-start | bytes 1966080 | tf_op jit(solution)/shard_map/reduce_scatter | solution.py:992
  491.8 51.1 %collective-permute-start.20 = (bf16[256,1536]{1,0:T(8,128)(2,1)S(1)}, bf16[256,1536]{1,0:T(8,128)(2,1)}, u32[]{:S(2)}, u32[]{:S(2)}) collective-permute-start(bf16[256,1536]{1,0:T(8,128)(2,1)S(1)} %get-tuple-element.177.x_ref), channel_id=1, source_target_pairs={{0,3},{1,0},{2,1},{3,2},{4,7},{5,4},{6,5},{7,6},{8,11},{9,8},{10,9... | collective-permute-start | bytes 2359304 | tf_op jit(solution)/shard_map/ppermute | solution.py:970
  491.8 51.1 %collective-permute-start.19 = (bf16[256,1536]{1,0:T(8,128)(2,1)S(1)}, bf16[256,1536]{1,0:T(8,128)(2,1)}, u32[]{:S(2)}, u32[]{:S(2)}) collective-permute-start(bf16[256,1536]{1,0:T(8,128)(2,1)S(1)} %get-tuple-element.177.x_ref), channel_id=1, source_target_pairs={{0,2},{1,3},{2,0},{3,1},{4,6},{5,7},{6,4},{7,5},{8,10},{9,11},{10,... | collective-permute-start | bytes 2359304 | tf_op jit(solution)/shard_map/ppermute | solution.py:970
  493.2 49.7 %collective-permute-start.18 = (bf16[256,1536]{1,0:T(8,128)(2,1)S(1)}, bf16[256,1536]{1,0:T(8,128)(2,1)}, u32[]{:S(2)}, u32[]{:S(2)}) collective-permute-start(bf16[256,1536]{1,0:T(8,128)(2,1)S(1)} %get-tuple-element.177.x_ref), channel_id=1, source_target_pairs={{0,1},{1,2},{2,3},{3,0},{4,5},{5,6},{6,7},{7,4},{8,9},{9,10},{10,1... | collective-permute-start | bytes 2359304 | tf_op jit(solution)/shard_map/ppermute | solution.py:970
  493.9 142.1 %reduce-scatter.7.cloned.1.call-start = ((), (), s32[]{:S(2)}) async-start(), calls=%async_computation.6 | async-start | bytes 1474560 | tf_op jit(solution)/shard_map/reduce_scatter | solution.py:992
  557.1 78.9 %reduce-scatter.15.cloned.1.call-start = ((), (), s32[]{:S(2)}) async-start(), calls=%async_computation.10 | async-start | bytes 1474560 | tf_op jit(solution)/shard_map/reduce_scatter | solution.py:992
  561.2 25.8 %collective-permute-start.25 = (bf16[256,896]{1,0:T(8,128)(2,1)}, bf16[256,896]{1,0:T(8,128)(2,1)}, u32[]{:S(2)}, u32[]{:S(2)}) collective-permute-start(bf16[256,896]{1,0:T(8,128)(2,1)} %get-tuple-element.201), channel_id=1, source_target_pairs={{0,3},{1,0},{2,1},{3,2},{4,7},{5,4},{6,5},{7,6},{8,11},{9,8},{10,9... | collective-permute-start | bytes 1376264 | tf_op jit(solution)/shard_map/ppermute | solution.py:1160
  564.8 22.4 %collective-permute-start.24 = (bf16[256,896]{1,0:T(8,128)(2,1)}, bf16[256,896]{1,0:T(8,128)(2,1)}, u32[]{:S(2)}, u32[]{:S(2)}) collective-permute-start(bf16[256,896]{1,0:T(8,128)(2,1)} %get-tuple-element.202), channel_id=1, source_target_pairs={{0,2},{1,3},{2,0},{3,1},{4,6},{5,7},{6,4},{7,5},{8,10},{9,11},{10,... | collective-permute-start | bytes 1376264 | tf_op jit(solution)/shard_map/ppermute | solution.py:1160
  565.4 21.7 %collective-permute-start.23 = (bf16[256,896]{1,0:T(8,128)(2,1)}, bf16[256,896]{1,0:T(8,128)(2,1)}, u32[]{:S(2)}, u32[]{:S(2)}) collective-permute-start(bf16[256,896]{1,0:T(8,128)(2,1)} %get-tuple-element.203), channel_id=1, source_target_pairs={{0,1},{1,2},{2,3},{3,0},{4,5},{5,6},{6,7},{7,4},{8,9},{9,10},{10,1... | collective-permute-start | bytes 1376264 | tf_op jit(solution)/shard_map/ppermute | solution.py:1160
  570.8 81.8 %reduce-scatter.9.cloned.1.call-start = ((), (), s32[]{:S(2)}) async-start(), calls=%async_computation.7 | async-start | bytes 1966080 | tf_op jit(solution)/shard_map/reduce_scatter | solution.py:992
  (137 other events, 1990.3 us)
Sparse Core Ops, SparseCore 0:
  374.1 28.2 reduce-scatter.10
  404.7 27.8 reduce-scatter.16
  494.0 33.3 reduce-scatter.12
  557.3 28.4 reduce-scatter.6
  587.9 27.8 reduce-scatter.14
  618.0 34.5 reduce-scatter.8

commit v5 on v4

--- a/solution.py
+++ b/solution.py
@@ -255,10 +255,11 @@
     )
 
 
-def project_kernel(flag_ref, x_ref, before_ref, own_ref, other_ref, o_ref, halo_ref):
+def project_kernel(flag_ref, x_ref, own_ref, other_ref, o_ref, halo_ref):
     def product(w_ref):
-        o_ref[...] = dot_nt(x_ref[...], w_ref[...])
-        halo_ref[...] = dot_nt(before_ref[...], w_ref[...])
+        both = dot_nt(x_ref[...], w_ref[...])
+        o_ref[...] = both[0:ROWS]
+        halo_ref[...] = both[ROWS : ROWS + 16]
 
     @pl.when(flag_ref[0] == 1)
     def _():
@@ -272,14 +273,14 @@
 def project_mm(x, before, own, other, flag, tile):
     rows, depth = x.shape
     width = own.shape[0]
+    x = jnp.concatenate([x, before], axis=0)
     return pl.pallas_call(
         project_kernel,
         grid_spec=pltpu.PrefetchScalarGridSpec(
             num_scalar_prefetch=1,
             grid=(pl.cdiv(width, tile),),
             in_specs=[
-                pl.BlockSpec((rows, depth), lambda j, f: (0, 0)),
-                pl.BlockSpec((16, depth), lambda j, f: (0, 0)),
+                pl.BlockSpec((rows + 16, depth), lambda j, f: (0, 0)),
                 pl.BlockSpec((tile, depth), lambda j, f: (j * f[0], 0)),
                 pl.BlockSpec((tile, depth), lambda j, f: (j * (1 - f[0]), 0)),
             ],
@@ -293,7 +294,7 @@
         cost_estimate=pl.CostEstimate(
             flops=2 * rows * depth * width, bytes_accessed=2 * depth * width, transcendentals=0
         ),
-    )(flag, x, before, own, other)
+    )(flag, x, own, other)
 
 
 def back_kernel(flag_ref, gate_ref, rest_ref, own_ref, other_ref, o_ref):
@@ -849,15 +850,93 @@
     )
 
 
+def row_copies(layer, gate, rest, gate_in, rest_in, sems, spot, base, core, mine):
+    send_g, recv_g, send_r, recv_r = sems
+    rows = gate_in.shape[1]
+    copies = []
+    for k in range(1 if mine else 0, PLANE):
+        peer = lax.rem(spot + k, PLANE)
+        block = pl.ds(pl.multiple_of(peer * rows, rows), rows)
+        at = 2 * k + core
+        for src, dst, send, recv in ((gate, gate_in, send_g, recv_g), (rest, rest_in, send_r, recv_r)):
+            copies.append(
+                pltpu.make_async_remote_copy(
+                    src_ref=src.at[block], dst_ref=dst.at[2 * spot + core], send_sem=send.at[at],
+                    recv_sem=recv.at[at], device_id=(layer, base + peer), device_id_type=MESH,
+                )
+            )
+    return copies
+
+
+def keep_rows(layer, gate, rest, gate_in, rest_in, spot):
+    rows = gate_in.shape[1]
+    block = pl.ds(pl.multiple_of(spot * rows, rows), rows)
+    gate_in[2 * spot + layer] = gate[block, :]
+    rest_in[2 * spot + layer] = rest[block, :]
+
+
+def wait_rows(layer, gate, rest, gate_in, rest_in, sems, spot, base):
+    for core in range(2):
+        for copy in row_copies(layer, gate, rest, gate_in, rest_in, sems, spot, base, core, core == layer):
+            copy.wait_recv()
+
+
+def early_kernel(n, gate, rest, gate_in, rest_in, send_g, recv_g, send_r, recv_r):
+    core, q = lax.axis_index("section"), lax.axis_index("seq")
+    spot = lax.rem(q, PLANE)
+    base = q - spot
+    sems = (send_g, recv_g, send_r, recv_r)
+    barrier = pltpu.get_barrier_semaphore()
+
+    @pl.when(core == 1)
+    def _():
+        for k in range(PLANE):
+            for other in range(2 if k else 1):
+                to = (other, base + lax.rem(spot + k, PLANE))
+                pl.semaphore_signal(barrier, inc=1, device_id=to, device_id_type=MESH)
+
+    pl.semaphore_wait(barrier, PLANE - core)
+    for side in range(2):
+
+        @pl.when(core == side)
+        def _():
+            copies = row_copies(1, gate, rest, gate_in, rest_in, sems, spot, base, side, side == 1)
+            for copy in copies:
+                copy.start()
+            if side:
+                keep_rows(1, gate, rest, gate_in, rest_in, spot)
+            for copy in copies:
+                copy.wait_send()
+            if side:
+                wait_rows(1, gate, rest, gate_in, rest_in, sems, spot, base)
+
+
+def settle_early(gate, rest, n):
+    vmem = pl.BlockSpec(memory_space=pltpu.VMEM)
+    dma = pltpu.SemaphoreType.DMA
+    rows, eight = D // n, 2 * PLANE
+    return pl.pallas_call(
+        functools.partial(early_kernel, n),
+        out_shape=[
+            jax.ShapeDtypeStruct((eight, rows, gate.shape[1]), BF16),
+            jax.ShapeDtypeStruct((eight, rows, rest.shape[1]), BF16),
+        ],
+        in_specs=[vmem, vmem],
+        out_specs=[vmem, vmem],
+        scratch_shapes=[dma((eight,)), dma((eight,)), dma((eight,)), dma((eight,))],
+        compiler_params=pltpu.CompilerParams(collective_id=8, has_side_effects=True, vmem_limit_bytes=32 * MIB),
+    )(gate, rest)
+
+
 def settle_kernel(
-    n, ga0, re0, ga1, re1, ow0, ow1, a0, a1, d0, d1, gin_ref, gout_ref, acts_ref, grads_ref,
+    n, gate, rest, gate_1, rest_1, ow0, ow1, a0, a1, d0, d1, gin_ref, gout_ref, acts_ref, grads_ref,
     gate_in, rest_in, out_in, send_g, recv_g, send_r, recv_r, send_o, recv_o, send_x, recv_x, keep_x,
 ):
     core = lax.axis_index("section")
     q = lax.axis_index("seq")
     spot = lax.rem(q, PLANE)
     base = q - spot
-    rows = gin_ref.shape[0]
+    sems = (send_g, recv_g, send_r, recv_r)
     barrier = pltpu.get_barrier_semaphore()
     for k in range(PLANE):
         for flip in range(2):
@@ -866,62 +945,59 @@
                 pl.semaphore_signal(barrier, inc=1, device_id=to, device_id_type=MESH)
     pl.semaphore_wait(barrier, 2 * PLANE - 1)
 
-    def run(layer, gate, rest, outw, act, grad, away_act, away_grad, away_outw, away_gate, away_rest):
+    def fill(gates, rests):
+        for p in range(2 * PLANE):
+            wide = gates.shape[2]
+            gin_ref[:, p * wide : p * wide + wide] = gates[p].astype(F32)
+            wide = rests.shape[2]
+            at = INNER + p * wide
+            width = min(wide, PROJ - at)
+            gin_ref[:, at : at + width] = rests[p].astype(F32)[:, :width]
+
+    def run(layer, outw, act, grad, away_act, away_grad, away_outw):
+        rows = row_copies(0, gate, rest, gate_in, rest_in, sems, spot, base, layer, layer == 0)
+        for copy in rows:
+            copy.start()
         copies = []
 
-        def send(src, dst, sems, at, to):
+        def send(src, dst, sems, at):
             copy = pltpu.make_async_remote_copy(
                 src_ref=src, dst_ref=dst, send_sem=sems[0].at[at], recv_sem=sems[1].at[at],
-                device_id=to, device_id_type=MESH,
+                device_id=(1 - layer, q), device_id_type=MESH,
             )
             copy.start()
             copies.append(copy)
 
-        across = (1 - layer, q)
-        kept = []
         for at, (own, away, dst) in enumerate(((grad, away_grad, grads_ref), (act, away_act, acts_ref))):
-            send(away, dst.at[layer], (send_x, recv_x), at, across)
-            kept.append(pltpu.make_async_copy(own, dst.at[layer], keep_x.at[at]))
-            kept[-1].start()
-        send(away_outw, out_in, (send_o, recv_o), 0, across)
-        for k in range(PLANE):
-            peer = lax.rem(spot + k, PLANE)
-            block = pl.ds(pl.multiple_of(peer * rows, rows), rows)
-            for flip in range(2):
-                if not (k or flip):
-                    continue
-                at = 2 * k + flip
-                to = (1 - layer if flip else layer, base + peer)
-                slot = 2 * spot + layer
-                send((away_gate if flip else gate).at[block], gate_in.at[slot], (send_g, recv_g), at, to)
-                send((away_rest if flip else rest).at[block], rest_in.at[slot], (send_r, recv_r), at, to)
-        mine = pl.ds(pl.multiple_of(spot * rows, rows), rows)
-        gate_in[2 * spot + layer] = gate[mine, :]
-        rest_in[2 * spot + layer] = rest[mine, :]
+            send(away, dst.at[layer], (send_x, recv_x), at)
+            copies.append(pltpu.make_async_copy(own, dst.at[layer], keep_x.at[at]))
+            copies[-1].start()
+        send(away_outw, out_in, (send_o, recv_o), 0)
         half = D // 2
         gout_ref[:, layer * half : layer * half + half] = outw[...].astype(F32)
-        for copy in copies + kept:
+        if layer:
+            fill(gate_1, rest_1)
+        else:
+            keep_rows(0, gate, rest, gate_in, rest_in, spot)
+        for copy in rows:
+            copy.wait_send()
+        if not layer:
+            wait_rows(0, gate, rest, gate_in, rest_in, sems, spot, base)
+            fill(gate_in, rest_in)
+        for copy in copies:
             copy.wait()
         gout_ref[:, (1 - layer) * half : (1 - layer) * half + half] = out_in[...].astype(F32)
 
     @pl.when(core == 0)
     def _():
-        run(0, ga0, re0, ow0, a0, d0, a1, d1, ow1, ga1, re1)
+        run(0, ow0, a0, d0, a1, d1, ow1)
 
     @pl.when(core == 1)
     def _():
-        run(1, ga1, re1, ow1, a1, d1, a0, d0, ow0, ga0, re0)
-
-    for p in range(2 * PLANE):
-        wide = gate_in.shape[2]
-        gin_ref[:, p * wide : p * wide + wide] = gate_in[p].astype(F32)
-        wide = rest_in.shape[2]
-        at = INNER + p * wide
-        width = min(wide, PROJ - at)
-        gin_ref[:, at : at + width] = rest_in[p].astype(F32)[:, :width]
-
-
-def settle(gates, rests, outs, acts, grads, n):
+        run(1, ow1, a1, d1, a0, d0, ow0)
+
+
+def settle(gate, rest, early, outs, acts, grads, n):
     vmem = pl.BlockSpec(memory_space=pltpu.VMEM)
     anywhere = pl.BlockSpec(memory_space=pl.ANY)
     dma = pltpu.SemaphoreType.DMA
@@ -936,14 +1012,14 @@
         in_specs=[vmem] * 6 + [anywhere] * 4,
         out_specs=[vmem, vmem, anywhere, anywhere],
         scratch_shapes=[
-            pltpu.VMEM((eight, rows, gates[0].shape[1]), BF16),
-            pltpu.VMEM((eight, rows, rests[0].shape[1]), BF16),
+            pltpu.VMEM((eight, rows, gate.shape[1]), BF16),
+            pltpu.VMEM((eight, rows, rest.shape[1]), BF16),
             pltpu.VMEM((INNER // n, D // 2), BF16),
             dma((eight,)), dma((eight,)), dma((eight,)), dma((eight,)),
             dma((1,)), dma((1,)), dma((2,)), dma((2,)), dma((2,)),
         ],
         compiler_params=pltpu.CompilerParams(collective_id=3, has_side_effects=True, vmem_limit_bytes=40 * MIB),
-    )(gates[0], rests[0], gates[1], rests[1], outs[0], outs[1], acts[0], acts[1], grads[0], grads[1])
+    )(gate, rest, early[0], early[1], outs[0], outs[1], acts[0], acts[1], grads[0], grads[1])
 
 
 def swap(value):
@@ -1056,7 +1132,10 @@
     def finish(layer, h, proj, parts, carried):
         values, _, _, step, cum, cumt, _, c, _, g, _ = parts[:11]
         y, gated_low, owned = mix(g, step, cum, cumt, values, proj, c, carried, params[layer][3], n)
-        return y, owned, h + mm(gated_low, own_out, other_out, flags[layer], False, 768)
+        return y, owned, gated_low
+
+    def output(layer, h, gated_low):
+        return (h + mm(gated_low, own_out, other_out, flags[layer], False, 768)).astype(BF16)
 
     x_0 = mine(inputs)
     before_0 = shifted(x_0[ROWS - 16 :], 1, n)
@@ -1069,8 +1148,8 @@
     parts_0 = blocks(0, proj_0, halo_0)
     carried_0 = exchange(parts_0[1], parts_0[2], n, False)
     normeds_0 = copies_of(tied(normed_0, carried_0), n)
-    y_0, owned_0, out_0 = finish(0, h_0, proj_0, parts_0, carried_0)
-    act_0 = out_0.astype(BF16)
+    y_0, owned_0, low_0 = finish(0, h_0, proj_0, parts_0, carried_0)
+    act_0 = output(0, h_0, low_0)
 
     before_1 = shifted(act_0[ROWS - 16 :], 1, n)
     h_1 = act_0.astype(F32)
@@ -1080,8 +1159,7 @@
     parts_1 = blocks(1, proj_1, halo_1)
     carried_1 = exchange(parts_1[1], parts_1[2], n, False)
     carried_1, normeds_0, normeds_1 = arrived(carried_1, normeds_0, normeds_1)
-    y_1, owned_1, out_1 = finish(1, h_1, proj_1, parts_1, carried_1)
-    act_1 = out_1.astype(BF16)
+    y_1, owned_1, low_1 = finish(1, h_1, proj_1, parts_1, carried_1)
 
     def gate_side(layer, d_low, y, proj, parts, *spread):
         d_gated_low = mm(d_low, own_out, other_out, flags[layer], True, 1024)
@@ -1142,8 +1220,8 @@
     d_out_0 = d_1.astype(BF16)
     dy_0, d_gate_0, gain_0, d_carried_0, rests_1 = gate_side(0, d_out_0, y_0, proj_0, parts_0, (rest_1,), 6)
     restw_1 = partial_grad(normeds_1, rests_1)
-    late_0 = exchange(tied(d_carried_0, restw_1), parts_0[2], n, True)
-    restw_1 = plane_rows(restw_1, n)
+    late_0 = exchange(tied(d_carried_0, restw_1, outw_1, gatew_1), parts_0[2], n, True)
+    restw_1 = plane_rows(tied(restw_1, late_0), n)
     lows_0 = copies_of(tied(d_out_0, late_0), n)
     back_0 = core_side(
         0, proj_0, halo_0, parts_0, y_0, dy_0, carried_0, late_0, (d_gate_0,), 7
@@ -1160,10 +1238,13 @@
     rests_0 = pieces[:1] + [lax.ppermute(pieces[k], "seq", plane_route(k, n)) for k in range(1, PLANE)]
     d_0, ng_0 = norm_side(0, h_0, d_out_0.astype(F32), d_gate_0, rest_0)
     ng_0, rests_0 = arrived(ng_0, rests_0)
-    restw_0 = plane_rows(partial_grad(normeds_0, rests_0), n)
+    restw_0 = partial_grad(normeds_0, rests_0)
+    act_1 = output(1, h_1, tied(low_1, restw_0))
+    early = settle_early(tied(gatew_1, restw_0), restw_1, n)
+    restw_0 = plane_rows(restw_0, n)
 
     g_in, g_out, acts, input_grads = settle(
-        (gatew_0, gatew_1), (restw_0, restw_1), (outw_0, outw_1), (act_0, act_1), (d_0, d_1), n
+        gatew_0, restw_0, early, (outw_0, outw_1), (act_0, act_1), (d_0, d_1), n
     )
     small_0, small_1 = small_of(ng_0, back_0, gain_0), small_of(ng_1, back_1, gain_1)
     small = jnp.where(first, small_0, small_1) + swap(jnp.where(first, small_1, small_0))

time: 707 us -> 687 us (0.972)
  waiting for transfers between devices: 76 us -> 62.4 us
    reduce_scatter x6, waiting for transfers between devices: 16.6 us -> 7.64 us  [plane_rows(): lax.psum_scatter(partial, 'seq', scatter_dimension=0, axis_index_groups=c...]
    pallas_call x1, Pallas kernels: 19.4 us -> 12.1 us  [settle(): pl.pallas_call(functools.partial(settle_kernel, n), out_shape=[sds(rows,...]
    unnamed x248 -> x256, local copies, waits for them, and re-layouts: 44.9 us -> 45.3 us
  transfers between devices with their start and end apart: 39 -> 39, of which waited for: 11 -> 11; matrix products, arithmetic and copies ran while one was open for 11% -> 12% of each run, Pallas kernels for 41% -> 38%
where the time goes in v5:
time: 687 us; the launch traced here: 676 us
  Pallas kernels  435 us (63%)
  waiting for transfers between devices  62.4 us (9%)
  local copies, waits for them, and re-layouts  62.1 us (9%)
  matrix products  45.3 us (7%)
  starting transfers between devices  36.8 us (5%)
  other arithmetic  18.7 us (3%)
  between operations  16.4 us (2%)
    pallas_call x4, Pallas kernels, exchange(): pl.pallas_call(functools.partial(exchange_kernel, n, rev), out_shape=sds(...  155 us
    pallas_call x2, Pallas kernels, core_back(): pl.pallas_call(body, grid=(STEPS + 2,), in_specs=[lanes(ROWS, STEPS), fix...  76.9 us
    pallas_call x2, Pallas kernels, gate_back(): pl.pallas_call(body, grid=(2, STEPS), in_specs=[first(ROWS), first(ROWS),...  49.8 us
    unnamed x256, local copies, waits for them, and re-layouts  45.3 us
    dot_general x12, matrix products, part(): lax.dot_general(left, cols, (((0, 1), (0, 1)), ((), ())), preferred_eleme...  45.3 us
    ppermute x4, waiting for transfers between devices, shifted(): lax.ppermute(value, 'seq', [(i, i + distance) for i in range(n) if 0 <= i...  34.5 us
    pallas_call x2, Pallas kernels, mix(): pl.pallas_call(functools.partial(mix_kernel, n), grid=(STEPS,), in_specs=...  29.6 us
    pallas_call x2, Pallas kernels, project_mm(): pl.pallas_call(project_kernel, grid_spec=pltpu.PrefetchScalarGridSpec(num...  28.2 us
  transfers between devices with their start and end apart: 39, of which 11 were waited for; matrix products, arithmetic and copies ran while one was open for 12% of the time, Pallas kernels for 38%

profile of v5, /device:TPU:0, one launch (start us, length us, event | category | flops | bytes accessed | tf_op | source)
XLA Modules:
  0.0 676.2 jit_solution(9965035128011977127)
XLA Ops:
  19.9 28.0 %collective-permute-done.4 = bf16[16,1536]{1,0:T(8,128)(2,1)S(1)} collective-permute-done((bf16[16,1536]{1,0:T(8,128)(2,1)S(1)}, bf16[16,1536]{1,0:T(8,128)(2,1)S(1)}, u32[]{:S(2)}, u32[]{:S(2)}) %collective-permute-start.4) | collective-permute-done | bytes 49184 | tf_op jit(solution)/shard_map/ppermute | solution.py:1030
  50.8 14.1 %shard_map.194 = (f32[256,6448]{1,0:T(8,128)}, f32[16,6448]{1,0:T(8,128)S(1)}) custom-call(s32[1]{0:T(128)} %bitcast.2.flag_ref, bf16[272,1536]{1,0:T(8,128)(2,1)S(1)} %pad_maximum_fusion.5.x_ref, bf16[6448,1536]{1,0:T(8,128)(2,1)} %bitcast.146, bf16[6448,1536]{1,0:T(8,128)(2,1)} %collective-permute-done.5.other_ref), custom_call_target="tpu_custom_call" | custom-call | flops 5070913536 | bytes 19808256 | tf_op jit(solution)/shard_map/pallas_call | solution.py:277
  66.3 13.2 %shard_map.195 = (f32[256,3072]{1,0:T(8,128)}, f32[128,3072]{1,0:T(8,128)S(1)}, f32[8,3072]{1,0:T(8,128)S(1)}, bf16[256,384]{1,0:T(8,128)(2,1)S(1)}, bf16[256,38...) custom-call(f32[256,6448]{1,0:T(8,128)} %get-tuple-element.108.x_ref, ...), custom_call_target="tpu_custom_call" | custom-call | flops 1000000000 | bytes 10485760 | tf_op jit(solution)/shard_map/pallas_call | solution.py:401
  80.2 42.1 %shard_map.196.car_ref.refs_16_ = f32[128,3072]{1,0:T(8,128)S(1)} custom-call(f32[128,3072]{1,0:T(8,128)S(1)} %get-tuple-element.116.s_ref, f32[8,3072]{1,0:T(8,128)S(1)} %get-tuple-element.117.d_ref), custom_call_target="tpu_custom_call" | custom-call | tf_op jit(solution)/shard_map/pallas_call | solution.py:540
  125.3 14.7 %shard_map.197 = (f32[256,3072]{1,0:T(8,128)}, bf16[256,3072]{1,0:T(8,128)(2,1)S(1)}, bf16[256,3072]{1,0:T(8,128)(2,1)S(1)}) custom-call(f32[256,256]{1,0:T(8,128)S(1)} %get-tuple-element.110.g_ref, bf16[256,384]{1,0:T(8,128)(2,1)S(1)} %get-tuple-element.111.step_ref.refs_8_, bf16[256,384]{1,0:T(8,128)(2,1)S(1)} %get-tuple-element.112.cum_ref.refs_3_.refs_9_, ...), custom_call_target="tpu_custom_call" | custom-call | flops 3000000000 | bytes 14680064 | tf_op jit(solution)/shard_map/pallas_call | solution.py:624
  140.0 6.9 %shard_map.198 = f32[256,1536]{1,0:T(8,128)S(1)} custom-call(s32[1]{0:T(128)} %bitcast.2.flag_ref, bf16[256,3072]{1,0:T(8,128)(2,1)S(1)} %get-tuple-element.118.x_ref, bf16[3072,1536]{1,0:T(8,128)(2,1)} %bitcast.17.own_ref, bf16[3072,1536]{1,0:T(8,128)(2,1)} %collective-permute-done.6.other_ref), custom_call_target="tpu_custom_call" | custom-call | flops 2415919104 | bytes 9437184 | tf_op jit(solution)/shard_map/pallas_call | solution.py:157
  151.9 6.5 collective-permute-done.7
  162.9 14.1 %shard_map.199 = (f32[256,6448]{1,0:T(8,128)}, f32[16,6448]{1,0:T(8,128)S(1)}) custom-call(s32[1]{0:T(128)} %bitcast.flag_ref, bf16[272,1536]{1,0:T(8,128)(2,1)S(1)} %pad_maximum_fusion.6.x_ref, bf16[6448,1536]{1,0:T(8,128)(2,1)} %bitcast.147, bf16[6448,1536]{1,0:T(8,128)(2,1)} %collective-permute-done.5.other_ref), custom_call_target="tpu_custom_call" | custom-call | flops 5070913536 | bytes 19808256 | tf_op jit(solution)/shard_map/pallas_call | solution.py:277
  177.0 13.2 %shard_map.200 = (f32[256,3072]{1,0:T(8,128)}, f32[128,3072]{1,0:T(8,128)S(1)}, f32[8,3072]{1,0:T(8,128)S(1)}, bf16[256,384]{1,0:T(8,128)(2,1)S(1)}, bf16[256,38...) custom-call(f32[256,6448]{1,0:T(8,128)} %get-tuple-element.120.x_ref, ...), custom_call_target="tpu_custom_call" | custom-call | flops 1000000000 | bytes 10485760 | tf_op jit(solution)/shard_map/pallas_call | solution.py:401
  190.3 41.2 %shard_map.201.car_ref.refs_16_ = f32[128,3072]{1,0:T(8,128)S(1)} custom-call(f32[128,3072]{1,0:T(8,128)S(1)} %get-tuple-element.122.s_ref, f32[8,3072]{1,0:T(8,128)S(1)} %get-tuple-element.123.d_ref), custom_call_target="tpu_custom_call" | custom-call | tf_op jit(solution)/shard_map/pallas_call | solution.py:540
  232.5 15.0 %shard_map.203 = (f32[256,3072]{1,0:T(8,128)}, bf16[256,3072]{1,0:T(8,128)(2,1)S(1)}, bf16[256,3072]{1,0:T(8,128)(2,1)S(1)}) custom-call(f32[256,256]{1,0:T(8,128)S(1)} %get-tuple-element.135.g_ref, bf16[256,384]{1,0:T(8,128)(2,1)S(1)} %get-tuple-element.136.step_ref.refs_8_, bf16[256,384]{1,0:T(8,128)(2,1)S(1)} %get-tuple-element.137.cum_ref.refs_3_.refs_9_, ...), custom_call_target="tpu_custom_call" | custom-call | flops 3000000000 | bytes 14680064 | tf_op jit(solution)/shard_map/pallas_call | solution.py:624
  249.9 6.9 %shard_map.202.refs_0_ = f32[256,3072]{1,0:T(8,128)S(1)} custom-call(s32[1]{0:T(128)} %bitcast.flag_ref, bf16[256,1536]{1,0:T(8,128)(2,1)S(1)} %dynamic-slice_bitcast_fusion.x_ref, bf16[3072,1536]{1,0:T(8,128)(2,1)} %bitcast.17.own_ref, bf16[3072,1536]{1,0:T(8,128)(2,1)} %collective-permute-done.6.other_ref), custom_call_target="tpu_custom_call" | custom-call | flops 2415919104 | bytes 9437184 | tf_op jit(solution)/shard_map/pallas_call | solution.py:157
  258.5 22.1 %shard_map.204 = (f32[256,3072]{1,0:T(8,128)}, bf16[256,3072]{1,0:T(8,128)(2,1)S(1)}, f32[8,3072]{1,0:T(8,128)S(1)}, bf16[128,3072]{1,0:T(8,128)(2,1)S(1)}, bf16[4,256,768]{2,1,0:T(8,128)(2,1)S(1)}) custom-call(f32[256,3072]{1,0:T(8,128)} %copy-done.1, f32[256,3072]{1,0:T(8,128)} %get-tuple-element.141.refs_1_.refs_14_, ...), custom_call_target="tpu_custom_call" | custom-call | flops 1000000000 | bytes 16777216 | tf_op jit(solution)/shard_map/pallas_call | solution.py:694
  281.8 41.1 %shard_map.205.refs_17_ = bf16[128,3072]{1,0:T(8,128)(2,1)S(1)} custom-call(bf16[128,3072]{1,0:T(8,128)(2,1)S(1)} %get-tuple-element.148.s_ref, f32[8,3072]{1,0:T(8,128)S(1)} %get-tuple-element.123.d_ref), custom_call_target="tpu_custom_call" | custom-call | tf_op jit(solution)/shard_map/pallas_call | solution.py:540
  323.0 35.7 %shard_map.206 = (bf16[256,3584]{1,0:T(8,128)(2,1)}, f32[16,3584]{1,0:T(8,128)S(1)}, f32[8,3584]{1,0:T(8,128)}, f32[8,3584]{1,0:T(8,128)S(1)}, f32[8,128]{1,0:T(...) custom-call(f32[256,6448]{1,0:T(8,128)} %get-tuple-element.120.x_ref.bc_ref.raw_ref.gate_ref.refs_2_.refs_0_., ...), custom_call_target="tpu_custom_call" | custom-call | flops 8000000000 | bytes 14680064 | tf_op jit(solution)/shard_map/pallas_call | solution.py:830
  382.7 11.8 %shard_map.207 = f32[256,1536]{1,0:T(8,128)S(1)} custom-call(s32[1]{0:T(128)} %bitcast.flag_ref, bf16[256,3072]{1,0:T(8,128)(2,1)S(1)} %copy-done.10, bf16[256,3584]{1,0:T(8,128)(2,1)S(1)} %copy-done.6, bf16[6448,1536]{1,0:T(8,128)(2,1)} %bitcast.148, bf16[6448,1536]{1,0:T(8,128)(2,1)} %collective-permute-done.5.other_ref), custom_call_target="tpu_custom_call" | custom-call | flops 5070913536 | bytes 19808256 | tf_op jit(solution)/shard_map/pallas_call | solution.py:316
  397.5 7.0 %shard_map.208.refs_0_ = f32[256,3072]{1,0:T(8,128)S(1)} custom-call(s32[1]{0:T(128)} %bitcast.2.flag_ref, bf16[256,1536]{1,0:T(8,128)(2,1)S(1)} %get-tuple-element.186.x_ref, bf16[3072,1536]{1,0:T(8,128)(2,1)} %bitcast.17.own_ref, bf16[3072,1536]{1,0:T(8,128)(2,1)} %collective-permute-done.6.other_ref), custom_call_target="tpu_custom_call" | custom-call | flops 2415919104 | bytes 9437184 | tf_op jit(solution)/shard_map/pallas_call | solution.py:157
  406.2 27.6 %shard_map.209 = (f32[256,3072]{1,0:T(8,128)}, bf16[256,3072]{1,0:T(8,128)(2,1)S(1)}, f32[8,3072]{1,0:T(8,128)S(1)}, bf16[128,3072]{1,0:T(8,128)(2,1)S(1)}, bf16[4,256,896]{2,1,0:T(8,128)(2,1)S(1)}) custom-call(f32[256,3072]{1,0:T(8,128)} %copy-done.2, f32[256,3072]{1,0:T(8,128)} %get-tuple-element.132.refs_1_.refs_14_, ...), custom_call_target="tpu_custom_call" | custom-call | flops 1000000000 | bytes 16777216 | tf_op jit(solution)/shard_map/pallas_call | solution.py:694
  451.5 30.1 %shard_map.210.refs_17_ = bf16[128,3072]{1,0:T(8,128)(2,1)S(1)} custom-call(bf16[128,3072]{1,0:T(8,128)(2,1)S(1)} %copy-done.30, f32[8,3072]{1,0:T(8,128)S(1)} %copy-done.37), custom_call_target="tpu_custom_call" | custom-call | tf_op jit(solution)/shard_map/pallas_call | solution.py:540
  491.6 41.2 %shard_map.211 = (bf16[256,3584]{1,0:T(8,128)(2,1)}, f32[16,3584]{1,0:T(8,128)S(1)}, f32[8,3584]{1,0:T(8,128)S(1)}, f32[8,3584]{1,0:T(8,128)S(1)}, f32[8,128]{1,...) custom-call(f32[256,6448]{1,0:T(8,128)} %get-tuple-element.108.x_ref.bc_ref.raw_ref.gate_ref.refs_2_.refs_0_.refs_1_, ...), custom_call_target="tpu_custom_call" | custom-call | flops 8000000000 | bytes 14680064 | tf_op jit(solution)/shard_map/pallas_call | solution.py:830
  563.6 11.8 %shard_map.212 = f32[256,1536]{1,0:T(8,128)S(1)} custom-call(s32[1]{0:T(128)} %bitcast.2.flag_ref, bf16[256,3072]{1,0:T(8,128)(2,1)S(1)} %copy-done.8, bf16[256,3584]{1,0:T(8,128)(2,1)S(1)} %copy-done.5, bf16[6448,1536]{1,0:T(8,128)(2,1)} %bitcast.149, bf16[6448,1536]{1,0:T(8,128)(2,1)} %collective-permute-done.5.other_ref), custom_call_target="tpu_custom_call" | custom-call | flops 5070913536 | bytes 19808256 | tf_op jit(solution)/shard_map/pallas_call | solution.py:316
  629.0 6.8 %shard_map.214 = f32[256,1536]{1,0:T(8,128)S(1)} custom-call(s32[1]{0:T(128)} %bitcast.flag_ref, bf16[256,3072]{1,0:T(8,128)(2,1)S(1)} %copy-done.22, bf16[3072,1536]{1,0:T(8,128)(2,1)} %bitcast.17.own_ref, bf16[3072,1536]{1,0:T(8,128)(2,1)} %collective-permute-done.6.other_ref), custom_call_target="tpu_custom_call" | custom-call | flops 2415919104 | bytes 9437184 | tf_op jit(solution)/shard_map/pallas_call | solution.py:157
  636.1 7.6 %reduce-scatter.13.cloned.1.call-done.rest = bf16[384,448]{1,0:T(8,128)(2,1)} async-done(((bf16[1536,448]{1,0:T(8,128)(2,1)}), bf16[384,448]{1,0:T(8,128)(2,1)}) %reduce-scatter.13.cloned.1.call-update) | async-done | bytes 344080 | tf_op jit(solution)/shard_map/reduce_scatter | solution.py:1068
  650.3 12.1 %shard_map.215 = (f32[96,6448]{1,0:T(8,128)S(1)}, f32[192,1536]{1,0:T(8,128)S(1)}, bf16[2,256,1536]{2,1,0:T(8,128)(2,1)S(1)}, f32[2,256,1536]{2,1,0:T(8,128)}) custom-call(bf16[384,384]{1,0:T(8,128)(2,1)S(1)} %copy-done.40, bf16[384,448]{1,0:T(8,128)(2,1)S(1)} %copy-done.35, bf16[8,96,384]{2,1,0:T(8,128)(2,1)S(1)} %copy-done.32, ...), custom_call_target="tpu_custom_call" | custom-call | tf_op jit(solution)/shard_map/pallas_call | solution.py:1006
  (448 shorter events, 189.0 us)
Async XLA Ops:
  7.3 442.2 %reduce-scatter.9.cloned.1.call-start = ((), (), s32[]{:S(2)}) async-start(), calls=%async_computation.7 | async-start | bytes 1474560 | tf_op jit(solution)/shard_map/reduce_scatter | solution.py:1068
  7.3 43.3 %collective-permute-start.5 = (bf16[6448,1536]{1,0:T(8,128)(2,1)}, bf16[6448,1536]{1,0:T(8,128)(2,1)}, u32[]{:S(2)}, u32[]{:S(2)}) collective-permute-start(bf16[6448,1536]{1,0:T(8,128)(2,1)} %bitcast.145), channel_id=1, source_target_pairs={{0,16},{16,0},{1,17},{17,1},{2,18},{18,2},{3,19},{19,3},{4,20},{20... | collective-permute-start | bytes 59424776 | tf_op jit(solution)/shard_map/ppermute | solution.py:1026
  9.0 40.6 %collective-permute-start.3 = (bf16[256,1536]{1,0:T(8,128)(2,1)S(1)}, bf16[256,1536]{1,0:T(8,128)(2,1)S(1)}, u32[]{:S(2)}, u32[]{:S(2)}) collective-permute-start(bf16[256,1536]{1,0:T(8,128)(2,1)S(1)} %dynamic-slice_bitcast_fusion.x_ref), channel_id=1, source_target_pairs={{0,3},{1,0},{2,1},{3,2},{4,7},{5,4},{6,5},{7,6},{8,11},{9,8},{10,9... | collective-permute-start | bytes 2359304 | tf_op jit(solution)/shard_map/ppermute | solution.py:1046
  12.7 37.0 %collective-permute-start.2 = (bf16[256,1536]{1,0:T(8,128)(2,1)S(1)}, bf16[256,1536]{1,0:T(8,128)(2,1)}, u32[]{:S(2)}, u32[]{:S(2)}) collective-permute-start(bf16[256,1536]{1,0:T(8,128)(2,1)S(1)} %dynamic-slice_bitcast_fusion.x_ref), channel_id=1, source_target_pairs={{0,2},{1,3},{2,0},{3,1},{4,6},{5,7},{6,4},{7,5},{8,10},{9,11},{10,... | collective-permute-start | bytes 2359304 | tf_op jit(solution)/shard_map/ppermute | solution.py:1046
  13.2 37.4 %collective-permute-start.1 = (bf16[256,1536]{1,0:T(8,128)(2,1)S(1)}, bf16[256,1536]{1,0:T(8,128)(2,1)}, u32[]{:S(2)}, u32[]{:S(2)}) collective-permute-start(bf16[256,1536]{1,0:T(8,128)(2,1)S(1)} %dynamic-slice_bitcast_fusion.x_ref), channel_id=1, source_target_pairs={{0,1},{1,2},{2,3},{3,0},{4,5},{5,6},{6,7},{7,4},{8,9},{9,10},{10,1... | collective-permute-start | bytes 2359304 | tf_op jit(solution)/shard_map/ppermute | solution.py:1046
  14.6 33.4 %collective-permute-start.4 = (bf16[16,1536]{1,0:T(8,128)(2,1)S(1)}, bf16[16,1536]{1,0:T(8,128)(2,1)S(1)}, u32[]{:S(2)}, u32[]{:S(2)}) collective-permute-start(bf16[16,1536]{1,0:T(8,128)(2,1)S(1)} %dynamic-slice_bitcast_fusion.1), channel_id=1, source_target_pairs={{0,1},{1,2},{2,3},{3,4},{4,5},{5,6},{6,7},{7,8},{8,9},{9,10},{10,1... | collective-permute-start | bytes 147464 | tf_op jit(solution)/shard_map/ppermute | solution.py:1030
  64.9 75.1 %collective-permute-start.6 = (bf16[3072,1536]{1,0:T(8,128)(2,1)}, bf16[3072,1536]{1,0:T(8,128)(2,1)}, u32[]{:S(2)}, u32[]{:S(2)}) collective-permute-start(bf16[3072,1536]{1,0:T(8,128)(2,1)} %bitcast.17.own_ref), channel_id=1, source_target_pairs={{0,16},{16,0},{1,17},{17,1},{2,18},{18,2},{3,19},{19,3},{4,20},{20... | collective-permute-start | bytes 28311560 | tf_op jit(solution)/shard_map/ppermute | solution.py:1026
  122.3 40.2 %collective-permute-start.10 = (bf16[256,1536]{1,0:T(8,128)(2,1)S(1)}, bf16[256,1536]{1,0:T(8,128)(2,1)S(1)}, u32[]{:S(2)}, u32[]{:S(2)}) collective-permute-start(bf16[256,1536]{1,0:T(8,128)(2,1)S(1)} %copy-done.74), channel_id=1, source_target_pairs={{0,3},{1,0},{2,1},{3,2},{4,7},{5,4},{6,5},{7,6},{8,11},{9,8},{10,9... | collective-permute-start | bytes 2359304 | tf_op jit(solution)/shard_map/ppermute | solution.py:1046
  124.3 107.2 %collective-permute-start.9 = (bf16[256,1536]{1,0:T(8,128)(2,1)S(1)}, bf16[256,1536]{1,0:T(8,128)(2,1)S(1)}, u32[]{:S(2)}, u32[]{:S(2)}) collective-permute-start(bf16[256,1536]{1,0:T(8,128)(2,1)S(1)} %copy-done.74), channel_id=1, source_target_pairs={{0,2},{1,3},{2,0},{3,1},{4,6},{5,7},{6,4},{7,5},{8,10},{9,11},{10,... | collective-permute-start | bytes 2359304 | tf_op jit(solution)/shard_map/ppermute | solution.py:1046
  124.5 107.0 %collective-permute-start.8 = (bf16[256,1536]{1,0:T(8,128)(2,1)S(1)}, bf16[256,1536]{1,0:T(8,128)(2,1)S(1)}, u32[]{:S(2)}, u32[]{:S(2)}) collective-permute-start(bf16[256,1536]{1,0:T(8,128)(2,1)S(1)} %copy-done.74), channel_id=1, source_target_pairs={{0,1},{1,2},{2,3},{3,0},{4,5},{5,6},{6,7},{7,4},{8,9},{9,10},{10,1... | collective-permute-start | bytes 2359304 | tf_op jit(solution)/shard_map/ppermute | solution.py:1046
  158.4 73.1 %collective-permute-start.13 = (bf16[256,1536]{1,0:T(8,128)(2,1)S(1)}, bf16[256,1536]{1,0:T(8,128)(2,1)S(1)}, u32[]{:S(2)}, u32[]{:S(2)}) collective-permute-start(bf16[256,1536]{1,0:T(8,128)(2,1)S(1)} %fusion.12), channel_id=1, source_target_pairs={{0,3},{1,0},{2,1},{3,2},{4,7},{5,4},{6,5},{7,6},{8,11},{9,8},{10,9... | collective-permute-start | bytes 2359304 | tf_op jit(solution)/shard_map/ppermute | solution.py:1046
  160.3 71.2 %collective-permute-start.12 = (bf16[256,1536]{1,0:T(8,128)(2,1)S(1)}, bf16[256,1536]{1,0:T(8,128)(2,1)S(1)}, u32[]{:S(2)}, u32[]{:S(2)}) collective-permute-start(bf16[256,1536]{1,0:T(8,128)(2,1)S(1)} %fusion.12), channel_id=1, source_target_pairs={{0,2},{1,3},{2,0},{3,1},{4,6},{5,7},{6,4},{7,5},{8,10},{9,11},{10,... | collective-permute-start | bytes 2359304 | tf_op jit(solution)/shard_map/ppermute | solution.py:1046
  162.6 69.0 %collective-permute-start.11 = (bf16[256,1536]{1,0:T(8,128)(2,1)S(1)}, bf16[256,1536]{1,0:T(8,128)(2,1)S(1)}, u32[]{:S(2)}, u32[]{:S(2)}) collective-permute-start(bf16[256,1536]{1,0:T(8,128)(2,1)S(1)} %fusion.12), channel_id=1, source_target_pairs={{0,1},{1,2},{2,3},{3,0},{4,5},{5,6},{6,7},{7,4},{8,9},{9,10},{10,1... | collective-permute-start | bytes 2359304 | tf_op jit(solution)/shard_map/ppermute | solution.py:1046
  370.5 79.0 %reduce-scatter.7.cloned.1.call-start = ((), (), s32[]{:S(2)}) async-start(), calls=%async_computation.6 | async-start | bytes 1474560 | tf_op jit(solution)/shard_map/reduce_scatter | solution.py:1068
  379.5 239.6 %reduce-scatter.15.cloned.1.call-start = ((), (), s32[]{:S(2)}) async-start(), calls=%async_computation.10 | async-start | bytes 1966080 | tf_op jit(solution)/shard_map/reduce_scatter | solution.py:1068
  482.5 50.3 %collective-permute-start.20 = (bf16[256,1536]{1,0:T(8,128)(2,1)S(1)}, bf16[256,1536]{1,0:T(8,128)(2,1)}, u32[]{:S(2)}, u32[]{:S(2)}) collective-permute-start(bf16[256,1536]{1,0:T(8,128)(2,1)S(1)} %get-tuple-element.186.x_ref), channel_id=1, source_target_pairs={{0,3},{1,0},{2,1},{3,2},{4,7},{5,4},{6,5},{7,6},{8,11},{9,8},{10,9... | collective-permute-start | bytes 2359304 | tf_op jit(solution)/shard_map/ppermute | solution.py:1046
  482.5 50.3 %collective-permute-start.19 = (bf16[256,1536]{1,0:T(8,128)(2,1)S(1)}, bf16[256,1536]{1,0:T(8,128)(2,1)}, u32[]{:S(2)}, u32[]{:S(2)}) collective-permute-start(bf16[256,1536]{1,0:T(8,128)(2,1)S(1)} %get-tuple-element.186.x_ref), channel_id=1, source_target_pairs={{0,2},{1,3},{2,0},{3,1},{4,6},{5,7},{6,4},{7,5},{8,10},{9,11},{10,... | collective-permute-start | bytes 2359304 | tf_op jit(solution)/shard_map/ppermute | solution.py:1046
  483.2 49.6 %collective-permute-start.18 = (bf16[256,1536]{1,0:T(8,128)(2,1)S(1)}, bf16[256,1536]{1,0:T(8,128)(2,1)}, u32[]{:S(2)}, u32[]{:S(2)}) collective-permute-start(bf16[256,1536]{1,0:T(8,128)(2,1)S(1)} %get-tuple-element.186.x_ref), channel_id=1, source_target_pairs={{0,1},{1,2},{2,3},{3,0},{4,5},{5,6},{6,7},{7,4},{8,9},{9,10},{10,1... | collective-permute-start | bytes 2359304 | tf_op jit(solution)/shard_map/ppermute | solution.py:1046
  484.6 151.6 %reduce-scatter.11.cloned.1.call-start = ((), (), s32[]{:S(2)}) async-start(), calls=%async_computation.8 | async-start | bytes 1474560 | tf_op jit(solution)/shard_map/reduce_scatter | solution.py:1068
  547.1 89.1 %reduce-scatter.17.cloned.1.call-start = ((), (), s32[]{:S(2)}) async-start(), calls=%async_computation.11 | async-start | bytes 1474560 | tf_op jit(solution)/shard_map/reduce_scatter | solution.py:1068
  551.1 25.4 %collective-permute-start.25 = (bf16[256,896]{1,0:T(8,128)(2,1)}, bf16[256,896]{1,0:T(8,128)(2,1)}, u32[]{:S(2)}, u32[]{:S(2)}) collective-permute-start(bf16[256,896]{1,0:T(8,128)(2,1)} %get-tuple-element.211), channel_id=1, source_target_pairs={{0,3},{1,0},{2,1},{3,2},{4,7},{5,4},{6,5},{7,6},{8,11},{9,8},{10,9... | collective-permute-start | bytes 1376264 | tf_op jit(solution)/shard_map/ppermute | solution.py:1238
  554.3 22.3 %collective-permute-start.24 = (bf16[256,896]{1,0:T(8,128)(2,1)}, bf16[256,896]{1,0:T(8,128)(2,1)}, u32[]{:S(2)}, u32[]{:S(2)}) collective-permute-start(bf16[256,896]{1,0:T(8,128)(2,1)} %get-tuple-element.212), channel_id=1, source_target_pairs={{0,2},{1,3},{2,0},{3,1},{4,6},{5,7},{6,4},{7,5},{8,10},{9,11},{10,... | collective-permute-start | bytes 1376264 | tf_op jit(solution)/shard_map/ppermute | solution.py:1238
  555.3 21.4 %collective-permute-start.23 = (bf16[256,896]{1,0:T(8,128)(2,1)}, bf16[256,896]{1,0:T(8,128)(2,1)}, u32[]{:S(2)}, u32[]{:S(2)}) collective-permute-start(bf16[256,896]{1,0:T(8,128)(2,1)} %get-tuple-element.213), channel_id=1, source_target_pairs={{0,1},{1,2},{2,3},{3,0},{4,5},{5,6},{6,7},{7,4},{8,9},{9,10},{10,1... | collective-permute-start | bytes 1376264 | tf_op jit(solution)/shard_map/ppermute | solution.py:1238
  560.3 83.4 %reduce-scatter.13.cloned.1.call-start = ((), (), s32[]{:S(2)}) async-start(), calls=%async_computation.9 | async-start | bytes 1966080 | tf_op jit(solution)/shard_map/reduce_scatter | solution.py:1068
  (141 other events, 1978.8 us)
Sparse Core Ops, SparseCore 0:
  370.6 28.4 reduce-scatter.8
  401.4 27.8 reduce-scatter.6
  484.7 33.0 reduce-scatter.14
  547.2 28.2 reduce-scatter.10
  577.7 28.3 reduce-scatter.16
  608.8 34.9 reduce-scatter.12

commit v6 on v5

--- a/solution.py
+++ b/solution.py
@@ -449,31 +449,44 @@
     def group(at):
         return pl.ds(pl.multiple_of(at * LANES, LANES), LANES)
 
-    first = []
+    cuts = LANES // 256
+    first = [[] for _ in range(cuts)]
     for k, peer in enumerate(peers):
-        to = device(level * PLANE + peer)
-        first.append(
+        first[0].append(
             pltpu.make_async_remote_copy(
                 src_ref=d_ref.at[:, group(peer)], dst_ref=dbox.at[spot],
-                send_sem=send_d.at[k], recv_sem=recv_d.at[k], device_id=to, device_id_type=MESH,
+                send_sem=send_d.at[k], recv_sem=recv_d.at[k],
+                device_id=device(level * PLANE + peer), device_id_type=MESH,
             )
         )
-        first.append(
-            pltpu.make_async_remote_copy(
-                src_ref=s_ref.at[:, group(peer)], dst_ref=inbox.at[spot],
-                send_sem=send_a.at[k], recv_sem=recv_a.at[k], device_id=to, device_id_type=MESH,
+    for b in range(cuts):
+        for k, peer in enumerate(peers):
+            part = pl.ds(pl.multiple_of(peer * LANES + b * 256, 256), 256)
+            first[b].append(
+                pltpu.make_async_remote_copy(
+                    src_ref=s_ref.at[:, part], dst_ref=inbox.at[spot, :, pl.ds(b * 256, 256)],
+                    send_sem=send_a.at[3 * b + k], recv_sem=recv_a.at[3 * b + k],
+                    device_id=device(level * PLANE + peer), device_id_type=MESH,
+                )
             )
-        )
-    for copy in first:
-        copy.start()
+    for copies in first:
+        for copy in copies:
+            copy.start()
     inbox[spot] = s_ref[:, group(spot)]
     dbox[spot] = d_ref[:, group(spot)]
-    for copy in first:
-        copy.wait()
-
-    cuts = LANES // 256
+
+    def chain(b):
+        return pltpu.make_async_remote_copy(
+            src_ref=chain_out.at[b], dst_ref=chain_in.at[b],
+            send_sem=send_c.at[b], recv_sem=recv_c.at[b],
+            device_id=device(lax.rem(u + PLANE, n)), device_id_type=MESH,
+        )
+
+    last = []
     for b in range(cuts):
         at = slice(b * 256, b * 256 + 256)
+        for copy in first[b]:
+            copy.wait()
         state = inbox[0, :, at].astype(F32)
         decay = dbox[0, 0:1, at]
         for p in range(1, PLANE):
@@ -484,17 +497,6 @@
             decay = decay * d
         total[:, at] = state
         decs[0, 0:1, at] = decay
-
-    def chain(b):
-        return pltpu.make_async_remote_copy(
-            src_ref=chain_out.at[b], dst_ref=chain_in.at[b],
-            send_sem=send_c.at[b], recv_sem=recv_c.at[b],
-            device_id=device(lax.rem(u + PLANE, n)), device_id_type=MESH,
-        )
-
-    last = []
-    for b in range(cuts):
-        at = slice(b * 256, b * 256 + 256)
 
         @pl.when(level > 0)
         def _():
@@ -551,7 +553,7 @@
             pltpu.VMEM((cuts, 128, 256), state.dtype),
             pltpu.VMEM((cuts, 128, 256), state.dtype),
             pltpu.VMEM((PLANE, 128, LANES), state.dtype),
-            dma((3,)), dma((3,)), dma((3,)), dma((3,)),
+            dma((3 * cuts,)), dma((3 * cuts,)), dma((3,)), dma((3,)),
             dma((cuts,)), dma((cuts,)), dma((3 * cuts,)), dma((3 * cuts,)),
         ],
         compiler_params=pltpu.CompilerParams(

time: 687 us -> 676 us (0.984)
  Pallas kernels: 435 us -> 422 us
    pallas_call x4, Pallas kernels: 155 us -> 142 us  [exchange(): pl.pallas_call(functools.partial(exchange_kernel, n, rev), out_shape=sds(...]
  transfers between devices with their start and end apart: 39 -> 39, of which waited for: 11 -> 11; matrix products, arithmetic and copies ran while one was open for 12% -> 12% of each run, Pallas kernels for 38% -> 39%
where the time goes in v6:
time: 676 us; the launch traced here: 665 us
  Pallas kernels  422 us (62%)
  waiting for transfers between devices  63.2 us (9%)
  local copies, waits for them, and re-layouts  62.1 us (9%)
  matrix products  45.3 us (7%)
  starting transfers between devices  37.3 us (6%)
  other arithmetic  18.7 us (3%)
  between operations  16.4 us (2%)
    pallas_call x4, Pallas kernels, exchange(): pl.pallas_call(functools.partial(exchange_kernel, n, rev), out_shape=sds(...  142 us
    pallas_call x2, Pallas kernels, core_back(): pl.pallas_call(body, grid=(STEPS + 2,), in_specs=[lanes(ROWS, STEPS), fix...  78.3 us
    pallas_call x2, Pallas kernels, gate_back(): pl.pallas_call(body, grid=(2, STEPS), in_specs=[first(ROWS), first(ROWS),...  48.2 us
    unnamed x256, local copies, waits for them, and re-layouts  45.3 us
    dot_general x12, matrix products, part(): lax.dot_general(left, cols, (((0, 1), (0, 1)), ((), ())), preferred_eleme...  45.3 us
    ppermute x4, waiting for transfers between devices, shifted(): lax.ppermute(value, 'seq', [(i, i + distance) for i in range(n) if 0 <= i...  34.9 us
    pallas_call x2, Pallas kernels, mix(): pl.pallas_call(functools.partial(mix_kernel, n), grid=(STEPS,), in_specs=...  29.6 us
    pallas_call x2, Pallas kernels, project_mm(): pl.pallas_call(project_kernel, grid_spec=pltpu.PrefetchScalarGridSpec(num...  28.2 us
  transfers between devices with their start and end apart: 39, of which 11 were waited for; matrix products, arithmetic and copies ran while one was open for 12% of the time, Pallas kernels for 39%

profile of v6, /device:TPU:0, one launch (start us, length us, event | category | flops | bytes accessed | tf_op | source)
XLA Modules:
  0.0 664.6 jit_solution(5146089696442860278)
XLA Ops:
  19.9 28.0 %collective-permute-done.4 = bf16[16,1536]{1,0:T(8,128)(2,1)S(1)} collective-permute-done((bf16[16,1536]{1,0:T(8,128)(2,1)S(1)}, bf16[16,1536]{1,0:T(8,128)(2,1)S(1)}, u32[]{:S(2)}, u32[]{:S(2)}) %collective-permute-start.4) | collective-permute-done | bytes 49184 | tf_op jit(solution)/shard_map/ppermute | solution.py:1032
  50.8 14.1 %shard_map.194 = (f32[256,6448]{1,0:T(8,128)}, f32[16,6448]{1,0:T(8,128)S(1)}) custom-call(s32[1]{0:T(128)} %bitcast.2.flag_ref, bf16[272,1536]{1,0:T(8,128)(2,1)S(1)} %pad_maximum_fusion.5.x_ref, bf16[6448,1536]{1,0:T(8,128)(2,1)} %bitcast.146, bf16[6448,1536]{1,0:T(8,128)(2,1)} %collective-permute-done.5.other_ref), custom_call_target="tpu_custom_call" | custom-call | flops 5070913536 | bytes 19808256 | tf_op jit(solution)/shard_map/pallas_call | solution.py:277
  66.3 13.2 %shard_map.195 = (f32[256,3072]{1,0:T(8,128)}, f32[128,3072]{1,0:T(8,128)S(1)}, f32[8,3072]{1,0:T(8,128)S(1)}, bf16[256,384]{1,0:T(8,128)(2,1)S(1)}, bf16[256,38...) custom-call(f32[256,6448]{1,0:T(8,128)} %get-tuple-element.108.x_ref, ...), custom_call_target="tpu_custom_call" | custom-call | flops 1000000000 | bytes 10485760 | tf_op jit(solution)/shard_map/pallas_call | solution.py:401
  80.2 40.5 %shard_map.196.car_ref.refs_16_ = f32[128,3072]{1,0:T(8,128)S(1)} custom-call(f32[128,3072]{1,0:T(8,128)S(1)} %get-tuple-element.116.s_ref, f32[8,3072]{1,0:T(8,128)S(1)} %get-tuple-element.117.d_ref), custom_call_target="tpu_custom_call" | custom-call | tf_op jit(solution)/shard_map/pallas_call | solution.py:542
  123.5 14.7 %shard_map.197 = (f32[256,3072]{1,0:T(8,128)}, bf16[256,3072]{1,0:T(8,128)(2,1)S(1)}, bf16[256,3072]{1,0:T(8,128)(2,1)S(1)}) custom-call(f32[256,256]{1,0:T(8,128)S(1)} %get-tuple-element.110.g_ref, bf16[256,384]{1,0:T(8,128)(2,1)S(1)} %get-tuple-element.111.step_ref.refs_8_, bf16[256,384]{1,0:T(8,128)(2,1)S(1)} %get-tuple-element.112.cum_ref.refs_3_.refs_9_, ...), custom_call_target="tpu_custom_call" | custom-call | flops 3000000000 | bytes 14680064 | tf_op jit(solution)/shard_map/pallas_call | solution.py:626
  138.2 6.9 %shard_map.198 = f32[256,1536]{1,0:T(8,128)S(1)} custom-call(s32[1]{0:T(128)} %bitcast.2.flag_ref, bf16[256,3072]{1,0:T(8,128)(2,1)S(1)} %get-tuple-element.118.x_ref, bf16[3072,1536]{1,0:T(8,128)(2,1)} %bitcast.17.own_ref, bf16[3072,1536]{1,0:T(8,128)(2,1)} %collective-permute-done.6.other_ref), custom_call_target="tpu_custom_call" | custom-call | flops 2415919104 | bytes 9437184 | tf_op jit(solution)/shard_map/pallas_call | solution.py:157
  149.7 6.8 %collective-permute-done.7 = bf16[16,1536]{1,0:T(8,128)(2,1)S(1)} collective-permute-done((bf16[16,1536]{1,0:T(8,128)(2,1)S(1)}, bf16[16,1536]{1,0:T(8,128)(2,1)S(1)}, u32[]{:S(2)}, u32[]{:S(2)}) %collective-permute-start.7) | collective-permute-done | bytes 49184 | tf_op jit(solution)/shard_map/ppermute | solution.py:1032
  161.8 14.1 %shard_map.199 = (f32[256,6448]{1,0:T(8,128)}, f32[16,6448]{1,0:T(8,128)S(1)}) custom-call(s32[1]{0:T(128)} %bitcast.flag_ref, bf16[272,1536]{1,0:T(8,128)(2,1)S(1)} %pad_maximum_fusion.6.x_ref, bf16[6448,1536]{1,0:T(8,128)(2,1)} %bitcast.147, bf16[6448,1536]{1,0:T(8,128)(2,1)} %collective-permute-done.5.other_ref), custom_call_target="tpu_custom_call" | custom-call | flops 5070913536 | bytes 19808256 | tf_op jit(solution)/shard_map/pallas_call | solution.py:277
  176.0 13.2 %shard_map.200 = (f32[256,3072]{1,0:T(8,128)}, f32[128,3072]{1,0:T(8,128)S(1)}, f32[8,3072]{1,0:T(8,128)S(1)}, bf16[256,384]{1,0:T(8,128)(2,1)S(1)}, bf16[256,38...) custom-call(f32[256,6448]{1,0:T(8,128)} %get-tuple-element.120.x_ref, ...), custom_call_target="tpu_custom_call" | custom-call | flops 1000000000 | bytes 10485760 | tf_op jit(solution)/shard_map/pallas_call | solution.py:401
  189.2 40.6 %shard_map.201.car_ref.refs_16_ = f32[128,3072]{1,0:T(8,128)S(1)} custom-call(f32[128,3072]{1,0:T(8,128)S(1)} %get-tuple-element.122.s_ref, f32[8,3072]{1,0:T(8,128)S(1)} %get-tuple-element.123.d_ref), custom_call_target="tpu_custom_call" | custom-call | tf_op jit(solution)/shard_map/pallas_call | solution.py:542
  230.9 15.0 %shard_map.203 = (f32[256,3072]{1,0:T(8,128)}, bf16[256,3072]{1,0:T(8,128)(2,1)S(1)}, bf16[256,3072]{1,0:T(8,128)(2,1)S(1)}) custom-call(f32[256,256]{1,0:T(8,128)S(1)} %get-tuple-element.135.g_ref, bf16[256,384]{1,0:T(8,128)(2,1)S(1)} %get-tuple-element.136.step_ref.refs_8_, bf16[256,384]{1,0:T(8,128)(2,1)S(1)} %get-tuple-element.137.cum_ref.refs_3_.refs_9_, ...), custom_call_target="tpu_custom_call" | custom-call | flops 3000000000 | bytes 14680064 | tf_op jit(solution)/shard_map/pallas_call | solution.py:626
  248.3 6.9 %shard_map.202.refs_0_ = f32[256,3072]{1,0:T(8,128)S(1)} custom-call(s32[1]{0:T(128)} %bitcast.flag_ref, bf16[256,1536]{1,0:T(8,128)(2,1)S(1)} %dynamic-slice_bitcast_fusion.x_ref, bf16[3072,1536]{1,0:T(8,128)(2,1)} %bitcast.17.own_ref, bf16[3072,1536]{1,0:T(8,128)(2,1)} %collective-permute-done.6.other_ref), custom_call_target="tpu_custom_call" | custom-call | flops 2415919104 | bytes 9437184 | tf_op jit(solution)/shard_map/pallas_call | solution.py:157
  256.9 20.6 %shard_map.204 = (f32[256,3072]{1,0:T(8,128)}, bf16[256,3072]{1,0:T(8,128)(2,1)S(1)}, f32[8,3072]{1,0:T(8,128)S(1)}, bf16[128,3072]{1,0:T(8,128)(2,1)S(1)}, bf16[4,256,768]{2,1,0:T(8,128)(2,1)S(1)}) custom-call(f32[256,3072]{1,0:T(8,128)} %copy-done.1, f32[256,3072]{1,0:T(8,128)} %get-tuple-element.141.refs_1_.refs_14_, ...), custom_call_target="tpu_custom_call" | custom-call | flops 1000000000 | bytes 16777216 | tf_op jit(solution)/shard_map/pallas_call | solution.py:696
  278.6 34.4 %shard_map.205.refs_17_ = bf16[128,3072]{1,0:T(8,128)(2,1)S(1)} custom-call(bf16[128,3072]{1,0:T(8,128)(2,1)S(1)} %get-tuple-element.148.s_ref, f32[8,3072]{1,0:T(8,128)S(1)} %get-tuple-element.123.d_ref), custom_call_target="tpu_custom_call" | custom-call | tf_op jit(solution)/shard_map/pallas_call | solution.py:542
  313.1 36.0 %shard_map.206 = (bf16[256,3584]{1,0:T(8,128)(2,1)}, f32[16,3584]{1,0:T(8,128)S(1)}, f32[8,3584]{1,0:T(8,128)}, f32[8,3584]{1,0:T(8,128)S(1)}, f32[8,128]{1,0:T(...) custom-call(f32[256,6448]{1,0:T(8,128)} %get-tuple-element.120.x_ref.bc_ref.raw_ref.gate_ref.refs_2_.refs_0_., ...), custom_call_target="tpu_custom_call" | custom-call | flops 8000000000 | bytes 14680064 | tf_op jit(solution)/shard_map/pallas_call | solution.py:832
  373.1 11.8 %shard_map.207 = f32[256,1536]{1,0:T(8,128)S(1)} custom-call(s32[1]{0:T(128)} %bitcast.flag_ref, bf16[256,3072]{1,0:T(8,128)(2,1)S(1)} %copy-done.10, bf16[256,3584]{1,0:T(8,128)(2,1)S(1)} %copy-done.6, bf16[6448,1536]{1,0:T(8,128)(2,1)} %bitcast.148, bf16[6448,1536]{1,0:T(8,128)(2,1)} %collective-permute-done.5.other_ref), custom_call_target="tpu_custom_call" | custom-call | flops 5070913536 | bytes 19808256 | tf_op jit(solution)/shard_map/pallas_call | solution.py:316
  388.0 7.0 %shard_map.208.refs_0_ = f32[256,3072]{1,0:T(8,128)S(1)} custom-call(s32[1]{0:T(128)} %bitcast.2.flag_ref, bf16[256,1536]{1,0:T(8,128)(2,1)S(1)} %get-tuple-element.186.x_ref, bf16[3072,1536]{1,0:T(8,128)(2,1)} %bitcast.17.own_ref, bf16[3072,1536]{1,0:T(8,128)(2,1)} %collective-permute-done.6.other_ref), custom_call_target="tpu_custom_call" | custom-call | flops 2415919104 | bytes 9437184 | tf_op jit(solution)/shard_map/pallas_call | solution.py:157
  396.7 27.6 %shard_map.209 = (f32[256,3072]{1,0:T(8,128)}, bf16[256,3072]{1,0:T(8,128)(2,1)S(1)}, f32[8,3072]{1,0:T(8,128)S(1)}, bf16[128,3072]{1,0:T(8,128)(2,1)S(1)}, bf16[4,256,896]{2,1,0:T(8,128)(2,1)S(1)}) custom-call(f32[256,3072]{1,0:T(8,128)} %copy-done.2, f32[256,3072]{1,0:T(8,128)} %get-tuple-element.132.refs_1_.refs_14_, ...), custom_call_target="tpu_custom_call" | custom-call | flops 1000000000 | bytes 16777216 | tf_op jit(solution)/shard_map/pallas_call | solution.py:696
  441.9 26.2 %shard_map.210.refs_17_ = bf16[128,3072]{1,0:T(8,128)(2,1)S(1)} custom-call(bf16[128,3072]{1,0:T(8,128)(2,1)S(1)} %copy-done.30, f32[8,3072]{1,0:T(8,128)S(1)} %copy-done.37), custom_call_target="tpu_custom_call" | custom-call | tf_op jit(solution)/shard_map/pallas_call | solution.py:542
  479.1 42.3 %shard_map.211 = (bf16[256,3584]{1,0:T(8,128)(2,1)}, f32[16,3584]{1,0:T(8,128)S(1)}, f32[8,3584]{1,0:T(8,128)S(1)}, f32[8,3584]{1,0:T(8,128)S(1)}, f32[8,128]{1,...) custom-call(f32[256,6448]{1,0:T(8,128)} %get-tuple-element.108.x_ref.bc_ref.raw_ref.gate_ref.refs_2_.refs_0_.refs_1_, ...), custom_call_target="tpu_custom_call" | custom-call | flops 8000000000 | bytes 14680064 | tf_op jit(solution)/shard_map/pallas_call | solution.py:832
  552.8 11.8 %shard_map.212 = f32[256,1536]{1,0:T(8,128)S(1)} custom-call(s32[1]{0:T(128)} %bitcast.2.flag_ref, bf16[256,3072]{1,0:T(8,128)(2,1)S(1)} %copy-done.8, bf16[256,3584]{1,0:T(8,128)(2,1)S(1)} %copy-done.5, bf16[6448,1536]{1,0:T(8,128)(2,1)} %bitcast.149, bf16[6448,1536]{1,0:T(8,128)(2,1)} %collective-permute-done.5.other_ref), custom_call_target="tpu_custom_call" | custom-call | flops 5070913536 | bytes 19808256 | tf_op jit(solution)/shard_map/pallas_call | solution.py:316
  617.7 6.8 %shard_map.214 = f32[256,1536]{1,0:T(8,128)S(1)} custom-call(s32[1]{0:T(128)} %bitcast.flag_ref, bf16[256,3072]{1,0:T(8,128)(2,1)S(1)} %copy-done.22, bf16[3072,1536]{1,0:T(8,128)(2,1)} %bitcast.17.own_ref, bf16[3072,1536]{1,0:T(8,128)(2,1)} %collective-permute-done.6.other_ref), custom_call_target="tpu_custom_call" | custom-call | flops 2415919104 | bytes 9437184 | tf_op jit(solution)/shard_map/pallas_call | solution.py:157
  624.8 7.4 %reduce-scatter.13.cloned.1.call-done.rest = bf16[384,448]{1,0:T(8,128)(2,1)} async-done(((bf16[1536,448]{1,0:T(8,128)(2,1)}), bf16[384,448]{1,0:T(8,128)(2,1)}) %reduce-scatter.13.cloned.1.call-update) | async-done | bytes 344080 | tf_op jit(solution)/shard_map/reduce_scatter | solution.py:1070
  638.7 12.0 %shard_map.215 = (f32[96,6448]{1,0:T(8,128)S(1)}, f32[192,1536]{1,0:T(8,128)S(1)}, bf16[2,256,1536]{2,1,0:T(8,128)(2,1)S(1)}, f32[2,256,1536]{2,1,0:T(8,128)}) custom-call(bf16[384,384]{1,0:T(8,128)(2,1)S(1)} %copy-done.40, bf16[384,448]{1,0:T(8,128)(2,1)S(1)} %copy-done.35, bf16[8,96,384]{2,1,0:T(8,128)(2,1)S(1)} %copy-done.32, ...), custom_call_target="tpu_custom_call" | custom-call | tf_op jit(solution)/shard_map/pallas_call | solution.py:1008
  (448 shorter events, 190.1 us)
Async XLA Ops:
  7.3 432.6 %reduce-scatter.9.cloned.1.call-start = ((), (), s32[]{:S(2)}) async-start(), calls=%async_computation.7 | async-start | bytes 1474560 | tf_op jit(solution)/shard_map/reduce_scatter | solution.py:1070
  7.3 43.3 %collective-permute-start.5 = (bf16[6448,1536]{1,0:T(8,128)(2,1)}, bf16[6448,1536]{1,0:T(8,128)(2,1)}, u32[]{:S(2)}, u32[]{:S(2)}) collective-permute-start(bf16[6448,1536]{1,0:T(8,128)(2,1)} %bitcast.145), channel_id=1, source_target_pairs={{0,16},{16,0},{1,17},{17,1},{2,18},{18,2},{3,19},{19,3},{4,20},{20... | collective-permute-start | bytes 59424776 | tf_op jit(solution)/shard_map/ppermute | solution.py:1028
  9.0 40.6 %collective-permute-start.3 = (bf16[256,1536]{1,0:T(8,128)(2,1)S(1)}, bf16[256,1536]{1,0:T(8,128)(2,1)S(1)}, u32[]{:S(2)}, u32[]{:S(2)}) collective-permute-start(bf16[256,1536]{1,0:T(8,128)(2,1)S(1)} %dynamic-slice_bitcast_fusion.x_ref), channel_id=1, source_target_pairs={{0,3},{1,0},{2,1},{3,2},{4,7},{5,4},{6,5},{7,6},{8,11},{9,8},{10,9... | collective-permute-start | bytes 2359304 | tf_op jit(solution)/shard_map/ppermute | solution.py:1048
  12.7 37.0 %collective-permute-start.2 = (bf16[256,1536]{1,0:T(8,128)(2,1)S(1)}, bf16[256,1536]{1,0:T(8,128)(2,1)}, u32[]{:S(2)}, u32[]{:S(2)}) collective-permute-start(bf16[256,1536]{1,0:T(8,128)(2,1)S(1)} %dynamic-slice_bitcast_fusion.x_ref), channel_id=1, source_target_pairs={{0,2},{1,3},{2,0},{3,1},{4,6},{5,7},{6,4},{7,5},{8,10},{9,11},{10,... | collective-permute-start | bytes 2359304 | tf_op jit(solution)/shard_map/ppermute | solution.py:1048
  13.2 37.4 %collective-permute-start.1 = (bf16[256,1536]{1,0:T(8,128)(2,1)S(1)}, bf16[256,1536]{1,0:T(8,128)(2,1)}, u32[]{:S(2)}, u32[]{:S(2)}) collective-permute-start(bf16[256,1536]{1,0:T(8,128)(2,1)S(1)} %dynamic-slice_bitcast_fusion.x_ref), channel_id=1, source_target_pairs={{0,1},{1,2},{2,3},{3,0},{4,5},{5,6},{6,7},{7,4},{8,9},{9,10},{10,1... | collective-permute-start | bytes 2359304 | tf_op jit(solution)/shard_map/ppermute | solution.py:1048
  14.6 33.4 %collective-permute-start.4 = (bf16[16,1536]{1,0:T(8,128)(2,1)S(1)}, bf16[16,1536]{1,0:T(8,128)(2,1)S(1)}, u32[]{:S(2)}, u32[]{:S(2)}) collective-permute-start(bf16[16,1536]{1,0:T(8,128)(2,1)S(1)} %dynamic-slice_bitcast_fusion.1), channel_id=1, source_target_pairs={{0,1},{1,2},{2,3},{3,4},{4,5},{5,6},{6,7},{7,8},{8,9},{9,10},{10,1... | collective-permute-start | bytes 147464 | tf_op jit(solution)/shard_map/ppermute | solution.py:1032
  64.9 73.3 %collective-permute-start.6 = (bf16[3072,1536]{1,0:T(8,128)(2,1)}, bf16[3072,1536]{1,0:T(8,128)(2,1)}, u32[]{:S(2)}, u32[]{:S(2)}) collective-permute-start(bf16[3072,1536]{1,0:T(8,128)(2,1)} %bitcast.17.own_ref), channel_id=1, source_target_pairs={{0,16},{16,0},{1,17},{17,1},{2,18},{18,2},{3,19},{19,3},{4,20},{20... | collective-permute-start | bytes 28311560 | tf_op jit(solution)/shard_map/ppermute | solution.py:1028
  120.7 40.0 %collective-permute-start.10 = (bf16[256,1536]{1,0:T(8,128)(2,1)S(1)}, bf16[256,1536]{1,0:T(8,128)(2,1)S(1)}, u32[]{:S(2)}, u32[]{:S(2)}) collective-permute-start(bf16[256,1536]{1,0:T(8,128)(2,1)S(1)} %copy-done.74), channel_id=1, source_target_pairs={{0,3},{1,0},{2,1},{3,2},{4,7},{5,4},{6,5},{7,6},{8,11},{9,8},{10,9... | collective-permute-start | bytes 2359304 | tf_op jit(solution)/shard_map/ppermute | solution.py:1048
  122.1 107.8 %collective-permute-start.9 = (bf16[256,1536]{1,0:T(8,128)(2,1)S(1)}, bf16[256,1536]{1,0:T(8,128)(2,1)S(1)}, u32[]{:S(2)}, u32[]{:S(2)}) collective-permute-start(bf16[256,1536]{1,0:T(8,128)(2,1)S(1)} %copy-done.74), channel_id=1, source_target_pairs={{0,2},{1,3},{2,0},{3,1},{4,6},{5,7},{6,4},{7,5},{8,10},{9,11},{10,... | collective-permute-start | bytes 2359304 | tf_op jit(solution)/shard_map/ppermute | solution.py:1048
  123.5 106.3 %collective-permute-start.8 = (bf16[256,1536]{1,0:T(8,128)(2,1)S(1)}, bf16[256,1536]{1,0:T(8,128)(2,1)S(1)}, u32[]{:S(2)}, u32[]{:S(2)}) collective-permute-start(bf16[256,1536]{1,0:T(8,128)(2,1)S(1)} %copy-done.74), channel_id=1, source_target_pairs={{0,1},{1,2},{2,3},{3,0},{4,5},{5,6},{6,7},{7,4},{8,9},{9,10},{10,1... | collective-permute-start | bytes 2359304 | tf_op jit(solution)/shard_map/ppermute | solution.py:1048
  156.5 73.3 %collective-permute-start.13 = (bf16[256,1536]{1,0:T(8,128)(2,1)S(1)}, bf16[256,1536]{1,0:T(8,128)(2,1)S(1)}, u32[]{:S(2)}, u32[]{:S(2)}) collective-permute-start(bf16[256,1536]{1,0:T(8,128)(2,1)S(1)} %fusion.12), channel_id=1, source_target_pairs={{0,3},{1,0},{2,1},{3,2},{4,7},{5,4},{6,5},{7,6},{8,11},{9,8},{10,9... | collective-permute-start | bytes 2359304 | tf_op jit(solution)/shard_map/ppermute | solution.py:1048
  159.9 70.0 %collective-permute-start.12 = (bf16[256,1536]{1,0:T(8,128)(2,1)S(1)}, bf16[256,1536]{1,0:T(8,128)(2,1)S(1)}, u32[]{:S(2)}, u32[]{:S(2)}) collective-permute-start(bf16[256,1536]{1,0:T(8,128)(2,1)S(1)} %fusion.12), channel_id=1, source_target_pairs={{0,2},{1,3},{2,0},{3,1},{4,6},{5,7},{6,4},{7,5},{8,10},{9,11},{10,... | collective-permute-start | bytes 2359304 | tf_op jit(solution)/shard_map/ppermute | solution.py:1048
  160.7 69.2 %collective-permute-start.11 = (bf16[256,1536]{1,0:T(8,128)(2,1)S(1)}, bf16[256,1536]{1,0:T(8,128)(2,1)S(1)}, u32[]{:S(2)}, u32[]{:S(2)}) collective-permute-start(bf16[256,1536]{1,0:T(8,128)(2,1)S(1)} %fusion.12), channel_id=1, source_target_pairs={{0,1},{1,2},{2,3},{3,0},{4,5},{5,6},{6,7},{7,4},{8,9},{9,10},{10,1... | collective-permute-start | bytes 2359304 | tf_op jit(solution)/shard_map/ppermute | solution.py:1048
  360.9 79.0 %reduce-scatter.7.cloned.1.call-start = ((), (), s32[]{:S(2)}) async-start(), calls=%async_computation.6 | async-start | bytes 1474560 | tf_op jit(solution)/shard_map/reduce_scatter | solution.py:1070
  370.0 237.9 %reduce-scatter.15.cloned.1.call-start = ((), (), s32[]{:S(2)}) async-start(), calls=%async_computation.10 | async-start | bytes 1966080 | tf_op jit(solution)/shard_map/reduce_scatter | solution.py:1070
  469.1 52.4 %collective-permute-start.20 = (bf16[256,1536]{1,0:T(8,128)(2,1)S(1)}, bf16[256,1536]{1,0:T(8,128)(2,1)}, u32[]{:S(2)}, u32[]{:S(2)}) collective-permute-start(bf16[256,1536]{1,0:T(8,128)(2,1)S(1)} %get-tuple-element.186.x_ref), channel_id=1, source_target_pairs={{0,3},{1,0},{2,1},{3,2},{4,7},{5,4},{6,5},{7,6},{8,11},{9,8},{10,9... | collective-permute-start | bytes 2359304 | tf_op jit(solution)/shard_map/ppermute | solution.py:1048
  470.2 51.2 %collective-permute-start.19 = (bf16[256,1536]{1,0:T(8,128)(2,1)S(1)}, bf16[256,1536]{1,0:T(8,128)(2,1)}, u32[]{:S(2)}, u32[]{:S(2)}) collective-permute-start(bf16[256,1536]{1,0:T(8,128)(2,1)S(1)} %get-tuple-element.186.x_ref), channel_id=1, source_target_pairs={{0,2},{1,3},{2,0},{3,1},{4,6},{5,7},{6,4},{7,5},{8,10},{9,11},{10,... | collective-permute-start | bytes 2359304 | tf_op jit(solution)/shard_map/ppermute | solution.py:1048
  471.0 50.5 %collective-permute-start.18 = (bf16[256,1536]{1,0:T(8,128)(2,1)S(1)}, bf16[256,1536]{1,0:T(8,128)(2,1)}, u32[]{:S(2)}, u32[]{:S(2)}) collective-permute-start(bf16[256,1536]{1,0:T(8,128)(2,1)S(1)} %get-tuple-element.186.x_ref), channel_id=1, source_target_pairs={{0,1},{1,2},{2,3},{3,0},{4,5},{5,6},{6,7},{7,4},{8,9},{9,10},{10,1... | collective-permute-start | bytes 2359304 | tf_op jit(solution)/shard_map/ppermute | solution.py:1048
  472.0 152.8 %reduce-scatter.11.cloned.1.call-start = ((), (), s32[]{:S(2)}) async-start(), calls=%async_computation.8 | async-start | bytes 1474560 | tf_op jit(solution)/shard_map/reduce_scatter | solution.py:1070
  535.7 89.1 %reduce-scatter.17.cloned.1.call-start = ((), (), s32[]{:S(2)}) async-start(), calls=%async_computation.11 | async-start | bytes 1474560 | tf_op jit(solution)/shard_map/reduce_scatter | solution.py:1070
  539.8 26.0 %collective-permute-start.25 = (bf16[256,896]{1,0:T(8,128)(2,1)}, bf16[256,896]{1,0:T(8,128)(2,1)}, u32[]{:S(2)}, u32[]{:S(2)}) collective-permute-start(bf16[256,896]{1,0:T(8,128)(2,1)} %get-tuple-element.211), channel_id=1, source_target_pairs={{0,3},{1,0},{2,1},{3,2},{4,7},{5,4},{6,5},{7,6},{8,11},{9,8},{10,9... | collective-permute-start | bytes 1376264 | tf_op jit(solution)/shard_map/ppermute | solution.py:1240
  543.6 22.3 %collective-permute-start.24 = (bf16[256,896]{1,0:T(8,128)(2,1)}, bf16[256,896]{1,0:T(8,128)(2,1)}, u32[]{:S(2)}, u32[]{:S(2)}) collective-permute-start(bf16[256,896]{1,0:T(8,128)(2,1)} %get-tuple-element.212), channel_id=1, source_target_pairs={{0,2},{1,3},{2,0},{3,1},{4,6},{5,7},{6,4},{7,5},{8,10},{9,11},{10,... | collective-permute-start | bytes 1376264 | tf_op jit(solution)/shard_map/ppermute | solution.py:1240
  543.9 22.0 %collective-permute-start.23 = (bf16[256,896]{1,0:T(8,128)(2,1)}, bf16[256,896]{1,0:T(8,128)(2,1)}, u32[]{:S(2)}, u32[]{:S(2)}) collective-permute-start(bf16[256,896]{1,0:T(8,128)(2,1)} %get-tuple-element.213), channel_id=1, source_target_pairs={{0,1},{1,2},{2,3},{3,0},{4,5},{5,6},{6,7},{7,4},{8,9},{9,10},{10,1... | collective-permute-start | bytes 1376264 | tf_op jit(solution)/shard_map/ppermute | solution.py:1240
  549.5 82.7 %reduce-scatter.13.cloned.1.call-start = ((), (), s32[]{:S(2)}) async-start(), calls=%async_computation.9 | async-start | bytes 1966080 | tf_op jit(solution)/shard_map/reduce_scatter | solution.py:1070
  (141 other events, 1933.4 us)
Sparse Core Ops, SparseCore 0:
  361.0 28.4 reduce-scatter.8
  391.9 27.8 reduce-scatter.6
  472.2 32.9 reduce-scatter.14
  535.8 28.6 reduce-scatter.10
  566.7 28.6 reduce-scatter.16
  598.1 34.0 reduce-scatter.12
